TPU v7x, 32 devices: a whole 2x2x4 slice. The times are simulated.
32 devices in a mesh: ctx: 8 (over z, x), dp: 4 (over y, core).
Axes of the slice: x: 2, y: 2, z: 4, core: 2. Of those that a mesh axis runs over, the one named last changes fastest.
Arguments:
- inner_input: bfloat16 [24576, 4096], P(('dp', 'ctx')), parts along dimension 0, may hold values from -6 to 6
- state_proj: bfloat16 [24576, 256], P(('dp', 'ctx')), parts along dimension 0, may hold values from -6 to 6
- step_size: float32 [24576, 64], P(('dp', 'ctx')), parts along dimension 0, may hold values from 0.004 to 0.04
- decay_log: float32 [24576, 64], P(('dp', 'ctx')), parts along dimension 0, may hold values from -1 to 0
- conv_inner: float32 [4, 4096], replicated, may hold values from -3 to 3
- conv_proj: float32 [4, 256], replicated, may hold values from -3 to 3
- skip_weight: float32 [64], replicated, may hold values from 0.5 to 2.5
- norm_gain: float32 [4096], replicated, may hold values from 0.5 to 1.5
Outputs:
- layer_output: bfloat16 [24576, 4096], P(('dp', 'ctx')), parts along dimension 0
There are 4 independent parts, one for each index of `dp`. A program takes and returns all parts, laid end to end along the dimension named above; an argument that names none is the same for every part. Nothing has to cross between parts.
All inputs are finite; a program needn't handle non-finite values.
Results may differ from a plain program's by a relative error of at most 0.0045.
Values may be sent and summed in bfloat16 or wider, within the bound.
No kernel may reach another device: no remote copies, remote signals or barrier semaphores. Data moves between devices by JAX's collectives and lax.ppermute only.
A program may use at most 192 MiB of HBM per device.

v0:
```python
import jax
import jax.numpy as jnp
from jax import lax
from jax.sharding import PartitionSpec as P

BLOCK = 256


def passed_along(x, axis, by):
    length = lax.axis_size(axis)
    pairs = [(i, i + by) for i in range(length) if 0 <= i + by < length]
    return lax.ppermute(x, axis, pairs)


def silu_conv(window, weights, length):
    summed = jnp.zeros((length, weights.shape[1]), jnp.float32)
    for offset in range(weights.shape[0]):
        summed = summed + window[offset : offset + length].astype(jnp.float32) * weights[offset]
    return jax.nn.silu(summed).astype(jnp.bfloat16)


def block_terms(inner_rows, project, step_block, decays):
    length = inner_rows.shape[0]
    width = inner_rows.shape[1]
    head_count = step_block.shape[1]
    head_width = width // head_count
    state_width = project.shape[1] // 2
    b_rows = project[:, :state_width]
    c_rows = project[:, state_width:]
    cum_heads = jnp.cumsum(decays.T, axis=1)
    step_heads = step_block.T
    scores = jnp.dot(c_rows, b_rows.T, preferred_element_type=jnp.float32)
    positions = jnp.arange(length)
    causal = positions[:, None] >= positions[None, :]
    spread = cum_heads[:, :, None] - cum_heads[:, None, :]
    decay_table = jnp.where(causal[None], jnp.exp(jnp.minimum(spread, 0.0)), 0.0)
    weights = (scores[None] * decay_table * step_heads[:, None, :]).astype(jnp.bfloat16)
    inner_cols = inner_rows.T.reshape(head_count, head_width, length)
    inside = jnp.einsum("hts,hps->hpt", weights, inner_cols, preferred_element_type=jnp.float32)
    totals = cum_heads[:, -1]
    factor = jnp.exp(totals[:, None] - cum_heads) * step_heads
    scaled = (factor[:, None, :] * inner_cols).astype(jnp.bfloat16)
    block_state = jnp.einsum("hps,sn->hpn", scaled, b_rows, preferred_element_type=jnp.float32)
    return (inside, block_state.reshape(head_count, -1), cum_heads, totals, inner_cols)


def owner_chain(states_in, totals_in):
    summed = jnp.cumsum(totals_in, axis=0)
    before = summed - totals_in
    spread = before.T[:, :, None] - summed.T[:, None, :]
    positions = jnp.arange(totals_in.shape[0])
    causal = positions[:, None] > positions[None, :]
    lower = jnp.where(causal[None], jnp.exp(jnp.minimum(spread, 0.0)), 0.0)
    return jnp.einsum("hij,jhm->ihm", lower, states_in, precision=lax.Precision.HIGHEST)


def local_chain(states, totals, opening):

    def advance(carry_state, item):
        block_state, block_total = item
        return (jnp.exp(block_total)[:, None] * carry_state + block_state, carry_state)

    final_state, incoming = lax.scan(advance, opening, (states, totals))
    return (incoming, final_state)


def body(
    inner_input, state_proj, step_size, decay_log, conv_inner, conv_proj, skip_weight, norm_gain
):
    rows_here = inner_input.shape[0]
    width = inner_input.shape[1]
    head_count = step_size.shape[1]
    head_width = width // head_count
    state_width = state_proj.shape[1] // 2
    pad_rows = conv_inner.shape[0] - 1
    block_count = rows_here // BLOCK
    edges = jnp.concatenate(
        [inner_input[rows_here - pad_rows :], state_proj[rows_here - pad_rows :]], axis=1
    )
    arrived = passed_along(edges, "ctx", 1)
    inner_rows = silu_conv(
        jnp.concatenate([arrived[:, :width], inner_input], axis=0), conv_inner, rows_here
    )
    project = silu_conv(
        jnp.concatenate([arrived[:, width:], state_proj], axis=0), conv_proj, rows_here
    )
    inner_blocks = inner_rows.reshape(block_count, BLOCK, width)
    proj_blocks = project.reshape(block_count, BLOCK, 2 * state_width)
    step_blocks = step_size.reshape(block_count, BLOCK, head_count)
    decay_blocks = decay_log.reshape(block_count, BLOCK, head_count)
    inside, states, cumulative, totals, inner_cols = lax.map(
        lambda item: block_terms(item[0], item[1], item[2], item[3]),
        (inner_blocks, proj_blocks, step_blocks, decay_blocks),
    )
    ignored, summary = local_chain(states, totals, jnp.zeros_like(states[0]))
    device_total = jnp.sum(totals, axis=0)
    states_in, totals_in = (
        lax.all_to_all(summary[None], "ctx", split_axis=1, concat_axis=0, tiled=True),
        lax.all_to_all(device_total[None], "ctx", split_axis=1, concat_axis=0, tiled=True),
    )
    returned = lax.all_to_all(
        owner_chain(states_in, totals_in).astype(jnp.bfloat16),
        "ctx",
        split_axis=0,
        concat_axis=1,
        tiled=True,
    ).astype(jnp.float32)
    incoming, ignored = local_chain(states, totals, returned[0])
    entering_b = incoming.astype(jnp.bfloat16).reshape(
        block_count, head_count, head_width, state_width
    )
    c_cols = jnp.swapaxes(proj_blocks[:, :, state_width:], 1, 2)
    carried_part = jnp.einsum(
        "chpn,cnt->chpt", entering_b, c_cols, preferred_element_type=jnp.float32
    )
    combined = (
        inside
        + jnp.exp(cumulative)[:, :, None, :] * carried_part
        + skip_weight[None, :, None, None] * inner_cols.astype(jnp.float32)
    )
    inverse_rms = lax.rsqrt(jnp.mean(combined * combined, axis=2, keepdims=True) + 1e-05)
    gain_table = norm_gain.reshape(head_count, head_width)
    result = (combined * inverse_rms * gain_table[None, :, :, None]).astype(jnp.bfloat16)
    result = jnp.swapaxes(result.reshape(block_count, width, BLOCK), 1, 2)
    return result.reshape(rows_here, width)


def solution(mesh):
    placed = (
        P(("dp", "ctx"), None),
        P(("dp", "ctx"), None),
        P(("dp", "ctx"), None),
        P(("dp", "ctx"), None),
        P(),
        P(),
        P(),
        P(),
    )
    return jax.shard_map(
        body, mesh=mesh, in_specs=placed, out_specs=P(("dp", "ctx"), None), check_vma=False
    )
```

profile of v0, /device:TPU:0, one launch (start us, length us, event | category | flops | bytes accessed | tf_op | source)
XLA Modules:
  0.0 256.1 jit_solution(10837117518225074528)
XLA Ops:
  1.6 4.8 %collective-permute-start = (bf16[3,4352]{1,0:T(4,128)(2,1)S(1)}, bf16[3,4352]{1,0:T(4,128)(2,1)S(1)}, u32[]{:S(2)}, u32[]{:S(2)}) collective-permute-start(bf16[3,4352]{1,0:T(4,128)(2,1)S(1)} %pad_maximum_fusion.2), channel_id=1, source_target_pairs={{0,4},{4,8},{8,12},{12,16},{16,20},{20,24},{24,28},{1,5},{5,9},{9,... | collective-permute-start | bytes 78344 | tf_op jit(solution)/shard_map/ppermute | solution.py:12
  10.5 2.1 multiply_convert_fusion.8
  12.6 15.2 %multiply_convert_fusion.7 = bf16[768,4096]{1,0:T(8,128)(2,1)} fusion(bf16[768,4096]{1,0:T(8,128)(2,1)} %param.14, bf16[3,4096]{1,0:T(4,128)(2,1)S(1)} %slice.95, f32[4096]{0:T(1024)S(1)} %bitcast.170, f32[4096]{0:T(1024)S(1)} %bitcast.171, f32[4096]{0:T(1024)S(1)} %bitcast.169, f32[4096]{0:T(1024)S(1)} %bitcast.168), kind=kLoop, calls=%fused_computation.45 | loop fusion | flops 78643200 | bytes 12673024 | tf_op jit(solution)/shard_map/convert_element_type | solution.py:19
  27.8 74.4 %while.44 = (s32[]{:T(128)}, f32[3,64,64,256]{3,2,1,0:T(8,128)}, f32[3,64,8192]{2,1,0:T(8,128)}, f32[3,64,256]{2,1,0:T(8,128)}, f32[3,64]{1,0:T(4,128)S(1)}, /*i...) while((s32[]{:T(128)}, f32[3,64,64,256]{3,2,1,0:T(8,128)}, ...), condition=%wide.region_3.4_spmd.clone, body=%wide.region_0.3_spmd.sunk.clone | while | flops 852623552 | bytes 34349180 | solution.py:91
  28.9 3.1 %constant_dynamic-slice_fusion.8 = bf16[1,256,4096]{2,1,0:T(8,128)(2,1)} fusion(bf16[3,256,4096]{2,1,0:T(8,128)(2,1)} %get-tuple-element.408, s32[]{:T(128)} %get-tuple-element.392), kind=kLoop, calls=%fused_computation.40.clone.1.clone | loop fusion | bytes 4194308 | tf_op jit(solution)/shard_map/while/body/jit(dynamic_index_in_dim)/dynamic_slice | solution.py:91
  32.0 3.3 %copy.93 = bf16[1,256,4096]{1,2,0:T(8,128)(2,1)S(1)} copy(bf16[1,256,4096]{2,1,0:T(8,128)(2,1)} %constant_dynamic-slice_fusion.8) | data formatting | bytes 4194304 | tf_op jit(solution)/shard_map/while/body/jit(dynamic_index_in_dim)/dynamic_slice | solution.py:91
  35.5 6.5 %bitcast_dynamic-update-slice_fusion.6 = f32[3,64,64,256]{3,2,1,0:T(8,128)} fusion(f32[3,64,64,256]{3,2,1,0:T(8,128)} %get-tuple-element.393, s32[]{:T(128)} %get-tuple-element.392, bf16[64,64,256]{2,1,0:T(8,128)(2,1)S(1)} %bitcast.157, f32[64,256]{1,0:T(8,128)S(1)} %bitcast.166, f32[64,256]{1,0:T(8,128)S(1)} %copy_bitcast_fusion.14, ...), kind=kOutput, calls=%fused_computation.16.clone.1.clone | convolution fusion | flops 562036736 | bytes 6816256 | tf_op jit(solution)/shard_map/while/body/eval_jaxpr/hts,hps->hpt/dot_general | solution.py:39
  42.3 2.1 fusion.64
  44.4 2.8 %broadcast_in_dim.100 = f32[1,64,8192]{2,1,0:T(8,128)} reshape(f32[64,64,128]{2,1,0:T(8,128)} %fusion.64) | data formatting | bytes 4194304 | tf_op jit(solution)/shard_map/while/body/jit(dynamic_update_index_in_dim)/broadcast_in_dim | solution.py:91
  47.2 3.1 %constant_dynamic-update-slice_fusion.9 = f32[3,64,8192]{2,1,0:T(8,128)} fusion(f32[3,64,8192]{2,1,0:T(8,128)} %get-tuple-element.394, f32[1,64,8192]{2,1,0:T(8,128)} %broadcast_in_dim.100, s32[]{:T(128)} %get-tuple-element.392), kind=kLoop, calls=%fused_computation.37.clone.1.clone | loop fusion | bytes 4194816 | tf_op jit(solution)/shard_map/while/body/jit(dynamic_update_index_in_dim)/dynamic_update_slice | solution.py:91
  51.1 1.5 constant_dynamic-update-slice_fusion.11
  53.7 3.1 %constant_dynamic-slice_fusion.8 = bf16[1,256,4096]{2,1,0:T(8,128)(2,1)} fusion(bf16[3,256,4096]{2,1,0:T(8,128)(2,1)} %get-tuple-element.408, s32[]{:T(128)} %get-tuple-element.392), kind=kLoop, calls=%fused_computation.40.clone.1.clone | loop fusion | bytes 4194308 | tf_op jit(solution)/shard_map/while/body/jit(dynamic_index_in_dim)/dynamic_slice | solution.py:91
  56.8 3.3 %copy.93 = bf16[1,256,4096]{1,2,0:T(8,128)(2,1)S(1)} copy(bf16[1,256,4096]{2,1,0:T(8,128)(2,1)} %constant_dynamic-slice_fusion.8) | data formatting | bytes 4194304 | tf_op jit(solution)/shard_map/while/body/jit(dynamic_index_in_dim)/dynamic_slice | solution.py:91
  60.4 6.5 %bitcast_dynamic-update-slice_fusion.6 = f32[3,64,64,256]{3,2,1,0:T(8,128)} fusion(f32[3,64,64,256]{3,2,1,0:T(8,128)} %get-tuple-element.393, s32[]{:T(128)} %get-tuple-element.392, bf16[64,64,256]{2,1,0:T(8,128)(2,1)S(1)} %bitcast.157, f32[64,256]{1,0:T(8,128)S(1)} %bitcast.166, f32[64,256]{1,0:T(8,128)S(1)} %copy_bitcast_fusion.14, ...), kind=kOutput, calls=%fused_computation.16.clone.1.clone | convolution fusion | flops 562036736 | bytes 6816256 | tf_op jit(solution)/shard_map/while/body/eval_jaxpr/hts,hps->hpt/dot_general | solution.py:39
  67.2 2.1 fusion.64
  69.2 2.8 %broadcast_in_dim.100 = f32[1,64,8192]{2,1,0:T(8,128)} reshape(f32[64,64,128]{2,1,0:T(8,128)} %fusion.64) | data formatting | bytes 4194304 | tf_op jit(solution)/shard_map/while/body/jit(dynamic_update_index_in_dim)/broadcast_in_dim | solution.py:91
  72.0 3.1 %constant_dynamic-update-slice_fusion.9 = f32[3,64,8192]{2,1,0:T(8,128)} fusion(f32[3,64,8192]{2,1,0:T(8,128)} %get-tuple-element.394, f32[1,64,8192]{2,1,0:T(8,128)} %broadcast_in_dim.100, s32[]{:T(128)} %get-tuple-element.392), kind=kLoop, calls=%fused_computation.37.clone.1.clone | loop fusion | bytes 4194816 | tf_op jit(solution)/shard_map/while/body/jit(dynamic_update_index_in_dim)/dynamic_update_slice | solution.py:91
  75.9 1.4 constant_dynamic-update-slice_fusion.11
  78.4 3.1 %constant_dynamic-slice_fusion.8 = bf16[1,256,4096]{2,1,0:T(8,128)(2,1)} fusion(bf16[3,256,4096]{2,1,0:T(8,128)(2,1)} %get-tuple-element.408, s32[]{:T(128)} %get-tuple-element.392), kind=kLoop, calls=%fused_computation.40.clone.1.clone | loop fusion | bytes 4194308 | tf_op jit(solution)/shard_map/while/body/jit(dynamic_index_in_dim)/dynamic_slice | solution.py:91
  81.6 3.3 %copy.93 = bf16[1,256,4096]{1,2,0:T(8,128)(2,1)S(1)} copy(bf16[1,256,4096]{2,1,0:T(8,128)(2,1)} %constant_dynamic-slice_fusion.8) | data formatting | bytes 4194304 | tf_op jit(solution)/shard_map/while/body/jit(dynamic_index_in_dim)/dynamic_slice | solution.py:91
  85.1 6.5 %bitcast_dynamic-update-slice_fusion.6 = f32[3,64,64,256]{3,2,1,0:T(8,128)} fusion(f32[3,64,64,256]{3,2,1,0:T(8,128)} %get-tuple-element.393, s32[]{:T(128)} %get-tuple-element.392, bf16[64,64,256]{2,1,0:T(8,128)(2,1)S(1)} %bitcast.157, f32[64,256]{1,0:T(8,128)S(1)} %bitcast.166, f32[64,256]{1,0:T(8,128)S(1)} %copy_bitcast_fusion.14, ...), kind=kOutput, calls=%fused_computation.16.clone.1.clone | convolution fusion | flops 562036736 | bytes 6816256 | tf_op jit(solution)/shard_map/while/body/eval_jaxpr/hts,hps->hpt/dot_general | solution.py:39
  91.9 2.1 fusion.64
  94.0 2.8 %broadcast_in_dim.100 = f32[1,64,8192]{2,1,0:T(8,128)} reshape(f32[64,64,128]{2,1,0:T(8,128)} %fusion.64) | data formatting | bytes 4194304 | tf_op jit(solution)/shard_map/while/body/jit(dynamic_update_index_in_dim)/broadcast_in_dim | solution.py:91
  96.7 3.1 %constant_dynamic-update-slice_fusion.9 = f32[3,64,8192]{2,1,0:T(8,128)} fusion(f32[3,64,8192]{2,1,0:T(8,128)} %get-tuple-element.394, f32[1,64,8192]{2,1,0:T(8,128)} %broadcast_in_dim.100, s32[]{:T(128)} %get-tuple-element.392), kind=kLoop, calls=%fused_computation.37.clone.1.clone | loop fusion | bytes 4194816 | tf_op jit(solution)/shard_map/while/body/jit(dynamic_update_index_in_dim)/dynamic_update_slice | solution.py:91
  100.7 1.5 constant_dynamic-update-slice_fusion.11
  102.9 4.9 %all-to-all-start.1 = ((f32[1,8,8]{2,0,1:T(1,128)}), f32[1,8,8]{2,0,1:T(1,128)S(1)}, u32[]{:S(2)}, u32[]{:S(2)}) async-start(f32[1,8,8]{2,0,1:T(1,128)} %bitcast.27), calls=%async_computation.1 | async-start | bytes 8192 | tf_op jit(solution)/shard_map/all_to_all | solution.py:99
  107.7 10.8 %while.46 = (s32[]{:T(128)}, f32[64,8192]{1,0:T(8,128)}, f32[3,64]{1,0:T(4,128)S(1)}, f32[3,64,8192]{2,1,0:T(8,128)}) while((s32[]{:T(128)}, f32[64,8192]{1,0:T(8,128)}, f32[3,64]{1,0:T(4,128)S(1)}, f32[3,64,8192]{2,1,0:T(8,128)}) %tuple.74), condition=%wide.region_5.6_spmd.clone.clone, body=%wide.region_4.5_spmd.clone.sunk.clone | while | flops 1572867 | bytes 6292295 | solution.py:63
  107.7 3.2 %bitcast_add_fusion.7 = f32[64,8192]{1,0:T(8,128)} fusion(f32[64,8192]{1,0:T(8,128)} %get-tuple-element.417, f32[3,64,8192]{2,1,0:T(8,128)} %get-tuple-element.423, s32[]{:T(128)} %get-tuple-element.416, f32[64]{0:T(128)S(1)} %exponential_bitcast_fusion.3, pred[]{:T(512)S(6)} %compare.4), kind=kLoop, calls=%fused_computation.5.clone.1.clone | loop fusion | flops 1572864 | bytes 6291717 | tf_op jit(solution)/shard_map/while/body/eval_jaxpr/add | solution.py:61
  110.9 3.8 %bitcast_add_fusion.7 = f32[64,8192]{1,0:T(8,128)} fusion(f32[64,8192]{1,0:T(8,128)} %get-tuple-element.417, f32[3,64,8192]{2,1,0:T(8,128)} %get-tuple-element.423, s32[]{:T(128)} %get-tuple-element.416, f32[64]{0:T(128)S(1)} %exponential_bitcast_fusion.3, pred[]{:T(512)S(6)} %compare.4), kind=kLoop, calls=%fused_computation.5.clone.1.clone | loop fusion | flops 1572864 | bytes 6291717 | tf_op jit(solution)/shard_map/while/body/eval_jaxpr/add | solution.py:61
  114.7 3.8 %bitcast_add_fusion.7 = f32[64,8192]{1,0:T(8,128)} fusion(f32[64,8192]{1,0:T(8,128)} %get-tuple-element.417, f32[3,64,8192]{2,1,0:T(8,128)} %get-tuple-element.423, s32[]{:T(128)} %get-tuple-element.416, f32[64]{0:T(128)S(1)} %exponential_bitcast_fusion.3, pred[]{:T(512)S(6)} %compare.4), kind=kLoop, calls=%fused_computation.5.clone.1.clone | loop fusion | flops 1572864 | bytes 6291717 | tf_op jit(solution)/shard_map/while/body/eval_jaxpr/add | solution.py:61
  118.5 5.3 %broadcast_in_dim.83 = f32[1,64,8192]{2,0,1:T(1,128)} reshape(f32[64,8192]{1,0:T(8,128)} %get-tuple-element.114) | data formatting | bytes 4194304 | tf_op jit(solution)/shard_map/broadcast_in_dim | solution.py:98
  123.8 6.0 %all-to-all-start = ((f32[1,64,8192]{2,0,1:T(1,128)}), f32[1,64,8192]{2,0,1:T(1,128)S(1)}, u32[]{:S(2)}, u32[]{:S(2)}) async-start(f32[1,64,8192]{2,0,1:T(1,128)} %broadcast_in_dim.83), calls=%async_computation | async-start | bytes 4194304 | tf_op jit(solution)/shard_map/all_to_all | solution.py:98
  130.0 47.2 %all-to-all-done = f32[1,64,8192]{2,0,1:T(1,128)S(1)} async-done(((f32[1,64,8192]{2,0,1:T(1,128)}), f32[1,64,8192]{2,0,1:T(1,128)S(1)}, u32[]{:S(2)}, u32[]{:S(2)}) %all-to-all-start) | async-done | bytes 2097184 | tf_op jit(solution)/shard_map/all_to_all | solution.py:98
  177.2 1.2 copy.71
  178.4 3.1 %fusion.17 = bf16[8,8,8192]{2,0,1:T(8,128)(2,1)S(1)} fusion(f32[8,8,8192]{2,1,0:T(8,128)S(1)} %bitcast.164, f32[8,8]{1,0:T(8,128)S(1)} %copy.46, f32[8,8]{1,0:T(8,128)S(1)} %copy.45, pred[8,8]{1,0:T(8,128)(4,1)S(1)} %iota_compare_fusion.1), kind=kOutput, calls=%fused_computation.47 | convolution fusion | flops 50857472 | bytes 3146304 | tf_op jit(solution)/shard_map/hij,jhm->ihm/dot_general | solution.py:54
  181.5 1.6 copy.48
  183.1 3.6 %all-to-all-start.2 = ((bf16[8,8,8192]{2,1,0:T(8,128)(2,1)}), bf16[8,8,8192]{2,1,0:T(8,128)(2,1)S(1)}, u32[]{:S(2)}, u32[]{:S(2)}) async-start(bf16[8,8,8192]{2,1,0:T(8,128)(2,1)} %copy.48), calls=%async_computation.2 | async-start | bytes 2097152 | tf_op jit(solution)/shard_map/all_to_all | solution.py:101
  187.4 2.0 broadcast_convert_fusion
  190.1 22.6 %all-to-all-done.2 = bf16[8,8,8192]{2,1,0:T(8,128)(2,1)S(1)} async-done(((bf16[8,8,8192]{2,1,0:T(8,128)(2,1)}), bf16[8,8,8192]{2,1,0:T(8,128)(2,1)S(1)}, u32[]{:S(2)}, u32[]{:S(2)}) %all-to-all-start.2) | async-done | bytes 1048608 | tf_op jit(solution)/shard_map/all_to_all | solution.py:101
  212.8 11.8 %while.45 = (s32[]{:T(128)}, f32[64,8192]{1,0:T(8,128)S(1)}, bf16[3,64,8192]{2,1,0:T(8,128)(2,1)}, f32[3,64]{1,0:T(4,128)}, f32[3,64,8192]{2,1,0:T(8,128)}) while((s32[]{:T(128)}, f32[64,8192]{1,0:T(8,128)S(1)}, bf16[3,64,8192]{2,1,0:T(8,128)(2,1)}, f32[3,64]{1,0:T(4,128)}, f32[3,64,8192]{2,1,0:T(8,128)}) %tuple.83), condition=%wide.region_9.10_spmd.clone, body=%wide.region_8.9_spmd.sunk.clone | while | flops 1048578 | bytes 10487109 | solution.py:63
  212.9 1.2 bitcast_dynamic-update-slice_fusion.7
  214.7 2.1 bitcast_add_fusion.6
  218.6 2.1 bitcast_add_fusion.6
  222.5 2.1 bitcast_add_fusion.6
  224.6 2.8 %copy.57 = bf16[24,8,64,128]{3,2,1,0:T(8,128)(2,1)S(1)} copy(bf16[24,8,64,128]{3,1,2,0:T(8,128)(2,1)} %bitcast.162) | data formatting | bytes 6291456
  227.5 11.2 %multiply_reduce_fusion = (f32[3,64,256]{2,1,0:T(8,128)S(1)}, f32[3,64,64,256]{3,2,1,0:T(8,128)}) fusion(bf16[3,64,64,256]{3,2,1,0:T(8,128)(2,1)} %get-tuple-element.116, f32[64]{0:T(128)S(1)} %copy-done.4, f32[3,64,64,256]{3,2,1,0:T(8,128)} %get-tuple-element.110, bf16[3,256,256]{2,1,0:T(8,128)(2,1)S(1)} %get-tuple-element.442, ...), kind=kOutput, calls=%fused_computation.43 | convolution fusion | flops 827277312 | bytes 35193344 | tf_op jit(solution)/shard_map/chpn,cnt->chpt/dot_general | solution.py:113
  238.7 8.7 %multiply_convert_fusion.6 = bf16[3,64,64,256]{3,2,1,0:T(8,128)(2,1)} fusion(f32[3,64,64,256]{3,2,1,0:T(8,128)} %get-tuple-element.211, f32[64,64]{1,0:T(8,128)S(1)} %copy-done.2, f32[3,64,256]{2,1,0:T(8,128)S(1)} %add_rsqrt_fusion), kind=kLoop, calls=%fused_computation.42 | loop fusion | flops 9437184 | bytes 19087360 | tf_op jit(solution)/shard_map/convert_element_type | solution.py:123
  247.5 8.6 %copy.49 = bf16[3,256,4096]{2,1,0:T(8,128)(2,1)} copy(bf16[3,256,4096]{1,2,0:T(8,128)(2,1)} %bitcast.161) | data formatting | bytes 12582912 | tf_op jit(solution)/shard_map/transpose | solution.py:124
  (102 shorter events, 19.5 us)
Async XLA Ops:
  1.6 8.9 %collective-permute-start = (bf16[3,4352]{1,0:T(4,128)(2,1)S(1)}, bf16[3,4352]{1,0:T(4,128)(2,1)S(1)}, u32[]{:S(2)}, u32[]{:S(2)}) collective-permute-start(bf16[3,4352]{1,0:T(4,128)(2,1)S(1)} %pad_maximum_fusion.2), channel_id=1, source_target_pairs={{0,4},{4,8},{8,12},{12,16},{16,20},{20,24},{24,28},{1,5},{5,9},{9,... | collective-permute-start | bytes 78344 | tf_op jit(solution)/shard_map/ppermute | solution.py:12
  102.9 21.0 %all-to-all-start.1 = ((f32[1,8,8]{2,0,1:T(1,128)}), f32[1,8,8]{2,0,1:T(1,128)S(1)}, u32[]{:S(2)}, u32[]{:S(2)}) async-start(f32[1,8,8]{2,0,1:T(1,128)} %bitcast.27), calls=%async_computation.1 | async-start | bytes 8192 | tf_op jit(solution)/shard_map/all_to_all | solution.py:99
  118.5 59.9 %copy-start.5 = (f32[3,64]{1,0:T(4,128)}, f32[3,64]{1,0:T(4,128)S(1)}, u32[]{:S(2)}) copy-start(f32[3,64]{1,0:T(4,128)S(1)} %get-tuple-element.446) | copy-start | bytes 2308
  123.8 53.4 %all-to-all-start = ((f32[1,64,8192]{2,0,1:T(1,128)}), f32[1,64,8192]{2,0,1:T(1,128)S(1)}, u32[]{:S(2)}, u32[]{:S(2)}) async-start(f32[1,64,8192]{2,0,1:T(1,128)} %broadcast_in_dim.83), calls=%async_computation | async-start | bytes 4194304 | tf_op jit(solution)/shard_map/all_to_all | solution.py:98
  129.8 56.9 %copy-start.3 = (f32[4096]{0:T(1024)S(1)}, f32[4096]{0:T(1024)}, u32[]{:S(2)}) copy-start(f32[4096]{0:T(1024)} %param.21) | copy-start | bytes 49156
  178.4 11.0 %copy-start.1 = (f32[3,64,256]{2,1,0:T(8,128)S(1)}, f32[3,64,256]{2,1,0:T(8,128)}, u32[]{:S(2)}) copy-start(f32[3,64,256]{2,1,0:T(8,128)} %get-tuple-element.111) | copy-start | bytes 589828
  183.1 29.6 %all-to-all-start.2 = ((bf16[8,8,8192]{2,1,0:T(8,128)(2,1)}), bf16[8,8,8192]{2,1,0:T(8,128)(2,1)S(1)}, u32[]{:S(2)}, u32[]{:S(2)}) async-start(bf16[8,8,8192]{2,1,0:T(8,128)(2,1)} %copy.48), calls=%async_computation.2 | async-start | bytes 2097152 | tf_op jit(solution)/shard_map/all_to_all | solution.py:101
  224.6 2.8 %copy-start = (f32[3,64,256]{2,1,0:T(8,128)S(1)}, f32[3,64,256]{2,1,0:T(8,128)}, u32[]{:S(2)}) copy-start(f32[3,64,256]{2,1,0:T(8,128)} %exp.42) | copy-start | bytes 589828
  224.6 2.8 %copy-start.4 = (f32[64]{0:T(128)S(1)}, f32[64]{0:T(128)}, u32[]{:S(2)}) copy-start(f32[64]{0:T(128)} %param.20) | copy-start | bytes 772
  227.5 11.3 %copy-start.2 = (f32[64,64]{1,0:T(8,128)S(1)}, f32[64,64]{1,0:T(8,128)}, u32[]{:S(2)}) copy-start(f32[64,64]{1,0:T(8,128)} %mul.201) | copy-start | bytes 49156
where the time goes:
time: 258 us; the launch traced here: 256 us
  local copies, waits for them, and re-layouts  77.6 us (30%)
  waiting for transfers between devices  69.8 us (27%)
  other arithmetic  48.2 us (19%)
  matrix products  40.6 us (16%)
  starting transfers between devices  19.4 us (8%)
    all_to_all x1, waiting for transfers between devices, body(): lax.all_to_all(summary[None], 'ctx', split_axis=1, concat_axis=0, tiled=T...  47.2 us
    all_to_all x1, waiting for transfers between devices, body(): lax.all_to_all(owner_chain(states_in, totals_in).astype(jnp.bfloat16), 'c...  22.6 us
    dynamic_slice x12, local copies, waits for them, and re-layouts, body(): lax.map(lambda item: block_terms(item[0], item[1], item[2], item[3]), (in...  19.7 us
    dot_general x3, matrix products, block_terms(): jnp.einsum('hts,hps->hpt', weights, inner_cols, preferred_element_type=jn...  19.5 us
    dynamic_update_slice x15, local copies, waits for them, and re-layouts, body(): lax.map(lambda item: block_terms(item[0], item[1], item[2], item[3]), (in...  18.9 us
    convert_element_type x2, other arithmetic, silu_conv(): return jax.nn.silu(summed).astype(jnp.bfloat16)  17.3 us
    add x6, other arithmetic, advance(): jnp.exp(block_total)[:, None] * carry_state + block_state  17.1 us
    dot_general x1, matrix products, body(): jnp.einsum('chpn,cnt->chpt', entering_b, c_cols, preferred_element_type=j...  11.2 us
  transfers between devices with their start and end apart: 4, of which 2 were waited for; matrix products, arithmetic and copies ran while one was open for 9% of the time, Pallas kernels for 0%

commit v1 on v0

v1 whole, which is shorter than its diff:
```python
import jax
import jax.numpy as jnp
from jax import lax
from jax.experimental import pallas as pl
from jax.experimental.pallas import tpu as pltpu
from jax.sharding import PartitionSpec as P

CHUNK = 128
SQUARE = 4
GROUPS = 2
SUB = 256
EDGE = 16
F32 = jnp.float32
BF16 = jnp.bfloat16


def params(mib=16):
    return pltpu.CompilerParams(vmem_limit_bytes=mib * 1024 * 1024)


def dot(a, b):
    return jnp.dot(a, b, preferred_element_type=F32)


def exact_dot(a, b):
    return jnp.dot(a, b, preferred_element_type=F32, precision=lax.Precision.HIGHEST)


def iota(shape, axis):
    return lax.broadcasted_iota(jnp.int32, shape, axis)


def hi_lo(value):
    half = value.shape[1] // 2
    high = value.astype(BF16).astype(F32)
    return jnp.where(iota(value.shape, 1) < half, high, value - high).astype(BF16)


def spread(heads, head_width, first, cols):
    row = iota((2 * heads, cols), 0)
    row = jnp.where(row >= heads, row - heads, row)
    col = first + iota((2 * heads, cols), 1)
    low = row * head_width
    return jnp.where((col >= low) & (col < low + head_width), 1.0, 0.0).astype(BF16)


def silu_conv(window, half_taps):
    taps = len(half_taps)
    summed = window[8:] * half_taps[taps - 1]
    for back in range(1, taps):
        summed = summed + pltpu.roll(window, back, 0)[8:] * half_taps[taps - 1 - back]
    return (summed + summed * jnp.tanh(summed)).astype(BF16)


def decay_kernel(decay_ref, step_ref, skip_ref, fwd_ref, inv_ref, dev_ref, end_ref, fac_ref, total_ref):
    rows, heads = decay_ref.shape
    chunks = rows // CHUNK
    twice = jnp.where(iota((heads, 2 * heads), 0) == iota((heads, 2 * heads), 1) % heads, 1.0, 0.0)
    lower = jnp.where(iota((CHUNK, CHUNK), 0) >= iota((CHUNK, CHUNK), 1), 1.0, 0.0)
    cums, steps = [], []
    for c in range(chunks):
        at = pl.ds(c * CHUNK, CHUNK)
        cums.append(exact_dot(lower, exact_dot(decay_ref[at, :], twice)))
        steps.append(exact_dot(step_ref[at, :], twice))
    totals = [cum[CHUNK - 1 :] for cum in cums]
    middles = [cum[CHUNK // 2 - 1 : CHUNK // 2] for cum in cums]
    before = [jnp.zeros_like(totals[0])]
    for c in range(chunks):
        before.append(before[c] + totals[c])
    after = [jnp.zeros_like(totals[0])]
    for c in range(chunks - 1, 0, -1):
        after.insert(0, after[0] + totals[c])
    fac_rows = []
    for c in range(chunks):
        at = pl.ds(c * CHUNK, CHUNK)
        fwd_ref[at, :] = hi_lo(jnp.exp(cums[c] - middles[c]))
        inv_ref[at, :] = hi_lo(jnp.exp(middles[c] - cums[c]) * steps[c])
        dev_ref[at, :] = hi_lo(jnp.exp(before[c] + cums[c]))
        end_ref[at, :] = hi_lo(jnp.exp((totals[c] - cums[c]) + after[c]) * steps[c])
        following = middles[c + 1] if c + 1 < chunks else 0.0
        fac_rows.append(jnp.exp(totals[c] - middles[c] + following))
    skip = exact_dot(skip_ref[...], twice)
    row = iota((16, 2 * heads), 0)
    fac = jnp.where(row == chunks, skip[:1], 0.0)
    for c in range(chunks):
        fac = jnp.where(row == c, fac_rows[c], fac)
    fac_ref[...] = hi_lo(fac)
    total_ref[...] = jnp.broadcast_to(before[chunks], total_ref.shape)


def decays(decay_log, step_size, skip_weight):
    rows, heads = decay_log.shape
    wide = jax.ShapeDtypeStruct((rows, 2 * heads), BF16)
    return pl.pallas_call(
        decay_kernel,
        out_shape=(wide, wide, wide, wide, jax.ShapeDtypeStruct((16, 2 * heads), BF16), jax.ShapeDtypeStruct((8, 2 * heads), F32)),
        compiler_params=params(),
        name="decays",
    )(decay_log, step_size, jnp.broadcast_to(skip_weight[None], (8, heads)))


def chunk_window(ref, edge_ref, c, cols):
    if c == 0:
        past = edge_ref[:, cols].astype(F32)[EDGE - 8 :]
    else:
        past = ref[pl.ds(c * CHUNK - EDGE, EDGE), cols].astype(F32)[EDGE - 8 :]
    return jnp.concatenate([past, ref[pl.ds(c * CHUNK, CHUNK), cols].astype(F32)], axis=0)


def proj_kernel(proj_ref, edge_ref, taps_ref, mix_ref, bt_ref):
    rows, width = proj_ref.shape
    state = width // 2
    taps = [0.5 * taps_ref[k : k + 1, :] for k in range(taps_ref.shape[0])]
    causal = iota((CHUNK, CHUNK), 0) >= iota((CHUNK, CHUNK), 1)
    for c in range(rows // CHUNK):
        at = pl.ds(c * CHUNK, CHUNK)
        both = silu_conv(chunk_window(proj_ref, edge_ref, c, slice(None)), taps)
        b_rows, c_rows = both[:, :state], both[:, state:]
        b_cols = b_rows.astype(F32).T.astype(BF16)
        scores = dot(c_rows, b_cols)
        mix_ref[at, :CHUNK] = jnp.where(causal, scores, 0.0).astype(BF16)
        mix_ref[at, CHUNK:] = c_rows
        bt_ref[:, at] = b_cols


def projections(state_proj, edge, taps):
    rows, width = state_proj.shape
    state = width // 2
    return pl.pallas_call(
        proj_kernel,
        out_shape=(jax.ShapeDtypeStruct((rows, CHUNK + state), BF16), jax.ShapeDtypeStruct((state, rows), BF16)),
        compiler_params=params(),
        name="projections",
    )(state_proj, edge, taps)


def state_kernel(place_ref, in_ref, edge_ref, taps_ref, end_ref, bt_ref, x_ref, *rest, head_width, first):
    slots, scaled_ref = rest[:-1], rest[-1]
    rows, cols = in_ref.shape
    heads = end_ref.shape[1] // 2
    tile = pl.program_id(0)
    for sub in range(cols // SUB):
        at_cols = pl.ds(sub * SUB, SUB)
        table = spread(heads, head_width, first + tile * cols + sub * SUB, SUB)
        taps = [0.5 * taps_ref[k : k + 1, at_cols] for k in range(taps_ref.shape[0])]
        for c in range(rows // CHUNK):
            at = pl.ds(c * CHUNK, CHUNK)
            x = silu_conv(chunk_window(in_ref, edge_ref, c, at_cols), taps)
            x_ref[at, at_cols] = x
            scaled_ref[at, at_cols] = (dot(end_ref[at, :], table) * x.astype(F32)).astype(BF16)
    summary = dot(bt_ref[...], scaled_ref[...]).astype(BF16)
    slot = tile ^ place_ref[0]
    for k in range(len(slots)):

        @pl.when(slot == k)
        def _():
            slots[k][...] = summary


def device_states(place, inner, edge, taps, end, bt, head_width, group):
    rows, width = inner.shape
    state = bt.shape[0]
    wide = width // GROUPS
    cols = wide // SQUARE
    base = group * SQUARE
    whole = lambda a: pl.BlockSpec(a.shape, lambda j, p: (0,) * a.ndim)
    column = lambda n: pl.BlockSpec((n, cols), lambda j, p: (0, base + j))
    slot = jax.ShapeDtypeStruct((state, cols), BF16)
    out = pl.pallas_call(
        lambda *refs: state_kernel(*refs, head_width=head_width, first=group * wide),
        grid_spec=pltpu.PrefetchScalarGridSpec(
            num_scalar_prefetch=1,
            grid=(SQUARE,),
            in_specs=[column(rows), column(edge.shape[0]), column(taps.shape[0]), whole(end), whole(bt)],
            out_specs=[pl.BlockSpec((rows, cols), lambda j, p: (0, j))] + [pl.BlockSpec((state, cols), lambda j, p: (0, 0))] * SQUARE,
            scratch_shapes=[pltpu.VMEM((rows, cols), BF16)],
        ),
        out_shape=[jax.ShapeDtypeStruct((rows, wide), BF16)] + [slot] * SQUARE,
        compiler_params=params(),
        cost_estimate=pl.CostEstimate(flops=2 * rows * wide * 2 * state, bytes_accessed=4 * rows * wide, transcendentals=rows * wide),
        name="states",
    )(place, inner, edge, taps, end, bt)
    return out[0], out[1:]


def local_kernel(x_ref, fwd_ref, inv_ref, fac_ref, mix_ref, bt_ref, out_ref, both_ref, state_ref, *, head_width, first):
    rows, cols = x_ref.shape
    heads = fwd_ref.shape[1] // 2
    chunks = rows // CHUNK
    for sub in range(cols // SUB):
        at_cols = pl.ds(sub * SUB, SUB)
        table = spread(heads, head_width, first + pl.program_id(0) * cols + sub * SUB, SUB)
        factors = dot(fac_ref[...], table)
        skip = factors[chunks : chunks + 1]
        state = jnp.zeros((bt_ref.shape[0], SUB), F32)
        for c in range(chunks):
            at = pl.ds(c * CHUNK, CHUNK)
            x = x_ref[at, at_cols].astype(F32)
            scaled = (dot(inv_ref[at, :], table) * x).astype(BF16)
            both = jnp.concatenate([scaled, state.astype(BF16)], axis=0)
            mixed = dot(mix_ref[at, :], both)
            out_ref[at, at_cols] = dot(fwd_ref[at, :], table) * mixed + skip * x
            if c + 1 < chunks:
                state = factors[c : c + 1] * (state + dot(bt_ref[:, at], scaled))


def local_parts(x, fwd, inv, fac, mix, bt, head_width, group):
    rows, wide = x.shape
    cols = wide // SQUARE
    state = bt.shape[0]
    whole = lambda a: pl.BlockSpec(a.shape, lambda j: (0,) * a.ndim)
    column = pl.BlockSpec((rows, cols), lambda j: (0, j))
    return pl.pallas_call(
        lambda *refs: local_kernel(*refs, head_width=head_width, first=group * wide),
        grid=(SQUARE,),
        in_specs=[column, whole(fwd), whole(inv), whole(fac), whole(mix), whole(bt)],
        out_specs=column,
        out_shape=jax.ShapeDtypeStruct((rows, wide), F32),
        scratch_shapes=[pltpu.VMEM((CHUNK + state, SUB), BF16), pltpu.VMEM((state, SUB), F32)],
        compiler_params=params(),
        cost_estimate=pl.CostEstimate(flops=2 * rows * wide * 5 * state, bytes_accessed=6 * rows * wide, transcendentals=0),
        name="local",
    )(x, fwd, inv, fac, mix, bt)


def final_kernel(place_ref, local_ref, dev_ref, mix_ref, gain_ref, *rest, head_width, first):
    slots, out_ref, state_ref = rest[:-2], rest[-2], rest[-1]
    rows, cols = local_ref.shape
    heads = dev_ref.shape[1] // 2
    step = pl.program_id(0)
    tile = step ^ place_ref[0]
    for k in range(len(slots)):

        @pl.when(step == k)
        def _():
            state_ref[...] = slots[k][...]

    mean = jnp.where(iota((SUB, SUB), 0) // head_width == iota((SUB, SUB), 1) // head_width, 1.0 / head_width, 0.0).astype(BF16)
    for sub in range(cols // SUB):
        at_cols = pl.ds(sub * SUB, SUB)
        table = spread(heads, head_width, first + tile * cols + sub * SUB, SUB)
        gain = gain_ref[:, at_cols]
        for c in range(rows // CHUNK):
            at = pl.ds(c * CHUNK, CHUNK)
            carried = dot(mix_ref[at, CHUNK:], state_ref[:, at_cols])
            combined = local_ref[at, at_cols] + dot(dev_ref[at, :], table) * carried
            squares = dot((combined * combined).astype(BF16), mean)
            out_ref[at, at_cols] = (combined * lax.rsqrt(squares + 1e-05) * gain).astype(BF16)


def finish(place, local, dev, mix, gain, slots, head_width, group, into):
    rows, wide = local.shape
    cols = wide // SQUARE
    base = group * SQUARE
    whole = lambda a: pl.BlockSpec(a.shape, lambda k, p: (0,) * a.ndim)
    in_specs = [
        pl.BlockSpec((rows, cols), lambda k, p: (0, k ^ p[0])),
        whole(dev),
        whole(mix),
        pl.BlockSpec((1, cols), lambda k, p: (0, base + (k ^ p[0]))),
    ] + [whole(s) for s in slots]
    operands = [place, local, dev, mix, gain, *slots]
    aliases = {}
    if into is not None:
        in_specs.append(pl.BlockSpec(memory_space=pl.ANY))
        operands.append(into)
        aliases = {len(operands) - 1: 0}

    def kernel(*refs):
        count = 5 + len(slots)
        skipped = 0 if into is None else 1
        final_kernel(*refs[:count], *refs[count + skipped :], head_width=head_width, first=group * wide)

    return pl.pallas_call(
        kernel,
        grid_spec=pltpu.PrefetchScalarGridSpec(
            num_scalar_prefetch=1,
            grid=(SQUARE,),
            in_specs=in_specs,
            out_specs=pl.BlockSpec((rows, cols), lambda k, p: (0, base + (k ^ p[0]))),
            scratch_shapes=[pltpu.VMEM(slots[0].shape, BF16)],
        ),
        out_shape=jax.ShapeDtypeStruct((rows, wide * GROUPS), BF16),
        input_output_aliases=aliases,
        compiler_params=params(),
        cost_estimate=pl.CostEstimate(flops=2 * rows * wide * 512, bytes_accessed=6 * rows * wide, transcendentals=rows * wide),
        name="finish",
    )(*operands)


def shifted(x, by):
    length = lax.axis_size("ctx")
    return lax.ppermute(x, "ctx", [(i, i + by) for i in range(length - by)])


def swapped(x, k):
    length = lax.axis_size("ctx")
    return lax.ppermute(x, "ctx", [(i, i ^ k) for i in range(length)])


def per_column(weights, head_width):
    return jnp.repeat(weights, head_width, axis=-1)


def square_weights(totals, place):
    position = jnp.arange(SQUARE) ^ place
    between = lambda low, high: jnp.sum(jnp.where(((position > low) & (position < high))[:, None], totals, 0.0), axis=0)
    ends = [position[k] for k in range(SQUARE)] + [SQUARE]
    inner = jnp.stack([
        jnp.stack([jnp.where(position[q] < ends[k], jnp.exp(between(position[q], ends[k])), 0.0) for q in range(SQUARE)])
        for k in range(SQUARE + 1)
    ])
    opening = jnp.stack([jnp.exp(between(-1, ends[k])) for k in range(SQUARE)])
    return inner, opening, jnp.sum(totals, axis=0)


def previous_squares(leaving, total, head_width):
    squares = lax.axis_size("ctx") // SQUARE
    entering = shifted(leaving, SQUARE)
    span = 1
    if squares > 2:
        window = shifted(total, SQUARE)
    while span < squares - 1:
        behind = shifted(entering, SQUARE * span)
        entering = entering.astype(F32) + per_column(jnp.exp(window), head_width) * behind.astype(F32)
        entering = entering.astype(BF16)
        window = window + shifted(window, SQUARE * span)
        span *= 2
    return entering


def body(inner_input, state_proj, step_size, decay_log, conv_inner, conv_proj, skip_weight, norm_gain):
    rows, width = inner_input.shape
    heads = step_size.shape[1]
    head_width = width // heads
    spot = lax.axis_index("ctx") % SQUARE
    place = jnp.full((1,), spot, jnp.int32)
    edge_inner = shifted(inner_input[rows - EDGE :], 1)
    edge_proj = shifted(state_proj[rows - EDGE :], 1)
    fwd, inv, dev, end, fac, total = decays(decay_log, step_size, skip_weight)
    total = total[:1, :heads]
    totals = jnp.concatenate([total] + [swapped(total, k) for k in range(1, SQUARE)], axis=0)
    inner_weights, opening, square_total = square_weights(totals, spot)
    mix, bt = projections(state_proj, edge_proj, conv_proj)
    gain = norm_gain[None]
    wide = width // GROUPS
    xs, sent = [], []
    for group in range(GROUPS):
        x, slots = device_states(place, inner_input, edge_inner, conv_inner, end, bt, head_width, group)
        xs.append(x)
        sent.append([slots[0]] + [swapped(slots[k], k) for k in range(1, SQUARE)])
    quarter = wide // SQUARE
    quarter_heads = quarter // head_width
    returned = []
    for group in range(GROUPS):
        first = (group * SQUARE + spot) * quarter_heads
        pick = lambda w: per_column(lax.dynamic_slice_in_dim(w, first, quarter_heads, w.ndim - 1), head_width)
        weights, opened = pick(inner_weights), pick(opening)
        held = [s.astype(F32) for s in sent[group]]
        prefix = [sum(weights[k, q][None] * held[q] for q in range(SQUARE)) for k in range(SQUARE + 1)]
        leaving = prefix[SQUARE].astype(BF16)
        arrived = previous_squares(leaving, lax.dynamic_slice_in_dim(square_total, first, quarter_heads, 0), head_width).astype(F32)
        entering = [(prefix[k] + opened[k][None] * arrived).astype(BF16) for k in range(SQUARE)]
        returned.append([entering[0]] + [swapped(entering[k], k) for k in range(1, SQUARE)])
    locals_ = [local_parts(xs[g], fwd, inv, fac, mix, bt, head_width, g) for g in range(GROUPS)]
    out = None
    for group in range(GROUPS):
        out = finish(place, locals_[group], dev, mix, gain, returned[group], head_width, group, out)
    return out


def solution(mesh):
    split = P(("dp", "ctx"), None)
    return jax.shard_map(
        body, mesh=mesh, in_specs=(split, split, split, split, P(), P(), P(), P()), out_specs=split, check_vma=False
    )
```

time: 258 us -> 140 us (0.54)
  waiting for transfers between devices: 69.8 us -> 1.21 us
  local copies, waits for them, and re-layouts: 77.6 us -> 12.2 us
  Pallas kernels: 0 us -> 55.1 us
  matrix products: 40.6 us -> 0 us
  other arithmetic: 48.2 us -> 16.9 us
  between operations: 0.2 us -> 17.9 us
  starting transfers between devices: 19.4 us -> 35.7 us
    all_to_all x3 -> x0, waiting for transfers between devices: 69.8 us -> none  [the longest x1 47.2 us: body(): lax.all_to_all(summary[None], 'ctx', split_axis=1, concat_axis=0, tiled=T...]
    pallas_call x0 -> x8, Pallas kernels: none -> 55.1 us  [the longest x2 20.7 us: local_parts(): pl.pallas_call(lambda *refs: local_kernel(*refs, head_width=head_width, f...]
    dot_general x11 -> x0, matrix products: 40.6 us -> none  [the longest x3 19.5 us: block_terms(): jnp.einsum('hts,hps->hpt', weights, inner_cols, preferred_element_type=jn...]
    ppermute x1 -> x19, starting transfers between devices: 4.84 us -> 35.7 us  [the longest x15 20.9 us: swapped(): return lax.ppermute(x, 'ctx', [(i, i ^ k) for i in range(length)])]
    convert_element_type x4 -> x6, other arithmetic: 26.1 us -> 1.06 us  [the longest x4 0.85 us: body(): (prefix[k] + opened[k][None] * arrived).astype(BF16)]
    dynamic_slice x12 -> x2, local copies, waits for them, and re-layouts: 19.7 us -> 0.16 us  [body(): lax.dynamic_slice_in_dim(w, first, quarter_heads, w.ndim - 1)]
    dynamic_update_slice x15 -> x0, local copies, waits for them, and re-layouts: 18.9 us -> none  [body(): lax.map(lambda item: block_terms(item[0], item[1], item[2], item[3]), (in...]
    add x6 -> x0, other arithmetic: 17.1 us -> none  [advance(): jnp.exp(block_total)[:, None] * carry_state + block_state]
  transfers between devices with their start and end apart: 4 -> 19, of which waited for: 2 -> 2; matrix products, arithmetic and copies ran while one was open for 9% -> 15% of each run, Pallas kernels for 0% -> 27%
where the time goes in v1:
time: 140 us; the launch traced here: 139 us
  Pallas kernels  55.1 us (39%)
  starting transfers between devices  35.7 us (26%)
  between operations  17.9 us (13%)
  other arithmetic  16.9 us (12%)
  local copies, waits for them, and re-layouts  12.2 us (9%)
    ppermute x15, starting transfers between devices, swapped(): return lax.ppermute(x, 'ctx', [(i, i ^ k) for i in range(length)])  20.9 us
    pallas_call x2, Pallas kernels, local_parts(): pl.pallas_call(lambda *refs: local_kernel(*refs, head_width=head_width, f...  20.7 us
    pallas_call x2, Pallas kernels, finish(): pl.pallas_call(kernel, grid_spec=pltpu.PrefetchScalarGridSpec(num_scalar_...  19.2 us
    and x10, other arithmetic, square_weights(): (position > low) & (position < high)  15.5 us
    ppermute x4, starting transfers between devices, shifted(): return lax.ppermute(x, 'ctx', [(i, i + by) for i in range(length - by)])  14.8 us
    pallas_call x2, Pallas kernels, device_states(): pl.pallas_call(lambda *refs: state_kernel(*refs, head_width=head_width, f...  12.3 us
    unnamed x12, local copies, waits for them, and re-layouts  7.49 us
  transfers between devices with their start and end apart: 19, of which 2 were waited for; matrix products, arithmetic and copies ran while one was open for 15% of the time, Pallas kernels for 27%

profile of v1, /device:TPU:0, one launch (start us, length us, event | category | flops | bytes accessed | tf_op | source)
XLA Modules:
  0.0 139.1 jit_solution(2901865547308035859)
XLA Ops:
  0.0 1.1 copy.11.step_ref
  1.1 1.1 copy.10.decay_ref
  2.2 0.7 broadcast_in_dim.240.skip_ref
  2.9 2.3 %decays.1 = (bf16[768,128]{1,0:T(8,128)(2,1)S(1)}, bf16[768,128]{1,0:T(8,128)(2,1)S(1)}, bf16[768,128]{1,0:T(8,128)(2,1)S(1)}, bf16[768,128]{1,0:T(8,128)(2,1)S(...) custom-call(f32[768,64]{1,0:T(8,128)S(1)} %copy.10.decay_ref, f32[768,64]{1,0:T(8,128)S(1)} %copy.11.step_ref, ...), custom_call_target="tpu_custom_call" | custom-call | tf_op jit(solution)/shard_map/decays/pallas_call | solution.py:94
  5.1 4.0 %collective-permute-start.4 = (f32[1,64]{1,0:T(1,128)S(1)}, f32[1,64]{1,0:T(1,128)S(1)}, u32[]{:S(2)}, u32[]{:S(2)}) collective-permute-start(f32[1,64]{1,0:T(1,128)S(1)} %slice.241), channel_id=1, source_target_pairs={{0,12},{4,8},{8,4},{12,0},{16,28},{20,24},{24,20},{28,16},{1,13},{... | collective-permute-start | bytes 776 | tf_op jit(solution)/shard_map/ppermute | solution.py:298
  9.1 0.4 collective-permute-start.3
  9.8 0.7 slice.238
  10.5 3.7 %collective-permute-start.1 = (bf16[16,256]{1,0:T(8,128)(2,1)S(1)}, bf16[16,256]{1,0:T(8,128)(2,1)S(1)}, u32[]{:S(2)}, u32[]{:S(2)}) collective-permute-start(bf16[16,256]{1,0:T(8,128)(2,1)S(1)} %slice.238), channel_id=1, source_target_pairs={{0,4},{4,8},{8,12},{12,16},{16,20},{20,24},{24,28},{1,5},{5,9},{9,... | collective-permute-start | bytes 24584 | tf_op jit(solution)/shard_map/ppermute | solution.py:293
  14.2 0.9 slice.237
  15.1 3.5 %collective-permute-start = (bf16[16,4096]{1,0:T(8,128)(2,1)S(1)}, bf16[16,4096]{1,0:T(8,128)(2,1)S(1)}, u32[]{:S(2)}, u32[]{:S(2)}) collective-permute-start(bf16[16,4096]{1,0:T(8,128)(2,1)S(1)} %slice.237), channel_id=1, source_target_pairs={{0,4},{4,8},{8,12},{12,16},{16,20},{20,24},{24,28},{1,5},{5,9},{9,... | collective-permute-start | bytes 393224 | tf_op jit(solution)/shard_map/ppermute | solution.py:293
  18.6 0.7 fusion.86
  32.8 1.8 %fusion.72 = (pred[4]{0:T(512)(128)(4,1)S(1)}, pred[4]{0:T(512)(128)(4,1)S(1)}) fusion(s32[]{:T(128)} %bitcast.2, s32[]{:T(128)} %select_n.346, s32[]{:T(128)} %bitcast.7, s32[]{:T(128)} %bitcast.5), kind=kLoop, calls=%fused_computation.195 | loop fusion | flops 24 | bytes 24 | tf_op jit(solution)/shard_map/and | solution.py:307
  34.6 1.2 fusion.68
  35.8 1.9 %fusion.76 = (pred[4]{0:T(512)(128)(4,1)S(1)}, pred[4]{0:T(512)(128)(4,1)S(1)}) fusion(s32[]{:T(128)} %bitcast.2, s32[]{:T(128)} %select_n.346, s32[]{:T(128)} %bitcast.5, s32[]{:T(128)} %bitcast.3), kind=kLoop, calls=%fused_computation.199 | loop fusion | flops 24 | bytes 24 | tf_op jit(solution)/shard_map/and | solution.py:307
  37.7 1.2 fusion.82
  39.0 1.2 fusion.64
  40.2 1.8 %fusion.80 = (pred[4]{0:T(512)(128)(4,1)S(1)}, pred[4]{0:T(512)(128)(4,1)S(1)}) fusion(s32[]{:T(128)} %bitcast.3, s32[]{:T(128)} %select_n.346, s32[]{:T(128)} %bitcast.7, s32[]{:T(128)} %bitcast.5), kind=kLoop, calls=%fused_computation.203 | loop fusion | flops 24 | bytes 24 | tf_op jit(solution)/shard_map/and | solution.py:307
  42.0 1.8 %fusion.78 = (pred[4]{0:T(512)(128)(4,1)S(1)}, pred[4]{0:T(512)(128)(4,1)S(1)}) fusion(s32[]{:T(128)} %bitcast.3, s32[]{:T(128)} %select_n.346, s32[]{:T(128)} %bitcast.7, s32[]{:T(128)} %bitcast.5), kind=kLoop, calls=%fused_computation.201 | loop fusion | flops 24 | bytes 24 | tf_op jit(solution)/shard_map/and | solution.py:307
  43.9 1.8 %fusion.74 = (pred[4]{0:T(512)(128)(4,1)S(1)}, pred[4]{0:T(512)(128)(4,1)S(1)}) fusion(s32[]{:T(128)} %bitcast.2, s32[]{:T(128)} %select_n.346, s32[]{:T(128)} %bitcast.3, s32[]{:T(128)} %bitcast.7), kind=kLoop, calls=%fused_computation.197 | loop fusion | flops 28 | bytes 24 | tf_op jit(solution)/shard_map/and | solution.py:307
  45.7 1.3 fusion.66
  47.0 1.3 fusion.70
  54.6 1.0 copy-done.1
  55.6 0.7 copy-done.4
  56.3 0.6 projections.1
  56.9 2.8 %copy-done = bf16[768,4096]{1,0:T(8,128)(2,1)S(1)} copy-done((bf16[768,4096]{1,0:T(8,128)(2,1)S(1)}, bf16[768,4096]{1,0:T(8,128)(2,1)}, u32[]{:S(2)}) %copy-start) | copy-done | bytes 6291480
  59.7 0.8 copy-done.2
  60.6 6.2 %states.3 = (bf16[768,2048]{1,0:T(8,128)(2,1)S(1)}, bf16[128,512]{1,0:T(8,128)(2,1)S(1)}, bf16[128,512]{1,0:T(8,128)(2,1)S(1)}, bf16[128,512]{1,0:T(8,128)(2,1)S(1)}, bf16[128,512]{1,0:T(8,128)(2,1)S(1)}) custom-call(s32[1]{0:T(128)} %bitcast.refs_0_, bf16[768,4096]{1,0:T(8,128)(2,1)S(1)} %copy-done, bf16[16,4096]{1,0:T(8,128)(2,1)S(1)} %collective-permute-done.refs_2_, ...), custom_call_target="tpu_custom_call" | custom-call | flops 805306368 | bytes 6291456 | tf_op jit(solution)/shard_map/states/pallas_call | solution.py:169
  66.7 1.5 %collective-permute-start.12 = (bf16[128,512]{1,0:T(8,128)(2,1)S(1)}, bf16[128,512]{1,0:T(8,128)(2,1)S(1)}, u32[]{:S(2)}, u32[]{:S(2)}) collective-permute-start(bf16[128,512]{1,0:T(8,128)(2,1)S(1)} %get-tuple-element.38), channel_id=1, source_target_pairs={{0,4},{4,0},{8,12},{12,8},{16,20},{20,16},{24,28},{28,24},{1,5},{5... | collective-permute-start | bytes 393224 | tf_op jit(solution)/shard_map/ppermute | solution.py:298
  68.3 1.6 %collective-permute-start.13 = (bf16[128,512]{1,0:T(8,128)(2,1)S(1)}, bf16[128,512]{1,0:T(8,128)(2,1)S(1)}, u32[]{:S(2)}, u32[]{:S(2)}) collective-permute-start(bf16[128,512]{1,0:T(8,128)(2,1)S(1)} %get-tuple-element.39), channel_id=1, source_target_pairs={{0,8},{4,12},{8,0},{12,4},{16,24},{20,28},{24,16},{28,20},{1,9},{5... | collective-permute-start | bytes 393224 | tf_op jit(solution)/shard_map/ppermute | solution.py:298
  69.9 0.4 collective-permute-start.14
  70.3 6.2 %states.2 = (bf16[768,2048]{1,0:T(8,128)(2,1)S(1)}, bf16[128,512]{1,0:T(8,128)(2,1)S(1)}, bf16[128,512]{1,0:T(8,128)(2,1)S(1)}, bf16[128,512]{1,0:T(8,128)(2,1)S(1)}, bf16[128,512]{1,0:T(8,128)(2,1)S(1)}) custom-call(s32[1]{0:T(128)} %bitcast.refs_0_, bf16[768,4096]{1,0:T(8,128)(2,1)S(1)} %copy-done, bf16[16,4096]{1,0:T(8,128)(2,1)S(1)} %collective-permute-done.refs_2_, ...), custom_call_target="tpu_custom_call" | custom-call | flops 805306368 | bytes 6291456 | tf_op jit(solution)/shard_map/states/pallas_call | solution.py:169
  76.5 1.5 %collective-permute-start.5 = (bf16[128,512]{1,0:T(8,128)(2,1)S(1)}, bf16[128,512]{1,0:T(8,128)(2,1)S(1)}, u32[]{:S(2)}, u32[]{:S(2)}) collective-permute-start(bf16[128,512]{1,0:T(8,128)(2,1)S(1)} %get-tuple-element.33), channel_id=1, source_target_pairs={{0,4},{4,0},{8,12},{12,8},{16,20},{20,16},{24,28},{28,24},{1,5},{5... | collective-permute-start | bytes 393224 | tf_op jit(solution)/shard_map/ppermute | solution.py:298
  78.0 1.6 %collective-permute-start.6 = (bf16[128,512]{1,0:T(8,128)(2,1)S(1)}, bf16[128,512]{1,0:T(8,128)(2,1)S(1)}, u32[]{:S(2)}, u32[]{:S(2)}) collective-permute-start(bf16[128,512]{1,0:T(8,128)(2,1)S(1)} %get-tuple-element.34), channel_id=1, source_target_pairs={{0,8},{4,12},{8,0},{12,4},{16,24},{20,28},{24,16},{28,20},{1,9},{5... | collective-permute-start | bytes 393224 | tf_op jit(solution)/shard_map/ppermute | solution.py:298
  79.6 10.3 %local.3.refs_1_ = f32[768,2048]{1,0:T(8,128)S(1)} custom-call(bf16[768,2048]{1,0:T(8,128)(2,1)S(1)} %get-tuple-element.36.refs_0_, bf16[768,128]{1,0:T(8,128)(2,1)S(1)} %get-tuple-element.26.refs_1_, bf16[768,128]{1,0:T(8,128)(2,1)S(1)} %get-tuple-element.27.refs_2_, bf16[16,128]{1,0:T(8,128)(2,1)S(1)} %get-tuple-element.28.refs_3_, ...), custom_call_target="tpu_custom_call" | custom-call | flops 2013265920 | bytes 9437184 | tf_op jit(solution)/shard_map/local/pallas_call | solution.py:213
  90.0 10.3 %local.2.refs_1_ = f32[768,2048]{1,0:T(8,128)S(1)} custom-call(bf16[768,2048]{1,0:T(8,128)(2,1)S(1)} %get-tuple-element.25.refs_0_, bf16[768,128]{1,0:T(8,128)(2,1)S(1)} %get-tuple-element.26.refs_1_, bf16[768,128]{1,0:T(8,128)(2,1)S(1)} %get-tuple-element.27.refs_2_, bf16[16,128]{1,0:T(8,128)(2,1)S(1)} %get-tuple-element.28.refs_3_, ...), custom_call_target="tpu_custom_call" | custom-call | flops 2013265920 | bytes 9437184 | tf_op jit(solution)/shard_map/local/pallas_call | solution.py:213
  100.3 0.5 collective-permute-start.7
  100.9 4.5 %collective-permute-start.15 = (bf16[128,512]{1,0:T(8,128)(2,1)S(1)}, bf16[128,512]{1,0:T(8,128)(2,1)S(1)}, u32[]{:S(2)}, u32[]{:S(2)}) collective-permute-start(bf16[128,512]{1,0:T(8,128)(2,1)S(1)} %fusion.38), channel_id=1, source_target_pairs={{0,16},{4,20},{8,24},{12,28},{1,17},{5,21},{9,25},{13,29},{2,18},{... | collective-permute-start | bytes 393224 | tf_op jit(solution)/shard_map/ppermute | solution.py:293
  105.4 0.8 collective-permute-done.7
  106.4 3.1 %collective-permute-start.8 = (bf16[128,512]{1,0:T(8,128)(2,1)S(1)}, bf16[128,512]{1,0:T(8,128)(2,1)S(1)}, u32[]{:S(2)}, u32[]{:S(2)}) collective-permute-start(bf16[128,512]{1,0:T(8,128)(2,1)S(1)} %fusion.22), channel_id=1, source_target_pairs={{0,16},{4,20},{8,24},{12,28},{1,17},{5,21},{9,25},{13,29},{2,18},{... | collective-permute-start | bytes 393224 | tf_op jit(solution)/shard_map/ppermute | solution.py:293
  109.7 3.5 %collective-permute-start.18 = (bf16[128,512]{1,0:T(8,128)(2,1)S(1)}, bf16[128,512]{1,0:T(8,128)(2,1)S(1)}, u32[]{:S(2)}, u32[]{:S(2)}) collective-permute-start(bf16[128,512]{1,0:T(8,128)(2,1)S(1)} %get-tuple-element.62), channel_id=1, source_target_pairs={{0,12},{4,8},{8,4},{12,0},{16,28},{20,24},{24,20},{28,16},{1,13},{... | collective-permute-start | bytes 393224 | tf_op jit(solution)/shard_map/ppermute | solution.py:298
  113.2 0.4 collective-permute-start.16
  113.9 0.3 collective-permute-start.17
  114.4 2.9 %collective-permute-start.11 = (bf16[128,512]{1,0:T(8,128)(2,1)S(1)}, bf16[128,512]{1,0:T(8,128)(2,1)S(1)}, u32[]{:S(2)}, u32[]{:S(2)}) collective-permute-start(bf16[128,512]{1,0:T(8,128)(2,1)S(1)} %get-tuple-element.66), channel_id=1, source_target_pairs={{0,12},{4,8},{8,4},{12,0},{16,28},{20,24},{24,20},{28,16},{1,13},{... | collective-permute-start | bytes 393224 | tf_op jit(solution)/shard_map/ppermute | solution.py:298
  117.3 0.4 collective-permute-start.9
  117.9 1.6 %collective-permute-start.10 = (bf16[128,512]{1,0:T(8,128)(2,1)S(1)}, bf16[128,512]{1,0:T(8,128)(2,1)S(1)}, u32[]{:S(2)}, u32[]{:S(2)}) collective-permute-start(bf16[128,512]{1,0:T(8,128)(2,1)S(1)} %get-tuple-element.68), channel_id=1, source_target_pairs={{0,8},{4,12},{8,0},{12,4},{16,24},{20,28},{24,16},{28,20},{1,9},{5... | collective-permute-start | bytes 393224 | tf_op jit(solution)/shard_map/ppermute | solution.py:298
  119.5 0.3 collective-permute-done.16.refs_6_
  119.8 9.6 %finish.2.refs_9_ = bf16[768,4096]{1,0:T(8,128)(2,1)} custom-call(s32[1]{0:T(128)} %bitcast.refs_0_, f32[768,2048]{1,0:T(8,128)S(1)} %local.3.refs_1_, bf16[768,128]{1,0:T(8,128)(2,1)S(1)} %get-tuple-element.30.refs_2_, bf16[768,256]{1,0:T(8,128)(2,1)S(1)} %get-tuple-element.29.refs_4_.refs_3_, f32[1,4096]{1,0:T(1,128)S(1)} %bitcast.126, ...), custom_call_target="tpu_custom_call" | custom-call | flops 1610612736 | bytes 9437184 | tf_op jit(solution)/shard_map/finish/pallas_call | solution.py:274
  129.4 9.6 %finish.3 = bf16[768,4096]{1,0:T(8,128)(2,1)} custom-call(s32[1]{0:T(128)} %bitcast.refs_0_, f32[768,2048]{1,0:T(8,128)S(1)} %local.2.refs_1_, bf16[768,128]{1,0:T(8,128)(2,1)S(1)} %get-tuple-element.30.refs_2_, bf16[768,256]{1,0:T(8,128)(2,1)S(1)} %get-tuple-element.29.refs_4_.refs_3_, f32[1,4096]{1,0:T(1,128)S(1)} %bitcast.127, ...), custom_call_target="tpu_custom_call", output_to_operand_aliasing={{}: (9, {})} | custom-call | flops 1610612736 | bytes 9437184 | tf_op jit(solution)/shard_map/finish/pallas_call | solution.py:274
  (89 shorter events, 3.5 us)
Async XLA Ops:
  5.1 47.0 %collective-permute-start.4 = (f32[1,64]{1,0:T(1,128)S(1)}, f32[1,64]{1,0:T(1,128)S(1)}, u32[]{:S(2)}, u32[]{:S(2)}) collective-permute-start(f32[1,64]{1,0:T(1,128)S(1)} %slice.241), channel_id=1, source_target_pairs={{0,12},{4,8},{8,4},{12,0},{16,28},{20,24},{24,20},{28,16},{1,13},{... | collective-permute-start | bytes 776 | tf_op jit(solution)/shard_map/ppermute | solution.py:298
  9.1 43.0 %collective-permute-start.3 = (f32[1,64]{1,0:T(1,128)S(1)}, f32[1,64]{1,0:T(1,128)S(1)}, u32[]{:S(2)}, u32[]{:S(2)}) collective-permute-start(f32[1,64]{1,0:T(1,128)S(1)} %slice.241), channel_id=1, source_target_pairs={{0,8},{4,12},{8,0},{12,4},{16,24},{20,28},{24,16},{28,20},{1,9},{5... | collective-permute-start | bytes 776 | tf_op jit(solution)/shard_map/ppermute | solution.py:298
  9.6 42.6 %collective-permute-start.2 = (f32[1,64]{1,0:T(1,128)S(1)}, f32[1,64]{1,0:T(1,128)S(1)}, u32[]{:S(2)}, u32[]{:S(2)}) collective-permute-start(f32[1,64]{1,0:T(1,128)S(1)} %slice.241), channel_id=1, source_target_pairs={{0,4},{4,0},{8,12},{12,8},{16,20},{20,16},{24,28},{28,24},{1,5},{5... | collective-permute-start | bytes 776 | tf_op jit(solution)/shard_map/ppermute | solution.py:298
  10.5 44.1 %collective-permute-start.1 = (bf16[16,256]{1,0:T(8,128)(2,1)S(1)}, bf16[16,256]{1,0:T(8,128)(2,1)S(1)}, u32[]{:S(2)}, u32[]{:S(2)}) collective-permute-start(bf16[16,256]{1,0:T(8,128)(2,1)S(1)} %slice.238), channel_id=1, source_target_pairs={{0,4},{4,8},{8,12},{12,16},{16,20},{20,24},{24,28},{1,5},{5,9},{9,... | collective-permute-start | bytes 24584 | tf_op jit(solution)/shard_map/ppermute | solution.py:293
  15.1 41.8 %collective-permute-start = (bf16[16,4096]{1,0:T(8,128)(2,1)S(1)}, bf16[16,4096]{1,0:T(8,128)(2,1)S(1)}, u32[]{:S(2)}, u32[]{:S(2)}) collective-permute-start(bf16[16,4096]{1,0:T(8,128)(2,1)S(1)} %slice.237), channel_id=1, source_target_pairs={{0,4},{4,8},{8,12},{12,16},{16,20},{20,24},{24,28},{1,5},{5,9},{9,... | collective-permute-start | bytes 393224 | tf_op jit(solution)/shard_map/ppermute | solution.py:293
  54.6 1.0 copy-start.1
  55.6 0.7 copy-start.4
  56.9 2.8 %copy-start = (bf16[768,4096]{1,0:T(8,128)(2,1)S(1)}, bf16[768,4096]{1,0:T(8,128)(2,1)}, u32[]{:S(2)}) copy-start(bf16[768,4096]{1,0:T(8,128)(2,1)} %refs_1_.3) | copy-start | bytes 18874372
  59.7 0.8 copy-start.2
  66.7 33.6 %collective-permute-start.12 = (bf16[128,512]{1,0:T(8,128)(2,1)S(1)}, bf16[128,512]{1,0:T(8,128)(2,1)S(1)}, u32[]{:S(2)}, u32[]{:S(2)}) collective-permute-start(bf16[128,512]{1,0:T(8,128)(2,1)S(1)} %get-tuple-element.38), channel_id=1, source_target_pairs={{0,4},{4,0},{8,12},{12,8},{16,20},{20,16},{24,28},{28,24},{1,5},{5... | collective-permute-start | bytes 393224 | tf_op jit(solution)/shard_map/ppermute | solution.py:298
  68.3 32.5 %collective-permute-start.13 = (bf16[128,512]{1,0:T(8,128)(2,1)S(1)}, bf16[128,512]{1,0:T(8,128)(2,1)S(1)}, u32[]{:S(2)}, u32[]{:S(2)}) collective-permute-start(bf16[128,512]{1,0:T(8,128)(2,1)S(1)} %get-tuple-element.39), channel_id=1, source_target_pairs={{0,8},{4,12},{8,0},{12,4},{16,24},{20,28},{24,16},{28,20},{1,9},{5... | collective-permute-start | bytes 393224 | tf_op jit(solution)/shard_map/ppermute | solution.py:298
  69.9 30.9 %collective-permute-start.14 = (bf16[128,512]{1,0:T(8,128)(2,1)S(1)}, bf16[128,512]{1,0:T(8,128)(2,1)S(1)}, u32[]{:S(2)}, u32[]{:S(2)}) collective-permute-start(bf16[128,512]{1,0:T(8,128)(2,1)S(1)} %get-tuple-element.40), channel_id=1, source_target_pairs={{0,12},{4,8},{8,4},{12,0},{16,28},{20,24},{24,20},{28,16},{1,13},{... | collective-permute-start | bytes 393224 | tf_op jit(solution)/shard_map/ppermute | solution.py:298
  76.5 28.9 %collective-permute-start.5 = (bf16[128,512]{1,0:T(8,128)(2,1)S(1)}, bf16[128,512]{1,0:T(8,128)(2,1)S(1)}, u32[]{:S(2)}, u32[]{:S(2)}) collective-permute-start(bf16[128,512]{1,0:T(8,128)(2,1)S(1)} %get-tuple-element.33), channel_id=1, source_target_pairs={{0,4},{4,0},{8,12},{12,8},{16,20},{20,16},{24,28},{28,24},{1,5},{5... | collective-permute-start | bytes 393224 | tf_op jit(solution)/shard_map/ppermute | solution.py:298
  78.0 27.4 %collective-permute-start.6 = (bf16[128,512]{1,0:T(8,128)(2,1)S(1)}, bf16[128,512]{1,0:T(8,128)(2,1)S(1)}, u32[]{:S(2)}, u32[]{:S(2)}) collective-permute-start(bf16[128,512]{1,0:T(8,128)(2,1)S(1)} %get-tuple-element.34), channel_id=1, source_target_pairs={{0,8},{4,12},{8,0},{12,4},{16,24},{20,28},{24,16},{28,20},{1,9},{5... | collective-permute-start | bytes 393224 | tf_op jit(solution)/shard_map/ppermute | solution.py:298
  90.0 29.9 %copy-start.3 = (f32[4096]{0:T(1024)S(1)}, f32[4096]{0:T(1024)}, u32[]{:S(2)}) copy-start(f32[4096]{0:T(1024)} %param.15) | copy-start | bytes 49156
  100.3 5.9 %collective-permute-start.7 = (bf16[128,512]{1,0:T(8,128)(2,1)S(1)}, bf16[128,512]{1,0:T(8,128)(2,1)S(1)}, u32[]{:S(2)}, u32[]{:S(2)}) collective-permute-start(bf16[128,512]{1,0:T(8,128)(2,1)S(1)} %get-tuple-element.35), channel_id=1, source_target_pairs={{0,12},{4,8},{8,4},{12,0},{16,28},{20,24},{24,20},{28,16},{1,13},{... | collective-permute-start | bytes 393224 | tf_op jit(solution)/shard_map/ppermute | solution.py:298
  100.9 8.6 %collective-permute-start.15 = (bf16[128,512]{1,0:T(8,128)(2,1)S(1)}, bf16[128,512]{1,0:T(8,128)(2,1)S(1)}, u32[]{:S(2)}, u32[]{:S(2)}) collective-permute-start(bf16[128,512]{1,0:T(8,128)(2,1)S(1)} %fusion.38), channel_id=1, source_target_pairs={{0,16},{4,20},{8,24},{12,28},{1,17},{5,21},{9,25},{13,29},{2,18},{... | collective-permute-start | bytes 393224 | tf_op jit(solution)/shard_map/ppermute | solution.py:293
  106.4 7.8 %collective-permute-start.8 = (bf16[128,512]{1,0:T(8,128)(2,1)S(1)}, bf16[128,512]{1,0:T(8,128)(2,1)S(1)}, u32[]{:S(2)}, u32[]{:S(2)}) collective-permute-start(bf16[128,512]{1,0:T(8,128)(2,1)S(1)} %fusion.22), channel_id=1, source_target_pairs={{0,16},{4,20},{8,24},{12,28},{1,17},{5,21},{9,25},{13,29},{2,18},{... | collective-permute-start | bytes 393224 | tf_op jit(solution)/shard_map/ppermute | solution.py:293
  109.7 8.2 %collective-permute-start.18 = (bf16[128,512]{1,0:T(8,128)(2,1)S(1)}, bf16[128,512]{1,0:T(8,128)(2,1)S(1)}, u32[]{:S(2)}, u32[]{:S(2)}) collective-permute-start(bf16[128,512]{1,0:T(8,128)(2,1)S(1)} %get-tuple-element.62), channel_id=1, source_target_pairs={{0,12},{4,8},{8,4},{12,0},{16,28},{20,24},{24,20},{28,16},{1,13},{... | collective-permute-start | bytes 393224 | tf_op jit(solution)/shard_map/ppermute | solution.py:298
  113.2 6.6 %collective-permute-start.16 = (bf16[128,512]{1,0:T(8,128)(2,1)S(1)}, bf16[128,512]{1,0:T(8,128)(2,1)S(1)}, u32[]{:S(2)}, u32[]{:S(2)}) collective-permute-start(bf16[128,512]{1,0:T(8,128)(2,1)S(1)} %get-tuple-element.63), channel_id=1, source_target_pairs={{0,4},{4,0},{8,12},{12,8},{16,20},{20,16},{24,28},{28,24},{1,5},{5... | collective-permute-start | bytes 393224 | tf_op jit(solution)/shard_map/ppermute | solution.py:298
  113.9 6.0 %collective-permute-start.17 = (bf16[128,512]{1,0:T(8,128)(2,1)S(1)}, bf16[128,512]{1,0:T(8,128)(2,1)S(1)}, u32[]{:S(2)}, u32[]{:S(2)}) collective-permute-start(bf16[128,512]{1,0:T(8,128)(2,1)S(1)} %get-tuple-element.64), channel_id=1, source_target_pairs={{0,8},{4,12},{8,0},{12,4},{16,24},{20,28},{24,16},{28,20},{1,9},{5... | collective-permute-start | bytes 393224 | tf_op jit(solution)/shard_map/ppermute | solution.py:298
  114.4 15.0 %collective-permute-start.11 = (bf16[128,512]{1,0:T(8,128)(2,1)S(1)}, bf16[128,512]{1,0:T(8,128)(2,1)S(1)}, u32[]{:S(2)}, u32[]{:S(2)}) collective-permute-start(bf16[128,512]{1,0:T(8,128)(2,1)S(1)} %get-tuple-element.66), channel_id=1, source_target_pairs={{0,12},{4,8},{8,4},{12,0},{16,28},{20,24},{24,20},{28,16},{1,13},{... | collective-permute-start | bytes 393224 | tf_op jit(solution)/shard_map/ppermute | solution.py:298
  117.3 12.1 %collective-permute-start.9 = (bf16[128,512]{1,0:T(8,128)(2,1)S(1)}, bf16[128,512]{1,0:T(8,128)(2,1)S(1)}, u32[]{:S(2)}, u32[]{:S(2)}) collective-permute-start(bf16[128,512]{1,0:T(8,128)(2,1)S(1)} %get-tuple-element.67), channel_id=1, source_target_pairs={{0,4},{4,0},{8,12},{12,8},{16,20},{20,16},{24,28},{28,24},{1,5},{5... | collective-permute-start | bytes 393224 | tf_op jit(solution)/shard_map/ppermute | solution.py:298
  117.9 11.5 %collective-permute-start.10 = (bf16[128,512]{1,0:T(8,128)(2,1)S(1)}, bf16[128,512]{1,0:T(8,128)(2,1)S(1)}, u32[]{:S(2)}, u32[]{:S(2)}) collective-permute-start(bf16[128,512]{1,0:T(8,128)(2,1)S(1)} %get-tuple-element.68), channel_id=1, source_target_pairs={{0,8},{4,12},{8,0},{12,4},{16,24},{20,28},{24,16},{28,20},{1,9},{5... | collective-permute-start | bytes 393224 | tf_op jit(solution)/shard_map/ppermute | solution.py:298

commit v2 on v1

--- a/solution.py
+++ b/solution.py
@@ -126,8 +126,13 @@
 def projections(state_proj, edge, taps):
     rows, width = state_proj.shape
     state = width // 2
+    whole = lambda a, b: pl.BlockSpec((a, b), lambda i: (0, 0))
+    last = edge.shape[1] // width - 1
     return pl.pallas_call(
         proj_kernel,
+        grid=(1,),
+        in_specs=[whole(rows, width), pl.BlockSpec((EDGE, width), lambda i: (0, last)), whole(*taps.shape)],
+        out_specs=(whole(rows, CHUNK + state), whole(state, rows)),
         out_shape=(jax.ShapeDtypeStruct((rows, CHUNK + state), BF16), jax.ShapeDtypeStruct((state, rows), BF16)),
         compiler_params=params(),
         name="projections",
@@ -145,9 +150,8 @@
         taps = [0.5 * taps_ref[k : k + 1, at_cols] for k in range(taps_ref.shape[0])]
         for c in range(rows // CHUNK):
             at = pl.ds(c * CHUNK, CHUNK)
-            x = silu_conv(chunk_window(in_ref, edge_ref, c, at_cols), taps)
-            x_ref[at, at_cols] = x
-            scaled_ref[at, at_cols] = (dot(end_ref[at, :], table) * x.astype(F32)).astype(BF16)
+            x_ref[at, at_cols] = silu_conv(chunk_window(in_ref, edge_ref, c, at_cols), taps)
+        scaled_ref[:, at_cols] = (dot(end_ref[...], table) * x_ref[:, at_cols].astype(F32)).astype(BF16)
     summary = dot(bt_ref[...], scaled_ref[...]).astype(BF16)
     slot = tile ^ place_ref[0]
     for k in range(len(slots)):
@@ -183,7 +187,7 @@
     return out[0], out[1:]
 
 
-def local_kernel(x_ref, fwd_ref, inv_ref, fac_ref, mix_ref, bt_ref, out_ref, both_ref, state_ref, *, head_width, first):
+def local_kernel(x_ref, fwd_ref, inv_ref, fac_ref, mix_ref, bt_ref, out_ref, *, head_width, first):
     rows, cols = x_ref.shape
     heads = fwd_ref.shape[1] // 2
     chunks = rows // CHUNK
@@ -193,13 +197,15 @@
         factors = dot(fac_ref[...], table)
         skip = factors[chunks : chunks + 1]
         state = jnp.zeros((bt_ref.shape[0], SUB), F32)
+        all_scaled = (dot(inv_ref[...], table) * x_ref[:, at_cols].astype(F32)).astype(BF16)
+        forward = dot(fwd_ref[...], table)
         for c in range(chunks):
             at = pl.ds(c * CHUNK, CHUNK)
             x = x_ref[at, at_cols].astype(F32)
-            scaled = (dot(inv_ref[at, :], table) * x).astype(BF16)
+            scaled = all_scaled[c * CHUNK : (c + 1) * CHUNK]
             both = jnp.concatenate([scaled, state.astype(BF16)], axis=0)
             mixed = dot(mix_ref[at, :], both)
-            out_ref[at, at_cols] = dot(fwd_ref[at, :], table) * mixed + skip * x
+            out_ref[at, at_cols] = forward[c * CHUNK : (c + 1) * CHUNK] * mixed + skip * x
             if c + 1 < chunks:
                 state = factors[c : c + 1] * (state + dot(bt_ref[:, at], scaled))
 
@@ -216,7 +222,6 @@
         in_specs=[column, whole(fwd), whole(inv), whole(fac), whole(mix), whole(bt)],
         out_specs=column,
         out_shape=jax.ShapeDtypeStruct((rows, wide), F32),
-        scratch_shapes=[pltpu.VMEM((CHUNK + state, SUB), BF16), pltpu.VMEM((state, SUB), F32)],
         compiler_params=params(),
         cost_estimate=pl.CostEstimate(flops=2 * rows * wide * 5 * state, bytes_accessed=6 * rows * wide, transcendentals=0),
         name="local",
@@ -239,13 +244,10 @@
     for sub in range(cols // SUB):
         at_cols = pl.ds(sub * SUB, SUB)
         table = spread(heads, head_width, first + tile * cols + sub * SUB, SUB)
-        gain = gain_ref[:, at_cols]
-        for c in range(rows // CHUNK):
-            at = pl.ds(c * CHUNK, CHUNK)
-            carried = dot(mix_ref[at, CHUNK:], state_ref[:, at_cols])
-            combined = local_ref[at, at_cols] + dot(dev_ref[at, :], table) * carried
-            squares = dot((combined * combined).astype(BF16), mean)
-            out_ref[at, at_cols] = (combined * lax.rsqrt(squares + 1e-05) * gain).astype(BF16)
+        carried = dot(mix_ref[:, CHUNK:], state_ref[:, at_cols])
+        combined = local_ref[:, at_cols] + dot(dev_ref[...], table) * carried
+        squares = dot((combined * combined).astype(BF16), mean)
+        out_ref[:, at_cols] = (combined * lax.rsqrt(squares + 1e-05) * gain_ref[:, at_cols]).astype(BF16)
 
 
 def finish(place, local, dev, mix, gain, slots, head_width, group, into):
@@ -298,23 +300,46 @@
     return lax.ppermute(x, "ctx", [(i, i ^ k) for i in range(length)])
 
 
-def per_column(weights, head_width):
-    return jnp.repeat(weights, head_width, axis=-1)
-
-
-def square_weights(totals, place):
-    position = jnp.arange(SQUARE) ^ place
-    between = lambda low, high: jnp.sum(jnp.where(((position > low) & (position < high))[:, None], totals, 0.0), axis=0)
-    ends = [position[k] for k in range(SQUARE)] + [SQUARE]
-    inner = jnp.stack([
-        jnp.stack([jnp.where(position[q] < ends[k], jnp.exp(between(position[q], ends[k])), 0.0) for q in range(SQUARE)])
-        for k in range(SQUARE + 1)
-    ])
-    opening = jnp.stack([jnp.exp(between(-1, ends[k])) for k in range(SQUARE)])
-    return inner, opening, jnp.sum(totals, axis=0)
-
-
-def previous_squares(leaving, total, head_width):
+def weights_kernel(place_ref, *refs, head_width):
+    total_refs, out_ref = refs[:-1], refs[-1]
+    groups, _, cols = out_ref.shape
+    wide = total_refs[0].shape[1]
+    spot = place_ref[0]
+    places = [spot ^ k for k in range(SQUARE)]
+    for group in range(groups):
+        low = iota((wide, cols), 0) * head_width
+        col = (group * SQUARE + spot) * cols + iota((wide, cols), 1)
+        table = jnp.where((col >= low) & (col < low + head_width), 1.0, 0.0)
+        logs = [exact_dot(ref[...], table)[:1] for ref in total_refs]
+        between = lambda low, high: sum(jnp.where((at > low) & (at < high), log, 0.0) for at, log in zip(places, logs))
+        for k, end in enumerate(places + [SQUARE]):
+            for q in range(SQUARE):
+                weight = jnp.where(places[q] < end, jnp.exp(between(places[q], end)), 0.0)
+                out_ref[group, k * SQUARE + q : k * SQUARE + q + 1, :] = weight
+        for k in range(SQUARE):
+            row = SQUARE * (SQUARE + 1) + k
+            out_ref[group, row : row + 1, :] = jnp.exp(between(-1, places[k]))
+        row = SQUARE * (SQUARE + 2)
+        out_ref[group, row : row + 1, :] = sum(logs)
+
+
+def square_weights(place, totals, width, head_width):
+    cols = width // (GROUPS * SQUARE)
+    return pl.pallas_call(
+        lambda *refs: weights_kernel(*refs, head_width=head_width),
+        grid_spec=pltpu.PrefetchScalarGridSpec(
+            num_scalar_prefetch=1,
+            grid=(1,),
+            in_specs=[pl.BlockSpec(t.shape, lambda i, p: (0, 0)) for t in totals],
+            out_specs=pl.BlockSpec((GROUPS, 32, cols), lambda i, p: (0, 0, 0)),
+        ),
+        out_shape=jax.ShapeDtypeStruct((GROUPS, 32, cols), F32),
+        compiler_params=params(),
+        name="weights",
+    )(place, *totals)
+
+
+def previous_squares(leaving, total):
     squares = lax.axis_size("ctx") // SQUARE
     entering = shifted(leaving, SQUARE)
     span = 1
@@ -322,8 +347,7 @@
         window = shifted(total, SQUARE)
     while span < squares - 1:
         behind = shifted(entering, SQUARE * span)
-        entering = entering.astype(F32) + per_column(jnp.exp(window), head_width) * behind.astype(F32)
-        entering = entering.astype(BF16)
+        entering = (entering.astype(F32) + jnp.exp(window) * behind.astype(F32)).astype(BF16)
         window = window + shifted(window, SQUARE * span)
         span *= 2
     return entering
@@ -333,36 +357,31 @@
     rows, width = inner_input.shape
     heads = step_size.shape[1]
     head_width = width // heads
-    spot = lax.axis_index("ctx") % SQUARE
-    place = jnp.full((1,), spot, jnp.int32)
-    edge_inner = shifted(inner_input[rows - EDGE :], 1)
-    edge_proj = shifted(state_proj[rows - EDGE :], 1)
+    place = jnp.full((1,), lax.axis_index("ctx") % SQUARE, jnp.int32)
+    edge = shifted(jnp.concatenate([inner_input[rows - EDGE :], state_proj[rows - EDGE :]], axis=1), 1)
     fwd, inv, dev, end, fac, total = decays(decay_log, step_size, skip_weight)
-    total = total[:1, :heads]
-    totals = jnp.concatenate([total] + [swapped(total, k) for k in range(1, SQUARE)], axis=0)
-    inner_weights, opening, square_total = square_weights(totals, spot)
-    mix, bt = projections(state_proj, edge_proj, conv_proj)
+    totals = [total] + [swapped(total, k) for k in range(1, SQUARE)]
+    mix, bt = projections(state_proj, edge, conv_proj)
     gain = norm_gain[None]
-    wide = width // GROUPS
     xs, sent = [], []
     for group in range(GROUPS):
-        x, slots = device_states(place, inner_input, edge_inner, conv_inner, end, bt, head_width, group)
+        x, slots = device_states(place, inner_input, edge, conv_inner, end, bt, head_width, group)
         xs.append(x)
         sent.append([slots[0]] + [swapped(slots[k], k) for k in range(1, SQUARE)])
-    quarter = wide // SQUARE
-    quarter_heads = quarter // head_width
-    returned = []
+    weights = square_weights(place, totals, width, head_width)
+    returned, locals_ = [], []
     for group in range(GROUPS):
-        first = (group * SQUARE + spot) * quarter_heads
-        pick = lambda w: per_column(lax.dynamic_slice_in_dim(w, first, quarter_heads, w.ndim - 1), head_width)
-        weights, opened = pick(inner_weights), pick(opening)
+        x = xs[group]
+        if group:
+            x, leaving = lax.optimization_barrier((x, leaving))
+        locals_.append(local_parts(x, fwd, inv, fac, mix, bt, head_width, group))
+        w = [weights[group, r : r + 1] for r in range(SQUARE * (SQUARE + 2) + 1)]
         held = [s.astype(F32) for s in sent[group]]
-        prefix = [sum(weights[k, q][None] * held[q] for q in range(SQUARE)) for k in range(SQUARE + 1)]
+        prefix = [sum(w[k * SQUARE + q] * held[q] for q in range(SQUARE)) for k in range(SQUARE + 1)]
         leaving = prefix[SQUARE].astype(BF16)
-        arrived = previous_squares(leaving, lax.dynamic_slice_in_dim(square_total, first, quarter_heads, 0), head_width).astype(F32)
-        entering = [(prefix[k] + opened[k][None] * arrived).astype(BF16) for k in range(SQUARE)]
+        arrived = previous_squares(leaving, w[SQUARE * (SQUARE + 2)]).astype(F32)
+        entering = [(prefix[k] + w[SQUARE * (SQUARE + 1) + k] * arrived).astype(BF16) for k in range(SQUARE)]
         returned.append([entering[0]] + [swapped(entering[k], k) for k in range(1, SQUARE)])
-    locals_ = [local_parts(xs[g], fwd, inv, fac, mix, bt, head_width, g) for g in range(GROUPS)]
     out = None
     for group in range(GROUPS):
         out = finish(place, locals_[group], dev, mix, gain, returned[group], head_width, group, out)

time: 140 us -> 85.9 us (0.61)
  between operations: 17.9 us -> 0.24 us
  Pallas kernels: 55.1 us -> 38.3 us
  other arithmetic: 16.9 us -> 1.08 us
  local copies, waits for them, and re-layouts: 12.2 us -> 9.85 us
  starting transfers between devices: 35.7 us -> 34.3 us
    and x10 -> x0, other arithmetic: 15.5 us -> none  [square_weights(): (position > low) & (position < high)]
    pallas_call x2, Pallas kernels: 20.7 us -> 11.3 us  [local_parts(): pl.pallas_call(lambda *refs: local_kernel(*refs, head_width=head_width, f...]
    pallas_call x2, Pallas kernels: 19.2 us -> 10.1 us  [finish(): pl.pallas_call(kernel, grid_spec=pltpu.PrefetchScalarGridSpec(num_scalar_...]
    ppermute x4 -> x3, starting transfers between devices: 14.8 us -> 13.5 us  [shifted(): return lax.ppermute(x, 'ctx', [(i, i + by) for i in range(length - by)])]
  transfers between devices with their start and end apart: 19 -> 18, of which waited for: 2 -> 2; matrix products, arithmetic and copies ran while one was open for 15% -> 3% of each run, Pallas kernels for 27% -> 28%
where the time goes in v2:
time: 85.9 us; the launch traced here: 85.5 us
  Pallas kernels  38.3 us (45%)
  starting transfers between devices  34.3 us (40%)
  local copies, waits for them, and re-layouts  9.85 us (11%)
  waiting for transfers between devices  1.72 us (2%)
  other arithmetic  1.08 us (1%)
    ppermute x15, starting transfers between devices, swapped(): return lax.ppermute(x, 'ctx', [(i, i ^ k) for i in range(length)])  20.9 us
    ppermute x3, starting transfers between devices, shifted(): return lax.ppermute(x, 'ctx', [(i, i + by) for i in range(length - by)])  13.5 us
    pallas_call x2, Pallas kernels, device_states(): pl.pallas_call(lambda *refs: state_kernel(*refs, head_width=head_width, f...  12.8 us
    pallas_call x2, Pallas kernels, local_parts(): pl.pallas_call(lambda *refs: local_kernel(*refs, head_width=head_width, f...  11.3 us
    pallas_call x2, Pallas kernels, finish(): pl.pallas_call(kernel, grid_spec=pltpu.PrefetchScalarGridSpec(num_scalar_...  10.1 us
    unnamed x12, local copies, waits for them, and re-layouts  7.49 us
    pallas_call x1, Pallas kernels, decays(): pl.pallas_call(decay_kernel, out_shape=(wide, wide, wide, wide, jax.Shape...  2.25 us
  transfers between devices with their start and end apart: 18, of which 2 were waited for; matrix products, arithmetic and copies ran while one was open for 3% of the time, Pallas kernels for 28%

profile of v2, /device:TPU:0, one launch (start us, length us, event | category | flops | bytes accessed | tf_op | source)
XLA Modules:
  0.0 85.5 jit_solution(17054960085662586929)
XLA Ops:
  0.0 1.1 %copy.10.decay_ref = f32[768,64]{1,0:T(8,128)S(1)} copy(f32[768,64]{0,1:T(8,128)} %param.11) | data formatting | bytes 393216 | tf_op args[3]
  1.1 1.1 %copy.11.step_ref = f32[768,64]{1,0:T(8,128)S(1)} copy(f32[768,64]{0,1:T(8,128)} %param.10) | data formatting | bytes 393216 | tf_op args[2]
  2.2 0.7 broadcast_in_dim.13.skip_ref
  2.9 2.3 %decays.1 = (bf16[768,128]{1,0:T(8,128)(2,1)S(1)}, bf16[768,128]{1,0:T(8,128)(2,1)S(1)}, bf16[768,128]{1,0:T(8,128)(2,1)S(1)}, bf16[768,128]{1,0:T(8,128)(2,1)S(...) custom-call(f32[768,64]{1,0:T(8,128)S(1)} %copy.10.decay_ref, f32[768,64]{1,0:T(8,128)S(1)} %copy.11.step_ref, ...), custom_call_target="tpu_custom_call" | custom-call | tf_op jit(solution)/shard_map/decays/pallas_call | solution.py:94
  5.1 3.0 %collective-permute-start.1 = (f32[8,128]{1,0:T(8,128)S(1)}, f32[8,128]{1,0:T(8,128)S(1)}, u32[]{:S(2)}, u32[]{:S(2)}) collective-permute-start(f32[8,128]{1,0:T(8,128)S(1)} %get-tuple-element.27.refs_1_), channel_id=1, source_target_pairs={{0,4},{4,0},{8,12},{12,8},{16,20},{20,16},{24,28},{28,24},{1,5},{5... | collective-permute-start | bytes 12296 | tf_op jit(solution)/shard_map/ppermute | solution.py:300
  8.1 1.6 %collective-permute-start.2 = (f32[8,128]{1,0:T(8,128)S(1)}, f32[8,128]{1,0:T(8,128)S(1)}, u32[]{:S(2)}, u32[]{:S(2)}) collective-permute-start(f32[8,128]{1,0:T(8,128)S(1)} %get-tuple-element.27.refs_1_), channel_id=1, source_target_pairs={{0,8},{4,12},{8,0},{12,4},{16,24},{20,28},{24,16},{28,20},{1,9},{5... | collective-permute-start | bytes 12296 | tf_op jit(solution)/shard_map/ppermute | solution.py:300
  9.7 0.0 collective-permute-start.3
  9.7 0.9 %slice.150 = bf16[16,4096]{1,0:T(8,128)(2,1)S(1)} slice(bf16[768,4096]{1,0:T(8,128)(2,1)} %refs_1_.3), slice={[752:768], [0:4096]} | slice | bytes 262144 | tf_op jit(solution)/shard_map/slice | solution.py:361
  10.6 0.7 slice.151
  11.3 3.8 %collective-permute-start = (bf16[16,4352]{1,0:T(8,128)(2,1)S(1)}, bf16[16,4352]{1,0:T(8,128)(2,1)S(1)}, u32[]{:S(2)}, u32[]{:S(2)}) collective-permute-start(bf16[16,4352]{1,0:T(8,128)(2,1)S(1)} %pad_maximum_fusion), channel_id=1, source_target_pairs={{0,4},{4,8},{8,12},{12,16},{16,20},{20,24},{24,28},{1,5},{5,9},{9,... | collective-permute-start | bytes 417800 | tf_op jit(solution)/shard_map/ppermute | solution.py:295
  15.2 0.0 collective-permute-done.1.refs_2_
  15.2 0.0 collective-permute-done.2.refs_3_
  15.2 1.1 %weights.1 = f32[2,32,512]{2,1,0:T(8,128)S(1)} custom-call(s32[1]{0:T(128)} %bitcast.refs_0_, f32[8,128]{1,0:T(8,128)S(1)} %get-tuple-element.27.refs_1_, f32[8,128]{1,0:T(8,128)S(1)} %collective-permute-done.1.refs_2_, f32[8,128]{1,0:T(8,128)S(1)} %collective-permute-done.2.refs_3_, f32[8,128]{1,0:T(8,128)S(1)} %collective-permute-done.3.refs_4_), custom_call_target="tpu_custom_call" | custom-call | tf_op jit(solution)/shard_map/weights/pallas_call | solution.py:328
  16.5 1.3 %collective-permute-done.edge_ref.refs_2_ = bf16[16,4352]{1,0:T(8,128)(2,1)S(1)} collective-permute-done((bf16[16,4352]{1,0:T(8,128)(2,1)S(1)}, bf16[16,4352]{1,0:T(8,128)(2,1)S(1)}, u32[]{:S(2)}, u32[]{:S(2)}) %collective-permute-start) | collective-permute-done | bytes 139296 | tf_op jit(solution)/shard_map/ppermute | solution.py:295
  17.7 1.0 %copy-done.1 = bf16[768,256]{1,0:T(8,128)(2,1)S(1)} copy-done((bf16[768,256]{1,0:T(8,128)(2,1)S(1)}, bf16[768,256]{1,0:T(8,128)(2,1)}, u32[]{:S(2)}) %copy-start.1) | copy-done | bytes 393240
  18.7 0.7 copy-done.4
  19.4 0.6 projections.1
  20.1 2.8 %copy-done = bf16[768,4096]{1,0:T(8,128)(2,1)S(1)} copy-done((bf16[768,4096]{1,0:T(8,128)(2,1)S(1)}, bf16[768,4096]{1,0:T(8,128)(2,1)}, u32[]{:S(2)}) %copy-start) | copy-done | bytes 6291480
  22.8 0.8 copy-done.2
  23.7 6.4 %states.3 = (bf16[768,2048]{1,0:T(8,128)(2,1)S(1)}, bf16[128,512]{1,0:T(8,128)(2,1)S(1)}, bf16[128,512]{1,0:T(8,128)(2,1)S(1)}, bf16[128,512]{1,0:T(8,128)(2,1)S(1)}, bf16[128,512]{1,0:T(8,128)(2,1)S(1)}) custom-call(s32[1]{0:T(128)} %bitcast.refs_0_, bf16[768,4096]{1,0:T(8,128)(2,1)S(1)} %copy-done, ...), custom_call_target="tpu_custom_call" | custom-call | flops 805306368 | bytes 6291456 | tf_op jit(solution)/shard_map/states/pallas_call | solution.py:173
  30.1 2.5 %collective-permute-start.4 = (bf16[128,512]{1,0:T(8,128)(2,1)S(1)}, bf16[128,512]{1,0:T(8,128)(2,1)S(1)}, u32[]{:S(2)}, u32[]{:S(2)}) collective-permute-start(bf16[128,512]{1,0:T(8,128)(2,1)S(1)} %get-tuple-element.29), channel_id=1, source_target_pairs={{0,4},{4,0},{8,12},{12,8},{16,20},{20,16},{24,28},{28,24},{1,5},{5... | collective-permute-start | bytes 393224 | tf_op jit(solution)/shard_map/ppermute | solution.py:300
  32.6 1.6 %collective-permute-start.5 = (bf16[128,512]{1,0:T(8,128)(2,1)S(1)}, bf16[128,512]{1,0:T(8,128)(2,1)S(1)}, u32[]{:S(2)}, u32[]{:S(2)}) collective-permute-start(bf16[128,512]{1,0:T(8,128)(2,1)S(1)} %get-tuple-element.30), channel_id=1, source_target_pairs={{0,8},{4,12},{8,0},{12,4},{16,24},{20,28},{24,16},{28,20},{1,9},{5... | collective-permute-start | bytes 393224 | tf_op jit(solution)/shard_map/ppermute | solution.py:300
  34.2 0.9 %collective-permute-start.6 = (bf16[128,512]{1,0:T(8,128)(2,1)S(1)}, bf16[128,512]{1,0:T(8,128)(2,1)S(1)}, u32[]{:S(2)}, u32[]{:S(2)}) collective-permute-start(bf16[128,512]{1,0:T(8,128)(2,1)S(1)} %get-tuple-element.31), channel_id=1, source_target_pairs={{0,12},{4,8},{8,4},{12,0},{16,28},{20,24},{24,20},{28,16},{1,13},{... | collective-permute-start | bytes 393224 | tf_op jit(solution)/shard_map/ppermute | solution.py:300
  35.1 6.4 %states.2 = (bf16[768,2048]{1,0:T(8,128)(2,1)S(1)}, bf16[128,512]{1,0:T(8,128)(2,1)S(1)}, bf16[128,512]{1,0:T(8,128)(2,1)S(1)}, bf16[128,512]{1,0:T(8,128)(2,1)S(1)}, bf16[128,512]{1,0:T(8,128)(2,1)S(1)}) custom-call(s32[1]{0:T(128)} %bitcast.refs_0_, bf16[768,4096]{1,0:T(8,128)(2,1)S(1)} %copy-done, ...), custom_call_target="tpu_custom_call" | custom-call | flops 805306368 | bytes 6291456 | tf_op jit(solution)/shard_map/states/pallas_call | solution.py:173
  41.5 1.1 %collective-permute-start.7 = (bf16[128,512]{1,0:T(8,128)(2,1)S(1)}, bf16[128,512]{1,0:T(8,128)(2,1)S(1)}, u32[]{:S(2)}, u32[]{:S(2)}) collective-permute-start(bf16[128,512]{1,0:T(8,128)(2,1)S(1)} %get-tuple-element.39), channel_id=1, source_target_pairs={{0,4},{4,0},{8,12},{12,8},{16,20},{20,16},{24,28},{28,24},{1,5},{5... | collective-permute-start | bytes 393224 | tf_op jit(solution)/shard_map/ppermute | solution.py:300
  42.6 1.6 %collective-permute-start.8 = (bf16[128,512]{1,0:T(8,128)(2,1)S(1)}, bf16[128,512]{1,0:T(8,128)(2,1)S(1)}, u32[]{:S(2)}, u32[]{:S(2)}) collective-permute-start(bf16[128,512]{1,0:T(8,128)(2,1)S(1)} %get-tuple-element.40), channel_id=1, source_target_pairs={{0,8},{4,12},{8,0},{12,4},{16,24},{20,28},{24,16},{28,20},{1,9},{5... | collective-permute-start | bytes 393224 | tf_op jit(solution)/shard_map/ppermute | solution.py:300
  44.2 5.6 %local.3.refs_1_ = f32[768,2048]{1,0:T(8,128)S(1)} custom-call(bf16[768,2048]{1,0:T(8,128)(2,1)S(1)} %get-tuple-element.42.refs_0_, bf16[768,128]{1,0:T(8,128)(2,1)S(1)} %get-tuple-element.33.refs_1_, bf16[768,128]{1,0:T(8,128)(2,1)S(1)} %get-tuple-element.34.refs_2_, bf16[16,128]{1,0:T(8,128)(2,1)S(1)} %get-tuple-element.35.refs_3_, ...), custom_call_target="tpu_custom_call" | custom-call | flops 2013265920 | bytes 9437184 | tf_op jit(solution)/shard_map/local/pallas_call | solution.py:219
  49.8 0.9 %collective-permute-start.9 = (bf16[128,512]{1,0:T(8,128)(2,1)S(1)}, bf16[128,512]{1,0:T(8,128)(2,1)S(1)}, u32[]{:S(2)}, u32[]{:S(2)}) collective-permute-start(bf16[128,512]{1,0:T(8,128)(2,1)S(1)} %get-tuple-element.41), channel_id=1, source_target_pairs={{0,12},{4,8},{8,4},{12,0},{16,28},{20,24},{24,20},{28,16},{1,13},{... | collective-permute-start | bytes 393224 | tf_op jit(solution)/shard_map/ppermute | solution.py:300
  50.8 0.0 collective-permute-done.5
  50.8 0.1 fusion.19
  50.9 4.9 %collective-permute-start.14 = (bf16[128,512]{1,0:T(8,128)(2,1)S(1)}, bf16[128,512]{1,0:T(8,128)(2,1)S(1)}, u32[]{:S(2)}, u32[]{:S(2)}) collective-permute-start(bf16[128,512]{1,0:T(8,128)(2,1)S(1)} %fusion.19), channel_id=1, source_target_pairs={{0,16},{4,20},{8,24},{12,28},{1,17},{5,21},{9,25},{13,29},{2,18},{... | collective-permute-start | bytes 393224 | tf_op jit(solution)/shard_map/ppermute | solution.py:295
  55.9 0.1 fusion.38
  56.0 4.7 %collective-permute-start.10 = (bf16[128,512]{1,0:T(8,128)(2,1)S(1)}, bf16[128,512]{1,0:T(8,128)(2,1)S(1)}, u32[]{:S(2)}, u32[]{:S(2)}) collective-permute-start(bf16[128,512]{1,0:T(8,128)(2,1)S(1)} %fusion.38), channel_id=1, source_target_pairs={{0,16},{4,20},{8,24},{12,28},{1,17},{5,21},{9,25},{13,29},{2,18},{... | collective-permute-start | bytes 393224 | tf_op jit(solution)/shard_map/ppermute | solution.py:295
  60.7 0.0 copy-start.3
  60.7 5.6 %local.2.refs_1_ = f32[768,2048]{1,0:T(8,128)S(1)} custom-call(bf16[768,2048]{1,0:T(8,128)(2,1)S(1)} %get-tuple-element.32.refs_0_, bf16[768,128]{1,0:T(8,128)(2,1)S(1)} %get-tuple-element.33.refs_1_, bf16[768,128]{1,0:T(8,128)(2,1)S(1)} %get-tuple-element.34.refs_2_, bf16[16,128]{1,0:T(8,128)(2,1)S(1)} %get-tuple-element.35.refs_3_, ...), custom_call_target="tpu_custom_call" | custom-call | flops 2013265920 | bytes 9437184 | tf_op jit(solution)/shard_map/local/pallas_call | solution.py:219
  66.3 0.2 fusion.15
  66.6 1.4 %collective-permute-start.15 = (bf16[128,512]{1,0:T(8,128)(2,1)S(1)}, bf16[128,512]{1,0:T(8,128)(2,1)S(1)}, u32[]{:S(2)}, u32[]{:S(2)}) collective-permute-start(bf16[128,512]{1,0:T(8,128)(2,1)S(1)} %get-tuple-element.44), channel_id=1, source_target_pairs={{0,4},{4,0},{8,12},{12,8},{16,20},{20,16},{24,28},{28,24},{1,5},{5... | collective-permute-start | bytes 393224 | tf_op jit(solution)/shard_map/ppermute | solution.py:300
  67.9 2.1 %collective-permute-start.17 = (bf16[128,512]{1,0:T(8,128)(2,1)S(1)}, bf16[128,512]{1,0:T(8,128)(2,1)S(1)}, u32[]{:S(2)}, u32[]{:S(2)}) collective-permute-start(bf16[128,512]{1,0:T(8,128)(2,1)S(1)} %get-tuple-element.43), channel_id=1, source_target_pairs={{0,12},{4,8},{8,4},{12,0},{16,28},{20,24},{24,20},{28,16},{1,13},{... | collective-permute-start | bytes 393224 | tf_op jit(solution)/shard_map/ppermute | solution.py:300
  70.1 0.2 fusion.13
  70.3 0.6 collective-permute-start.16
  70.8 0.2 fusion.7
  71.0 1.6 %collective-permute-start.11 = (bf16[128,512]{1,0:T(8,128)(2,1)S(1)}, bf16[128,512]{1,0:T(8,128)(2,1)S(1)}, u32[]{:S(2)}, u32[]{:S(2)}) collective-permute-start(bf16[128,512]{1,0:T(8,128)(2,1)S(1)} %get-tuple-element.48), channel_id=1, source_target_pairs={{0,4},{4,0},{8,12},{12,8},{16,20},{20,16},{24,28},{28,24},{1,5},{5... | collective-permute-start | bytes 393224 | tf_op jit(solution)/shard_map/ppermute | solution.py:300
  72.6 1.5 %collective-permute-start.13 = (bf16[128,512]{1,0:T(8,128)(2,1)S(1)}, bf16[128,512]{1,0:T(8,128)(2,1)S(1)}, u32[]{:S(2)}, u32[]{:S(2)}) collective-permute-start(bf16[128,512]{1,0:T(8,128)(2,1)S(1)} %get-tuple-element.47), channel_id=1, source_target_pairs={{0,12},{4,8},{8,4},{12,0},{16,28},{20,24},{24,20},{28,16},{1,13},{... | collective-permute-start | bytes 393224 | tf_op jit(solution)/shard_map/ppermute | solution.py:300
  74.1 0.2 fusion.5
  74.3 0.6 collective-permute-start.12
  74.9 0.4 collective-permute-done.16.refs_7_
  75.3 5.0 %finish.2.refs_9_ = bf16[768,4096]{1,0:T(8,128)(2,1)} custom-call(s32[1]{0:T(128)} %bitcast.refs_0_, f32[768,2048]{1,0:T(8,128)S(1)} %local.3.refs_1_, bf16[768,128]{1,0:T(8,128)(2,1)S(1)} %get-tuple-element.37.refs_2_, bf16[768,256]{1,0:T(8,128)(2,1)S(1)} %get-tuple-element.36.refs_4_.refs_3_, f32[1,4096]{1,0:T(1,128)S(1)} %bitcast.50, ...), custom_call_target="tpu_custom_call" | custom-call | flops 1610612736 | bytes 9437184 | tf_op jit(solution)/shard_map/finish/pallas_call | solution.py:276
  80.4 5.1 %finish.3 = bf16[768,4096]{1,0:T(8,128)(2,1)} custom-call(s32[1]{0:T(128)} %bitcast.refs_0_, f32[768,2048]{1,0:T(8,128)S(1)} %local.2.refs_1_, bf16[768,128]{1,0:T(8,128)(2,1)S(1)} %get-tuple-element.37.refs_2_, bf16[768,256]{1,0:T(8,128)(2,1)S(1)} %get-tuple-element.36.refs_4_.refs_3_, f32[1,4096]{1,0:T(1,128)S(1)} %bitcast.51, ...), custom_call_target="tpu_custom_call", output_to_operand_aliasing={{}: (9, {})} | custom-call | flops 1610612736 | bytes 9437184 | tf_op jit(solution)/shard_map/finish/pallas_call | solution.py:276
  (22 shorter events, 0.1 us)
Async XLA Ops:
  5.1 10.1 %collective-permute-start.1 = (f32[8,128]{1,0:T(8,128)S(1)}, f32[8,128]{1,0:T(8,128)S(1)}, u32[]{:S(2)}, u32[]{:S(2)}) collective-permute-start(f32[8,128]{1,0:T(8,128)S(1)} %get-tuple-element.27.refs_1_), channel_id=1, source_target_pairs={{0,4},{4,0},{8,12},{12,8},{16,20},{20,16},{24,28},{28,24},{1,5},{5... | collective-permute-start | bytes 12296 | tf_op jit(solution)/shard_map/ppermute | solution.py:300
  8.1 7.1 %collective-permute-start.2 = (f32[8,128]{1,0:T(8,128)S(1)}, f32[8,128]{1,0:T(8,128)S(1)}, u32[]{:S(2)}, u32[]{:S(2)}) collective-permute-start(f32[8,128]{1,0:T(8,128)S(1)} %get-tuple-element.27.refs_1_), channel_id=1, source_target_pairs={{0,8},{4,12},{8,0},{12,4},{16,24},{20,28},{24,16},{28,20},{1,9},{5... | collective-permute-start | bytes 12296 | tf_op jit(solution)/shard_map/ppermute | solution.py:300
  9.7 5.5 %collective-permute-start.3 = (f32[8,128]{1,0:T(8,128)S(1)}, f32[8,128]{1,0:T(8,128)S(1)}, u32[]{:S(2)}, u32[]{:S(2)}) collective-permute-start(f32[8,128]{1,0:T(8,128)S(1)} %get-tuple-element.27.refs_1_), channel_id=1, source_target_pairs={{0,12},{4,8},{8,4},{12,0},{16,28},{20,24},{24,20},{28,16},{1,13},{... | collective-permute-start | bytes 12296 | tf_op jit(solution)/shard_map/ppermute | solution.py:300
  11.3 6.4 %collective-permute-start = (bf16[16,4352]{1,0:T(8,128)(2,1)S(1)}, bf16[16,4352]{1,0:T(8,128)(2,1)S(1)}, u32[]{:S(2)}, u32[]{:S(2)}) collective-permute-start(bf16[16,4352]{1,0:T(8,128)(2,1)S(1)} %pad_maximum_fusion), channel_id=1, source_target_pairs={{0,4},{4,8},{8,12},{12,16},{16,20},{20,24},{24,28},{1,5},{5,9},{9,... | collective-permute-start | bytes 417800 | tf_op jit(solution)/shard_map/ppermute | solution.py:295
  17.7 1.0 %copy-start.1 = (bf16[768,256]{1,0:T(8,128)(2,1)S(1)}, bf16[768,256]{1,0:T(8,128)(2,1)}, u32[]{:S(2)}) copy-start(bf16[768,256]{1,0:T(8,128)(2,1)} %proj_ref.1) | copy-start | bytes 1179652
  18.7 0.7 copy-start.4
  20.0 2.8 %copy-start = (bf16[768,4096]{1,0:T(8,128)(2,1)S(1)}, bf16[768,4096]{1,0:T(8,128)(2,1)}, u32[]{:S(2)}) copy-start(bf16[768,4096]{1,0:T(8,128)(2,1)} %refs_1_.3) | copy-start | bytes 18874372
  22.8 0.8 copy-start.2
  30.1 19.7 %collective-permute-start.4 = (bf16[128,512]{1,0:T(8,128)(2,1)S(1)}, bf16[128,512]{1,0:T(8,128)(2,1)S(1)}, u32[]{:S(2)}, u32[]{:S(2)}) collective-permute-start(bf16[128,512]{1,0:T(8,128)(2,1)S(1)} %get-tuple-element.29), channel_id=1, source_target_pairs={{0,4},{4,0},{8,12},{12,8},{16,20},{20,16},{24,28},{28,24},{1,5},{5... | collective-permute-start | bytes 393224 | tf_op jit(solution)/shard_map/ppermute | solution.py:300
  32.6 18.2 %collective-permute-start.5 = (bf16[128,512]{1,0:T(8,128)(2,1)S(1)}, bf16[128,512]{1,0:T(8,128)(2,1)S(1)}, u32[]{:S(2)}, u32[]{:S(2)}) collective-permute-start(bf16[128,512]{1,0:T(8,128)(2,1)S(1)} %get-tuple-element.30), channel_id=1, source_target_pairs={{0,8},{4,12},{8,0},{12,4},{16,24},{20,28},{24,16},{28,20},{1,9},{5... | collective-permute-start | bytes 393224 | tf_op jit(solution)/shard_map/ppermute | solution.py:300
  34.2 16.6 %collective-permute-start.6 = (bf16[128,512]{1,0:T(8,128)(2,1)S(1)}, bf16[128,512]{1,0:T(8,128)(2,1)S(1)}, u32[]{:S(2)}, u32[]{:S(2)}) collective-permute-start(bf16[128,512]{1,0:T(8,128)(2,1)S(1)} %get-tuple-element.31), channel_id=1, source_target_pairs={{0,12},{4,8},{8,4},{12,0},{16,28},{20,24},{24,20},{28,16},{1,13},{... | collective-permute-start | bytes 393224 | tf_op jit(solution)/shard_map/ppermute | solution.py:300
  41.5 14.3 %collective-permute-start.7 = (bf16[128,512]{1,0:T(8,128)(2,1)S(1)}, bf16[128,512]{1,0:T(8,128)(2,1)S(1)}, u32[]{:S(2)}, u32[]{:S(2)}) collective-permute-start(bf16[128,512]{1,0:T(8,128)(2,1)S(1)} %get-tuple-element.39), channel_id=1, source_target_pairs={{0,4},{4,0},{8,12},{12,8},{16,20},{20,16},{24,28},{28,24},{1,5},{5... | collective-permute-start | bytes 393224 | tf_op jit(solution)/shard_map/ppermute | solution.py:300
  42.6 13.2 %collective-permute-start.8 = (bf16[128,512]{1,0:T(8,128)(2,1)S(1)}, bf16[128,512]{1,0:T(8,128)(2,1)S(1)}, u32[]{:S(2)}, u32[]{:S(2)}) collective-permute-start(bf16[128,512]{1,0:T(8,128)(2,1)S(1)} %get-tuple-element.40), channel_id=1, source_target_pairs={{0,8},{4,12},{8,0},{12,4},{16,24},{20,28},{24,16},{28,20},{1,9},{5... | collective-permute-start | bytes 393224 | tf_op jit(solution)/shard_map/ppermute | solution.py:300
  49.8 6.0 %collective-permute-start.9 = (bf16[128,512]{1,0:T(8,128)(2,1)S(1)}, bf16[128,512]{1,0:T(8,128)(2,1)S(1)}, u32[]{:S(2)}, u32[]{:S(2)}) collective-permute-start(bf16[128,512]{1,0:T(8,128)(2,1)S(1)} %get-tuple-element.41), channel_id=1, source_target_pairs={{0,12},{4,8},{8,4},{12,0},{16,28},{20,24},{24,20},{28,16},{1,13},{... | collective-permute-start | bytes 393224 | tf_op jit(solution)/shard_map/ppermute | solution.py:300
  50.9 15.5 %collective-permute-start.14 = (bf16[128,512]{1,0:T(8,128)(2,1)S(1)}, bf16[128,512]{1,0:T(8,128)(2,1)S(1)}, u32[]{:S(2)}, u32[]{:S(2)}) collective-permute-start(bf16[128,512]{1,0:T(8,128)(2,1)S(1)} %fusion.19), channel_id=1, source_target_pairs={{0,16},{4,20},{8,24},{12,28},{1,17},{5,21},{9,25},{13,29},{2,18},{... | collective-permute-start | bytes 393224 | tf_op jit(solution)/shard_map/ppermute | solution.py:295
  56.0 14.9 %collective-permute-start.10 = (bf16[128,512]{1,0:T(8,128)(2,1)S(1)}, bf16[128,512]{1,0:T(8,128)(2,1)S(1)}, u32[]{:S(2)}, u32[]{:S(2)}) collective-permute-start(bf16[128,512]{1,0:T(8,128)(2,1)S(1)} %fusion.38), channel_id=1, source_target_pairs={{0,16},{4,20},{8,24},{12,28},{1,17},{5,21},{9,25},{13,29},{2,18},{... | collective-permute-start | bytes 393224 | tf_op jit(solution)/shard_map/ppermute | solution.py:295
  60.7 14.6 %copy-start.3 = (f32[4096]{0:T(1024)S(1)}, f32[4096]{0:T(1024)}, u32[]{:S(2)}) copy-start(f32[4096]{0:T(1024)} %param.15) | copy-start | bytes 49156
  66.6 7.8 %collective-permute-start.15 = (bf16[128,512]{1,0:T(8,128)(2,1)S(1)}, bf16[128,512]{1,0:T(8,128)(2,1)S(1)}, u32[]{:S(2)}, u32[]{:S(2)}) collective-permute-start(bf16[128,512]{1,0:T(8,128)(2,1)S(1)} %get-tuple-element.44), channel_id=1, source_target_pairs={{0,4},{4,0},{8,12},{12,8},{16,20},{20,16},{24,28},{28,24},{1,5},{5... | collective-permute-start | bytes 393224 | tf_op jit(solution)/shard_map/ppermute | solution.py:300
  67.9 7.0 %collective-permute-start.17 = (bf16[128,512]{1,0:T(8,128)(2,1)S(1)}, bf16[128,512]{1,0:T(8,128)(2,1)S(1)}, u32[]{:S(2)}, u32[]{:S(2)}) collective-permute-start(bf16[128,512]{1,0:T(8,128)(2,1)S(1)} %get-tuple-element.43), channel_id=1, source_target_pairs={{0,12},{4,8},{8,4},{12,0},{16,28},{20,24},{24,20},{28,16},{1,13},{... | collective-permute-start | bytes 393224 | tf_op jit(solution)/shard_map/ppermute | solution.py:300
  70.3 5.0 %collective-permute-start.16 = (bf16[128,512]{1,0:T(8,128)(2,1)S(1)}, bf16[128,512]{1,0:T(8,128)(2,1)S(1)}, u32[]{:S(2)}, u32[]{:S(2)}) collective-permute-start(bf16[128,512]{1,0:T(8,128)(2,1)S(1)} %get-tuple-element.45), channel_id=1, source_target_pairs={{0,8},{4,12},{8,0},{12,4},{16,24},{20,28},{24,16},{28,20},{1,9},{5... | collective-permute-start | bytes 393224 | tf_op jit(solution)/shard_map/ppermute | solution.py:300
  71.0 9.3 %collective-permute-start.11 = (bf16[128,512]{1,0:T(8,128)(2,1)S(1)}, bf16[128,512]{1,0:T(8,128)(2,1)S(1)}, u32[]{:S(2)}, u32[]{:S(2)}) collective-permute-start(bf16[128,512]{1,0:T(8,128)(2,1)S(1)} %get-tuple-element.48), channel_id=1, source_target_pairs={{0,4},{4,0},{8,12},{12,8},{16,20},{20,16},{24,28},{28,24},{1,5},{5... | collective-permute-start | bytes 393224 | tf_op jit(solution)/shard_map/ppermute | solution.py:300
  72.6 7.8 %collective-permute-start.13 = (bf16[128,512]{1,0:T(8,128)(2,1)S(1)}, bf16[128,512]{1,0:T(8,128)(2,1)S(1)}, u32[]{:S(2)}, u32[]{:S(2)}) collective-permute-start(bf16[128,512]{1,0:T(8,128)(2,1)S(1)} %get-tuple-element.47), channel_id=1, source_target_pairs={{0,12},{4,8},{8,4},{12,0},{16,28},{20,24},{24,20},{28,16},{1,13},{... | collective-permute-start | bytes 393224 | tf_op jit(solution)/shard_map/ppermute | solution.py:300
  74.3 6.0 %collective-permute-start.12 = (bf16[128,512]{1,0:T(8,128)(2,1)S(1)}, bf16[128,512]{1,0:T(8,128)(2,1)S(1)}, u32[]{:S(2)}, u32[]{:S(2)}) collective-permute-start(bf16[128,512]{1,0:T(8,128)(2,1)S(1)} %get-tuple-element.49), channel_id=1, source_target_pairs={{0,8},{4,12},{8,0},{12,4},{16,24},{20,28},{24,16},{28,20},{1,9},{5... | collective-permute-start | bytes 393224 | tf_op jit(solution)/shard_map/ppermute | solution.py:300

commit v3 on v0

v3 whole, which is shorter than its diff:
```python
import jax
import jax.numpy as jnp
from jax import lax
from jax.experimental import pallas as pl
from jax.experimental.pallas import tpu as pltpu
from jax.sharding import PartitionSpec as P

CHUNK = 128
SQUARE = 4
GROUPS = 2
SUB = 256
EDGE = 16
LANES = 128
F32 = jnp.float32
BF16 = jnp.bfloat16


def params(mib=16):
    return pltpu.CompilerParams(vmem_limit_bytes=mib * 1024 * 1024)


def dot(a, b):
    return jnp.dot(a, b, preferred_element_type=F32)


def dot_rows(a, b):
    return lax.dot_general(a, b, (((1,), (1,)), ((), ())), preferred_element_type=F32)


def pieces(value, count):
    out = []
    for _ in range(count):
        out.append(value.astype(BF16))
        value = value - out[-1].astype(F32)
    return out


def iota(shape, axis):
    return lax.broadcasted_iota(jnp.int32, shape, axis)


def hint(moved):
    return pl.CostEstimate(flops=0, bytes_accessed=moved, transcendentals=0)


def vmem():
    return pl.BlockSpec(memory_space=pltpu.VMEM)


def smem():
    return pl.BlockSpec(memory_space=pltpu.SMEM)


def anywhere():
    return pl.BlockSpec(memory_space=pl.ANY)


def over_heads(values, head_width, first, cols):
    blocks = []
    for lane in range(0, cols, LANES):
        head = (first + lane + iota(values.shape, 1)) // head_width
        blocks.append(jnp.take_along_axis(values, head, axis=1, mode="promise_in_bounds"))
    return jnp.concatenate(blocks, axis=1)


def silu_conv(rows_back, taps):
    count = len(taps)
    half = sum(rows_back(k) * (0.5 * taps[count - 1 - k]) for k in range(count))
    return half + half * jnp.tanh(half)


def edges_kernel(inner_ref, proj_ref, out_ref, sems):
    width = inner_ref.shape[1]
    last = pl.ds(inner_ref.shape[0] - EDGE, EDGE)
    copies = [
        pltpu.make_async_copy(inner_ref.at[last, :], out_ref.at[:, :width], sems.at[0]),
        pltpu.make_async_copy(proj_ref.at[last, :], out_ref.at[:, width:], sems.at[1]),
    ]
    for copy in copies:
        copy.start()
    for copy in copies:
        copy.wait()


def last_rows(inner, proj):
    width = inner.shape[1] + proj.shape[1]
    return pl.pallas_call(
        edges_kernel,
        in_specs=[anywhere()] * 2,
        out_specs=vmem(),
        out_shape=jax.ShapeDtypeStruct((EDGE, width), BF16),
        scratch_shapes=[pltpu.SemaphoreType.DMA((2,))],
        compiler_params=params(),
        name="edges",
    )(inner, proj)


def decay_kernel(decay_ref, step_ref, skip_ref, fwd_ref, inv_ref, dev_ref, end_ref, fac_ref):
    heads, rows = decay_ref.shape
    chunks = rows // CHUNK
    lower = jnp.where(iota((CHUNK, CHUNK), 0) >= iota((CHUNK, CHUNK), 1), 1.0, 0.0).astype(BF16)
    same = jnp.where(iota((CHUNK, CHUNK), 0) == iota((CHUNK, CHUNK), 1), 1.0, 0.0).astype(BF16)
    copies = LANES // heads
    cums, steps = [], []
    for c in range(chunks):
        at = pl.ds(c * CHUNK, CHUNK)
        decay = jnp.concatenate([decay_ref[:, at]] * copies, axis=0)
        step = jnp.concatenate([step_ref[:, at]] * copies, axis=0)
        cums.append(sum(dot_rows(lower, piece) for piece in pieces(decay, 3)))
        steps.append(sum(dot_rows(same, piece) for piece in pieces(step, 3)))
    totals = [cum[CHUNK - 1 :] for cum in cums]
    middles = [cum[CHUNK // 2 - 1 : CHUNK // 2] for cum in cums]
    before = [jnp.zeros_like(totals[0])]
    for c in range(chunks):
        before.append(before[c] + totals[c])
    after = [jnp.zeros_like(totals[0])]
    for c in range(chunks - 1, 0, -1):
        after.insert(0, after[0] + totals[c])
    fac_ref[...] = jnp.zeros_like(fac_ref)
    for c in range(chunks):
        at = pl.ds(c * CHUNK, CHUNK)
        fwd_ref[at, :] = jnp.exp(cums[c] - middles[c])
        inv_ref[at, :] = jnp.exp(middles[c] - cums[c]) * steps[c]
        dev_ref[at, :] = jnp.exp(before[c] + cums[c])
        end_ref[at, :] = jnp.exp((totals[c] - cums[c]) + after[c]) * steps[c]
        following = middles[c + 1] if c + 1 < chunks else 0.0
        fac_ref[c : c + 1, :] = jnp.exp(totals[c] - middles[c] + following)
    fac_ref[chunks : chunks + 1, :] = skip_ref[:1]
    fac_ref[8:9, :] = jnp.exp(before[chunks])


def decays(decay_log, step_size, skip_weight):
    rows, heads = decay_log.shape
    wide = jax.ShapeDtypeStruct((rows, LANES), F32)
    return pl.pallas_call(
        decay_kernel,
        out_shape=(wide, wide, wide, wide, jax.ShapeDtypeStruct((16, LANES), F32)),
        compiler_params=params(),
        name="decays",
    )(decay_log.T, step_size.T, jnp.broadcast_to(jnp.tile(skip_weight, LANES // heads)[None], (8, LANES)))


def project(proj_ref, edge_ref, taps_ref, mix_ref, bt_ref, wide_ref):
    rows, width = proj_ref.shape
    state = width // 2
    taps = [taps_ref[k : k + 1, :] for k in range(taps_ref.shape[0])]
    causal = iota((CHUNK, CHUNK), 0) >= iota((CHUNK, CHUNK), 1)
    past = edge_ref.shape[0]
    wide_ref[EDGE - past : EDGE, :] = edge_ref[:, edge_ref.shape[1] - width :].astype(F32)
    wide_ref[EDGE:, :] = proj_ref[...].astype(F32)
    for c in range(rows // CHUNK):
        at = pl.ds(c * CHUNK, CHUNK)
        both = silu_conv(lambda k: wide_ref[pl.ds(EDGE + c * CHUNK - k, CHUNK), :], taps).astype(BF16)
        b_rows, c_rows = both[:, :state], both[:, state:]
        mix_ref[at, :CHUNK] = jnp.where(causal, dot_rows(c_rows, b_rows), 0.0).astype(BF16)
        mix_ref[at, CHUNK:] = c_rows
        bt_ref[:, at] = b_rows.astype(F32).T.astype(BF16)


def summarize(place_ref, in_ref, ready, edge_ref, taps_ref, end_ref, fac_ref, bt_ref, x_ref, slots, window_ref, sum_ref, head_width, first):
    rows, wide = x_ref.shape
    cols = wide // SQUARE
    state = bt_ref.shape[0]
    count = taps_ref.shape[0]
    chunks = rows // CHUNK
    blocks = wide // LANES
    for block in range(blocks):
        at_lanes = pl.ds(first + block * LANES, LANES)
        window_ref[block, EDGE + CHUNK - count + 1 :, :] = edge_ref[:, at_lanes].astype(F32)
    sum_ref[...] = jnp.zeros_like(sum_ref)

    def chunk_step(c, _):
        ready(c)
        at = pl.ds(pl.multiple_of(c * CHUNK, CHUNK), CHUNK)
        for sub in range(wide // SUB):
            at_cols = pl.ds(sub * SUB, SUB)
            here = first + sub * SUB
            rows_here = in_ref[at, at_cols].astype(F32)
            xs = []
            for lane in range(0, SUB, LANES):
                block = (sub * SUB + lane) // LANES
                window_ref[block, EDGE - 8 : EDGE, :] = window_ref[block, EDGE + CHUNK - 8 :, :]
                window_ref[block, EDGE:, :] = rows_here[:, lane : lane + LANES]
                taps = [taps_ref[k : k + 1, pl.ds(here + lane, LANES)] for k in range(count)]
                xs.append(silu_conv(lambda k: window_ref[block, pl.ds(EDGE - k, CHUNK), :], taps))
            x = jnp.concatenate(xs, axis=1)
            x_ref[at, at_cols] = x.astype(BF16)
            scaled = (over_heads(end_ref[at, :], head_width, here, SUB) * x).astype(BF16)
            sum_ref[:, at_cols] += dot(bt_ref[:, at], scaled)
        return 0

    lax.fori_loop(0, chunks, chunk_step, 0)
    row = iota((EDGE, cols), 0)
    decay_rows = fac_ref[8:16, :]
    for k, slot in enumerate(slots):
        start = pl.multiple_of((k ^ place_ref[0]) * cols, cols)
        slot[:state, :] = sum_ref[:, pl.ds(start, cols)].astype(BF16)
        decay = over_heads(decay_rows, head_width, first + start, cols)[:1]
        high = decay.astype(BF16).astype(F32)
        slot[state:, :] = jnp.where(row == 0, high, jnp.where(row == 1, decay - high, 0.0)).astype(BF16)


def first_kernel(place_ref, in_ref, proj_ref, edge_ref, taps_ref, proj_taps_ref, end_ref, fac_ref, x_ref, later_ref, mix_ref, bt_ref, *rest, head_width):
    slots, (block_ref, wide_ref, window_ref, sum_ref, sems, later_sem) = rest[:SQUARE], rest[SQUARE:]
    rows, wide = x_ref.shape

    def fetch(c):
        at = pl.ds(pl.multiple_of(c * CHUNK, CHUNK), CHUNK)
        return pltpu.make_async_copy(in_ref.at[at, pl.ds(0, wide)], block_ref.at[at, :], sems.at[c])

    for c in range(rows // CHUNK):
        fetch(c).start()
    later = pltpu.make_async_copy(in_ref.at[:, pl.ds(wide, later_ref.shape[1])], later_ref, later_sem)
    later.start()
    project(proj_ref, edge_ref, proj_taps_ref, mix_ref, bt_ref, wide_ref)
    summarize(place_ref, block_ref, lambda c: fetch(c).wait(), edge_ref, taps_ref, end_ref, fac_ref, bt_ref, x_ref, slots, window_ref, sum_ref, head_width, 0)
    later.wait()


def slot_shapes(state, wide):
    return [jax.ShapeDtypeStruct((state + EDGE, wide // SQUARE), BF16)] * SQUARE


def sum_scratch(state, wide):
    return [pltpu.VMEM((wide // LANES, EDGE + CHUNK, LANES), F32), pltpu.VMEM((state, wide), F32)]


def first_states(place, inner, proj, edge, taps, proj_taps, end, fac, head_width):
    rows, width = inner.shape
    state = proj.shape[1] // 2
    wide = width // GROUPS
    chunks = rows // CHUNK
    out = pl.pallas_call(
        lambda *refs: first_kernel(*refs, head_width=head_width),
        in_specs=[smem(), pl.BlockSpec(memory_space=pltpu.HBM)] + [vmem()] * 6,
        out_specs=[vmem()] * (SQUARE + 4),
        out_shape=[
            jax.ShapeDtypeStruct((rows, wide), BF16),
            jax.ShapeDtypeStruct((rows, width - wide), BF16),
            jax.ShapeDtypeStruct((rows, CHUNK + state), BF16),
            jax.ShapeDtypeStruct((state, rows), BF16),
        ]
        + slot_shapes(state, wide),
        scratch_shapes=[pltpu.VMEM((rows, wide), BF16), pltpu.VMEM((EDGE + rows, 2 * state), F32)]
        + sum_scratch(state, wide)
        + [pltpu.SemaphoreType.DMA((chunks,)), pltpu.SemaphoreType.DMA],
        compiler_params=params(),
        cost_estimate=hint(4 * rows * wide),
        name="first_states",
    )(place, inner, proj, edge, taps, proj_taps, end, fac)
    return out[:4], out[4:]


def later_kernel(place_ref, in_ref, edge_ref, taps_ref, end_ref, fac_ref, bt_ref, x_ref, *rest, head_width, first):
    slots, (window_ref, sum_ref) = rest[:SQUARE], rest[SQUARE:]
    summarize(place_ref, in_ref, lambda c: None, edge_ref, taps_ref, end_ref, fac_ref, bt_ref, x_ref, slots, window_ref, sum_ref, head_width, first)


def later_states(place, inner, edge, taps, end, fac, bt, head_width):
    rows, wide = inner.shape
    state = bt.shape[0]
    first = taps.shape[1] - wide
    out = pl.pallas_call(
        lambda *refs: later_kernel(*refs, head_width=head_width, first=first),
        in_specs=[smem()] + [vmem()] * 6,
        out_specs=[vmem()] * (SQUARE + 1),
        out_shape=[jax.ShapeDtypeStruct((rows, wide), BF16)] + slot_shapes(state, wide),
        scratch_shapes=sum_scratch(state, wide),
        compiler_params=params(),
        cost_estimate=hint(4 * rows * wide),
        name="later_states",
    )(place, inner, edge, taps, end, fac, bt)
    return out[0], out[1:]


def combine_kernel(place_ref, *refs):
    slots, (leaving_ref, prefix_ref, opening_ref, placed_ref) = refs[:SQUARE], refs[SQUARE:]
    state, cols = leaving_ref.shape
    spot = place_ref[0]
    for k in range(SQUARE):
        placed_ref[spot ^ k] = slots[k][...]
    running = jnp.zeros((state, cols), F32)
    opening = jnp.ones((1, cols), F32)
    for p in range(SQUARE):
        prefix_ref[spot ^ p] = running
        opening_ref[spot ^ p] = jnp.broadcast_to(opening, (8, cols))
        tail = placed_ref[p, state:, :].astype(F32)
        decay = tail[0:1] + tail[1:2]
        running = decay * running + placed_ref[p, :state, :].astype(F32)
        opening = decay * opening
    leaving_ref[...] = running.astype(BF16)
    opening_ref[SQUARE] = jnp.broadcast_to(opening, (8, cols))


def combine(place, slots):
    rows, cols = slots[0].shape
    state = rows - EDGE
    return pl.pallas_call(
        combine_kernel,
        in_specs=[smem()] + [vmem()] * SQUARE,
        out_specs=[vmem()] * 3,
        out_shape=(
            jax.ShapeDtypeStruct((state, cols), BF16),
            jax.ShapeDtypeStruct((SQUARE, state, cols), F32),
            jax.ShapeDtypeStruct((SQUARE + 1, 8, cols), F32),
        ),
        scratch_shapes=[pltpu.VMEM((SQUARE, rows, cols), BF16)],
        compiler_params=params(),
        name="combine",
    )(place, *slots)


def local_kernel(x_ref, fwd_ref, inv_ref, fac_ref, mix_ref, bt_ref, out_ref, *, head_width, first):
    rows, wide = x_ref.shape
    chunks = rows // CHUNK
    cols = wide // SQUARE

    def tile_step(j, _):
        base = pl.multiple_of(j * cols, cols)
        for sub in range(cols // SUB):
            at_cols = pl.ds(base + sub * SUB, SUB)
            here = first + base + sub * SUB
            factors = over_heads(fac_ref[...], head_width, here, SUB)
            skip = factors[chunks : chunks + 1]
            state = jnp.zeros((bt_ref.shape[0], SUB), F32)
            for c in range(chunks):
                at = pl.ds(c * CHUNK, CHUNK)
                x = x_ref[at, at_cols].astype(F32)
                scaled = (over_heads(inv_ref[at, :], head_width, here, SUB) * x).astype(BF16)
                both = jnp.concatenate([scaled, state.astype(BF16)], axis=0)
                mixed = dot(mix_ref[at, :], both)
                out_ref[at, at_cols] = over_heads(fwd_ref[at, :], head_width, here, SUB) * mixed + skip * x
                if c + 1 < chunks:
                    state = factors[c : c + 1] * (state + dot(bt_ref[:, at], scaled))
        return 0

    lax.fori_loop(0, SQUARE, tile_step, 0)


def local_parts(x, fwd, inv, fac, mix, bt, head_width, group):
    rows, wide = x.shape
    state = bt.shape[0]
    return pl.pallas_call(
        lambda *refs: local_kernel(*refs, head_width=head_width, first=group * wide),
        in_specs=[vmem()] * 6,
        out_specs=vmem(),
        out_shape=jax.ShapeDtypeStruct((rows, wide), F32),
        compiler_params=params(),
        cost_estimate=pl.CostEstimate(flops=2 * rows * wide * 5 * state, bytes_accessed=6 * rows * wide, transcendentals=0),
        name="local",
    )(x, fwd, inv, fac, mix, bt)


def final_kernel(place_ref, local_ref, dev_ref, mix_ref, gain_ref, *rest, head_width, first):
    slots, (out_ref, stage_ref, sems) = rest[:SQUARE], rest[-3:]
    rows, wide = local_ref.shape
    cols = wide // SQUARE
    mean = jnp.where(iota((SUB, SUB), 0) // head_width == iota((SUB, SUB), 1) // head_width, 1.0 / head_width, 0.0).astype(BF16)
    copies = []
    for k in range(SQUARE):
        base = pl.multiple_of((k ^ place_ref[0]) * cols, cols)
        for sub in range(cols // SUB):
            at_cols = pl.ds(base + sub * SUB, SUB)
            carried = dot(mix_ref[:, CHUNK:], slots[k][:, sub * SUB : (sub + 1) * SUB])
            combined = local_ref[:, at_cols] + over_heads(dev_ref[...], head_width, first + base + sub * SUB, SUB) * carried
            squares = dot((combined * combined).astype(BF16), mean)
            gain = gain_ref[:, pl.ds(first + base + sub * SUB, SUB)]
            turn = k * (cols // SUB) + sub
            stage_ref[turn] = (combined * lax.rsqrt(squares + 1e-05) * gain).astype(BF16)
            copies.append(pltpu.make_async_copy(stage_ref.at[turn], out_ref.at[:, pl.ds(first + base + sub * SUB, SUB)], sems.at[turn]))
            copies[-1].start()
    for copy in copies:
        copy.wait()


def finish(place, local, dev, mix, gain, slots, head_width, group, into):
    rows, wide = local.shape
    operands = [place, local, dev, mix, gain, *slots]
    in_specs = [smem()] + [vmem()] * (len(operands) - 1)
    aliases = {}
    if into is not None:
        in_specs.append(anywhere())
        operands.append(into)
        aliases = {len(operands) - 1: 0}
    return pl.pallas_call(
        lambda *refs: final_kernel(*refs, head_width=head_width, first=group * wide),
        in_specs=in_specs,
        out_specs=anywhere(),
        out_shape=jax.ShapeDtypeStruct((rows, wide * GROUPS), BF16),
        scratch_shapes=[pltpu.VMEM((wide // SUB, rows, SUB), BF16), pltpu.SemaphoreType.DMA((wide // SUB,))],
        input_output_aliases=aliases,
        compiler_params=params(),
        cost_estimate=pl.CostEstimate(flops=2 * rows * wide * 512, bytes_accessed=6 * rows * wide, transcendentals=rows * wide),
        name="finish",
    )(*operands)


def shifted(x, by):
    length = lax.axis_size("ctx")
    return lax.ppermute(x, "ctx", [(i, i + by) for i in range(length - by)])


def swapped(x, k):
    length = lax.axis_size("ctx")
    return lax.ppermute(x, "ctx", [(i, i ^ k) for i in range(length)])


def previous_squares(leaving, decay):
    squares = lax.axis_size("ctx") // SQUARE
    entering = shifted(leaving, SQUARE)
    span = 1
    if squares > 2:
        window = shifted(decay, SQUARE)
    while span < squares - 1:
        behind = shifted(entering, SQUARE * span)
        entering = (entering.astype(F32) + window * behind.astype(F32)).astype(BF16)
        window = window * shifted(window, SQUARE * span)
        span *= 2
    return entering


def body(inner_input, state_proj, step_size, decay_log, conv_inner, conv_proj, skip_weight, norm_gain):
    rows, width = inner_input.shape
    heads = step_size.shape[1]
    head_width = width // heads
    past = conv_inner.shape[0] - 1
    kept = pltpu.with_memory_space_constraint(inner_input, pltpu.HBM)
    place = jnp.full((1,), lax.axis_index("ctx") % SQUARE, jnp.int32)
    edge = shifted(last_rows(kept, state_proj)[EDGE - past :], 1)
    fwd, inv, dev, end, fac = decays(decay_log, step_size, skip_weight)
    gain = norm_gain[None]
    (x, later, mix, bt), slots = first_states(place, kept, state_proj, edge, conv_inner, conv_proj, end, fac, head_width)
    xs, sent = [x], [[slots[0]] + [swapped(slots[k], k) for k in range(1, SQUARE)]]
    x, slots = later_states(place, later, edge, conv_inner, end, fac, bt, head_width)
    xs.append(x)
    sent.append([slots[0]] + [swapped(slots[k], k) for k in range(1, SQUARE)])
    returned, locals_ = [], []
    for group in range(GROUPS):
        x = xs[group]
        if group:
            x, leaving = lax.optimization_barrier((x, leaving))
        locals_.append(local_parts(x, fwd, inv, fac, mix, bt, head_width, group))
        leaving, prefix, opening = combine(place, sent[group])
        arrived = previous_squares(leaving, opening[SQUARE, :1]).astype(F32)
        entering = [(prefix[k] + opening[k, :1] * arrived).astype(BF16) for k in range(SQUARE)]
        returned.append([entering[0]] + [swapped(entering[k], k) for k in range(1, SQUARE)])
    out = None
    for group in range(GROUPS):
        out = finish(place, locals_[group], dev, mix, gain, returned[group], head_width, group, out)
    return out


def solution(mesh):
    split = P(("dp", "ctx"), None)
    return jax.shard_map(
        body, mesh=mesh, in_specs=(split, split, split, split, P(), P(), P(), P()), out_specs=split, check_vma=False
    )
```

time: 258 us -> 65.9 us (0.26)
  local copies, waits for them, and re-layouts: 77.6 us -> 1.15 us
  waiting for transfers between devices: 69.8 us -> 0.91 us
  other arithmetic: 48.2 us -> 0.31 us
  matrix products: 40.6 us -> 0 us
  Pallas kernels: 0 us -> 32.4 us
  starting transfers between devices: 19.4 us -> 30.5 us
    all_to_all x3 -> x0, waiting for transfers between devices: 69.8 us -> none  [the longest x1 47.2 us: body(): lax.all_to_all(summary[None], 'ctx', split_axis=1, concat_axis=0, tiled=T...]
    dot_general x11 -> x0, matrix products: 40.6 us -> none  [the longest x3 19.5 us: block_terms(): jnp.einsum('hts,hps->hpt', weights, inner_cols, preferred_element_type=jn...]
    pallas_call x0 -> x10, Pallas kernels: none -> 32.4 us  [the longest x2 11 us: local_parts(): pl.pallas_call(lambda *refs: local_kernel(*refs, head_width=head_width, f...]
    convert_element_type x4 -> x2, other arithmetic: 26.1 us -> 0.31 us  [body(): (prefix[k] + opening[k, :1] * arrived).astype(BF16)]
    ppermute x1 -> x15, starting transfers between devices: 4.84 us -> 30.5 us  [the longest x12 16.1 us: swapped(): return lax.ppermute(x, 'ctx', [(i, i ^ k) for i in range(length)])]
    dynamic_slice x12 -> x0, local copies, waits for them, and re-layouts: 19.7 us -> none  [body(): lax.map(lambda item: block_terms(item[0], item[1], item[2], item[3]), (in...]
    dynamic_update_slice x15 -> x0, local copies, waits for them, and re-layouts: 18.9 us -> none  [body(): lax.map(lambda item: block_terms(item[0], item[1], item[2], item[3]), (in...]
    add x6 -> x0, other arithmetic: 17.1 us -> none  [advance(): jnp.exp(block_total)[:, None] * carry_state + block_state]
  transfers between devices with their start and end apart: 4 -> 15, of which waited for: 2 -> 3; matrix products, arithmetic and copies ran while one was open for 9% -> 1% of each run, Pallas kernels for 0% -> 33%
where the time goes in v3:
time: 65.9 us; the launch traced here: 65.7 us
  Pallas kernels  32.4 us (49%)
  starting transfers between devices  30.5 us (46%)
  local copies, waits for them, and re-layouts  1.15 us (2%)
  waiting for transfers between devices  0.91 us (1%)
    ppermute x12, starting transfers between devices, swapped(): return lax.ppermute(x, 'ctx', [(i, i ^ k) for i in range(length)])  16.1 us
    ppermute x3, starting transfers between devices, shifted(): return lax.ppermute(x, 'ctx', [(i, i + by) for i in range(length - by)])  14.4 us
    pallas_call x2, Pallas kernels, local_parts(): pl.pallas_call(lambda *refs: local_kernel(*refs, head_width=head_width, f...  11 us
    pallas_call x2, Pallas kernels, finish(): pl.pallas_call(lambda *refs: final_kernel(*refs, head_width=head_width, f...  7.08 us
    pallas_call x1, Pallas kernels, first_states(): pl.pallas_call(lambda *refs: first_kernel(*refs, head_width=head_width),...  6.37 us
    pallas_call x1, Pallas kernels, later_states(): pl.pallas_call(lambda *refs: later_kernel(*refs, head_width=head_width, f...  5.45 us
  transfers between devices with their start and end apart: 15, of which 3 were waited for; matrix products, arithmetic and copies ran while one was open for 1% of the time, Pallas kernels for 33%

profile of v3, /device:TPU:0, one launch (start us, length us, event | category | flops | bytes accessed | tf_op | source)
XLA Modules:
  0.0 65.7 jit_solution(17002874935484492750)
XLA Ops:
  0.0 1.0 %copy-done = bf16[768,256]{1,0:T(8,128)(2,1)S(1)} copy-done((bf16[768,256]{1,0:T(8,128)(2,1)S(1)}, bf16[768,256]{1,0:T(8,128)(2,1)}, u32[]{:S(2)}) %copy-start) | copy-done | bytes 393240
  1.0 1.0 %edges.1 = bf16[16,4352]{1,0:T(8,128)(2,1)S(1)} custom-call(bf16[768,4096]{1,0:T(8,128)(2,1)} %refs_1_.1, bf16[768,256]{1,0:T(8,128)(2,1)S(1)} %copy-done), custom_call_target="tpu_custom_call" | custom-call | tf_op jit(solution)/shard_map/edges/pallas_call | solution.py:87
  2.1 4.8 %collective-permute-start = (bf16[3,4352]{1,0:T(4,128)(2,1)S(1)}, bf16[3,4352]{1,0:T(4,128)(2,1)S(1)}, u32[]{:S(2)}, u32[]{:S(2)}) collective-permute-start(bf16[3,4352]{1,0:T(4,128)(2,1)S(1)} %slice.68), channel_id=1, source_target_pairs={{0,4},{4,8},{8,12},{12,16},{16,20},{20,24},{24,28},{1,5},{5,9},{9,... | collective-permute-start | bytes 78344 | tf_op jit(solution)/shard_map/ppermute | solution.py:400
  6.9 0.0 copy-done.7
  7.0 0.1 broadcast_in_dim.14
  7.0 0.0 copy-done.3
  7.0 1.0 %decays.1 = (f32[768,128]{1,0:T(8,128)S(1)}, f32[768,128]{1,0:T(8,128)S(1)}, f32[768,128]{1,0:T(8,128)S(1)}, f32[768,128]{1,0:T(8,128)S(1)}, f32[16,128]{1,0:T(8,128)S(1)}) custom-call(f32[64,768]{1,0:T(8,128)S(1)} %bitcast.28, f32[64,768]{1,0:T(8,128)S(1)} %bitcast.29, f32[8,128]{1,0:T(8,128)S(1)} %broadcast_in_dim.15.skip_ref), custom_call_target="tpu_custom_call" | custom-call | tf_op jit(solution)/shard_map/decays/pallas_call | solution.py:135
  8.1 0.4 collective-permute-done.refs_3_.refs_2_
  8.5 0.0 copy-done.1
  8.5 6.4 %first_states.1 = (bf16[768,2048]{1,0:T(8,128)(2,1)S(1)}, bf16[768,2048]{1,0:T(8,128)(2,1)S(1)}, bf16[768,256]{1,0:T(8,128)(2,1)S(1)}, bf16[128,768]{1,0:T(8,128...) custom-call(s32[1]{0:T(128)} %bitcast.refs_0_.place_ref, ...), custom_call_target="tpu_custom_call" | custom-call | bytes 6291456 | tf_op jit(solution)/shard_map/first_states/pallas_call | solution.py:233
  14.9 2.4 %collective-permute-start.1 = (bf16[144,512]{1,0:T(8,128)(2,1)S(1)}, bf16[144,512]{1,0:T(8,128)(2,1)S(1)}, u32[]{:S(2)}, u32[]{:S(2)}) collective-permute-start(bf16[144,512]{1,0:T(8,128)(2,1)S(1)} %get-tuple-element.36), channel_id=1, source_target_pairs={{0,4},{4,0},{8,12},{12,8},{16,20},{20,16},{24,28},{28,24},{1,5},{5... | collective-permute-start | bytes 442376 | tf_op jit(solution)/shard_map/ppermute | solution.py:405
  17.3 1.6 %collective-permute-start.2 = (bf16[144,512]{1,0:T(8,128)(2,1)S(1)}, bf16[144,512]{1,0:T(8,128)(2,1)S(1)}, u32[]{:S(2)}, u32[]{:S(2)}) collective-permute-start(bf16[144,512]{1,0:T(8,128)(2,1)S(1)} %get-tuple-element.37), channel_id=1, source_target_pairs={{0,8},{4,12},{8,0},{12,4},{16,24},{20,28},{24,16},{28,20},{1,9},{5... | collective-permute-start | bytes 442376 | tf_op jit(solution)/shard_map/ppermute | solution.py:405
  18.9 0.9 %collective-permute-start.3 = (bf16[144,512]{1,0:T(8,128)(2,1)S(1)}, bf16[144,512]{1,0:T(8,128)(2,1)S(1)}, u32[]{:S(2)}, u32[]{:S(2)}) collective-permute-start(bf16[144,512]{1,0:T(8,128)(2,1)S(1)} %get-tuple-element.38), channel_id=1, source_target_pairs={{0,12},{4,8},{8,4},{12,0},{16,28},{20,24},{24,20},{28,16},{1,13},{... | collective-permute-start | bytes 442376 | tf_op jit(solution)/shard_map/ppermute | solution.py:405
  19.8 5.5 %later_states.1 = (bf16[768,2048]{1,0:T(8,128)(2,1)S(1)}, bf16[144,512]{1,0:T(8,128)(2,1)S(1)}, bf16[144,512]{1,0:T(8,128)(2,1)S(1)}, bf16[144,512]{1,0:T(8,128)(2,1)S(1)}, bf16[144,512]{1,0:T(8,128)(2,1)S(1)}) custom-call(s32[1]{0:T(128)} %bitcast.refs_0_.place_ref, bf16[768,2048]{1,0:T(8,128)(2,1)S(1)} %get-tuple-element.32.refs_1_, ...), custom_call_target="tpu_custom_call" | custom-call | bytes 6291456 | tf_op jit(solution)/shard_map/later_states/pallas_call | solution.py:263
  25.2 1.1 %collective-permute-start.4 = (bf16[144,512]{1,0:T(8,128)(2,1)S(1)}, bf16[144,512]{1,0:T(8,128)(2,1)S(1)}, u32[]{:S(2)}, u32[]{:S(2)}) collective-permute-start(bf16[144,512]{1,0:T(8,128)(2,1)S(1)} %get-tuple-element.46), channel_id=1, source_target_pairs={{0,4},{4,0},{8,12},{12,8},{16,20},{20,16},{24,28},{28,24},{1,5},{5... | collective-permute-start | bytes 442376 | tf_op jit(solution)/shard_map/ppermute | solution.py:405
  26.3 1.6 %collective-permute-start.5 = (bf16[144,512]{1,0:T(8,128)(2,1)S(1)}, bf16[144,512]{1,0:T(8,128)(2,1)S(1)}, u32[]{:S(2)}, u32[]{:S(2)}) collective-permute-start(bf16[144,512]{1,0:T(8,128)(2,1)S(1)} %get-tuple-element.47), channel_id=1, source_target_pairs={{0,8},{4,12},{8,0},{12,4},{16,24},{20,28},{24,16},{28,20},{1,9},{5... | collective-permute-start | bytes 442376 | tf_op jit(solution)/shard_map/ppermute | solution.py:405
  27.9 5.5 %local.3.refs_1_ = f32[768,2048]{1,0:T(8,128)S(1)} custom-call(bf16[768,2048]{1,0:T(8,128)(2,1)S(1)} %get-tuple-element.52.refs_0_, f32[768,128]{1,0:T(8,128)S(1)} %get-tuple-element.41.refs_1_, f32[768,128]{1,0:T(8,128)S(1)} %get-tuple-element.42.refs_2_, f32[16,128]{1,0:T(8,128)S(1)} %get-tuple-element.31.refs_7_.refs_5_.refs_3_, ...), custom_call_target="tpu_custom_call" | custom-call | flops 2013265920 | bytes 9437184 | tf_op jit(solution)/shard_map/local/pallas_call | solution.py:343
  33.4 0.0 collective-permute-done.1.refs_1_
  33.4 0.9 %collective-permute-start.6 = (bf16[144,512]{1,0:T(8,128)(2,1)S(1)}, bf16[144,512]{1,0:T(8,128)(2,1)S(1)}, u32[]{:S(2)}, u32[]{:S(2)}) collective-permute-start(bf16[144,512]{1,0:T(8,128)(2,1)S(1)} %get-tuple-element.48), channel_id=1, source_target_pairs={{0,12},{4,8},{8,4},{12,0},{16,28},{20,24},{24,20},{28,16},{1,13},{... | collective-permute-start | bytes 442376 | tf_op jit(solution)/shard_map/ppermute | solution.py:405
  34.3 0.0 collective-permute-done.2.refs_2_
  34.3 0.0 collective-permute-done.3.refs_3_
  34.3 0.2 combine.2
  34.6 4.9 %collective-permute-start.11 = (bf16[128,512]{1,0:T(8,128)(2,1)S(1)}, bf16[128,512]{1,0:T(8,128)(2,1)S(1)}, u32[]{:S(2)}, u32[]{:S(2)}) collective-permute-start(bf16[128,512]{1,0:T(8,128)(2,1)S(1)} %get-tuple-element.39), channel_id=1, source_target_pairs={{0,16},{4,20},{8,24},{12,28},{1,17},{5,21},{9,25},{13,29},{2,18},{... | collective-permute-start | bytes 393224 | tf_op jit(solution)/shard_map/ppermute | solution.py:400
  39.6 0.0 collective-permute-done.4.refs_1_
  39.6 0.0 collective-permute-done.5.refs_2_
  39.6 0.0 collective-permute-done.6.refs_3_
  39.6 0.2 combine.3
  39.8 4.6 %collective-permute-start.7 = (bf16[128,512]{1,0:T(8,128)(2,1)S(1)}, bf16[128,512]{1,0:T(8,128)(2,1)S(1)}, u32[]{:S(2)}, u32[]{:S(2)}) collective-permute-start(bf16[128,512]{1,0:T(8,128)(2,1)S(1)} %get-tuple-element.51), channel_id=1, source_target_pairs={{0,16},{4,20},{8,24},{12,28},{1,17},{5,21},{9,25},{13,29},{2,18},{... | collective-permute-start | bytes 393224 | tf_op jit(solution)/shard_map/ppermute | solution.py:400
  44.5 0.0 copy-start.5
  44.5 5.5 %local.2.refs_1_ = f32[768,2048]{1,0:T(8,128)S(1)} custom-call(bf16[768,2048]{1,0:T(8,128)(2,1)S(1)} %get-tuple-element.40.refs_0_, f32[768,128]{1,0:T(8,128)S(1)} %get-tuple-element.41.refs_1_, f32[768,128]{1,0:T(8,128)S(1)} %get-tuple-element.42.refs_2_, f32[16,128]{1,0:T(8,128)S(1)} %get-tuple-element.31.refs_7_.refs_5_.refs_3_, ...), custom_call_target="tpu_custom_call" | custom-call | flops 2013265920 | bytes 9437184 | tf_op jit(solution)/shard_map/local/pallas_call | solution.py:343
  50.0 0.0 collective-permute-done.11
  50.0 0.2 fusion.15
  50.2 1.5 %collective-permute-start.12 = (bf16[128,512]{1,0:T(8,128)(2,1)S(1)}, bf16[128,512]{1,0:T(8,128)(2,1)S(1)}, u32[]{:S(2)}, u32[]{:S(2)}) collective-permute-start(bf16[128,512]{1,0:T(8,128)(2,1)S(1)} %get-tuple-element.56), channel_id=1, source_target_pairs={{0,4},{4,0},{8,12},{12,8},{16,20},{20,16},{24,28},{28,24},{1,5},{5... | collective-permute-start | bytes 393224 | tf_op jit(solution)/shard_map/ppermute | solution.py:405
  51.7 0.9 %collective-permute-start.13 = (bf16[128,512]{1,0:T(8,128)(2,1)S(1)}, bf16[128,512]{1,0:T(8,128)(2,1)S(1)}, u32[]{:S(2)}, u32[]{:S(2)}) collective-permute-start(bf16[128,512]{1,0:T(8,128)(2,1)S(1)} %get-tuple-element.57), channel_id=1, source_target_pairs={{0,8},{4,12},{8,0},{12,4},{16,24},{20,28},{24,16},{28,20},{1,9},{5... | collective-permute-start | bytes 393224 | tf_op jit(solution)/shard_map/ppermute | solution.py:405
  52.5 1.2 %collective-permute-start.14 = (bf16[128,512]{1,0:T(8,128)(2,1)S(1)}, bf16[128,512]{1,0:T(8,128)(2,1)S(1)}, u32[]{:S(2)}, u32[]{:S(2)}) collective-permute-start(bf16[128,512]{1,0:T(8,128)(2,1)S(1)} %get-tuple-element.55), channel_id=1, source_target_pairs={{0,12},{4,8},{8,4},{12,0},{16,28},{20,24},{24,20},{28,16},{1,13},{... | collective-permute-start | bytes 393224 | tf_op jit(solution)/shard_map/ppermute | solution.py:405
  53.7 0.0 collective-permute-done.7
  53.7 0.2 fusion.7
  53.9 1.8 %collective-permute-start.10 = (bf16[128,512]{1,0:T(8,128)(2,1)S(1)}, bf16[128,512]{1,0:T(8,128)(2,1)S(1)}, u32[]{:S(2)}, u32[]{:S(2)}) collective-permute-start(bf16[128,512]{1,0:T(8,128)(2,1)S(1)} %get-tuple-element.59), channel_id=1, source_target_pairs={{0,12},{4,8},{8,4},{12,0},{16,28},{20,24},{24,20},{28,16},{1,13},{... | collective-permute-start | bytes 393224 | tf_op jit(solution)/shard_map/ppermute | solution.py:405
  55.7 1.1 %collective-permute-start.8 = (bf16[128,512]{1,0:T(8,128)(2,1)S(1)}, bf16[128,512]{1,0:T(8,128)(2,1)S(1)}, u32[]{:S(2)}, u32[]{:S(2)}) collective-permute-start(bf16[128,512]{1,0:T(8,128)(2,1)S(1)} %get-tuple-element.60), channel_id=1, source_target_pairs={{0,4},{4,0},{8,12},{12,8},{16,20},{20,16},{24,28},{28,24},{1,5},{5... | collective-permute-start | bytes 393224 | tf_op jit(solution)/shard_map/ppermute | solution.py:405
  56.7 0.1 collective-permute-done.12.refs_6_
  56.9 1.2 %collective-permute-start.9 = (bf16[128,512]{1,0:T(8,128)(2,1)S(1)}, bf16[128,512]{1,0:T(8,128)(2,1)S(1)}, u32[]{:S(2)}, u32[]{:S(2)}) collective-permute-start(bf16[128,512]{1,0:T(8,128)(2,1)S(1)} %get-tuple-element.61), channel_id=1, source_target_pairs={{0,8},{4,12},{8,0},{12,4},{16,24},{20,28},{24,16},{28,20},{1,9},{5... | collective-permute-start | bytes 393224 | tf_op jit(solution)/shard_map/ppermute | solution.py:405
  58.1 0.0 collective-permute-done.13.refs_7_
  58.1 0.3 collective-permute-done.14.refs_8_
  58.4 3.5 %finish.2.refs_9_ = bf16[768,4096]{1,0:T(8,128)(2,1)} custom-call(s32[1]{0:T(128)} %bitcast.refs_0_.place_ref, f32[768,2048]{1,0:T(8,128)S(1)} %local.3.refs_1_, f32[768,128]{1,0:T(8,128)S(1)} %get-tuple-element.44.refs_2_, bf16[768,256]{1,0:T(8,128)(2,1)S(1)} %get-tuple-element.43.refs_4_.refs_3_, f32[1,4096]{1,0:T(1,128)S(1)} %bitcast.30, ...), custom_call_target="tpu_custom_call" | custom-call | flops 1610612736 | bytes 9437184 | tf_op jit(solution)/shard_map/finish/pallas_call | solution.py:385
  61.9 0.0 collective-permute-done.10.refs_8_
  61.9 0.0 collective-permute-done.8.refs_6_
  61.9 0.0 collective-permute-done.9.refs_7_
  62.0 3.5 %finish.3 = bf16[768,4096]{1,0:T(8,128)(2,1)} custom-call(s32[1]{0:T(128)} %bitcast.refs_0_.place_ref, f32[768,2048]{1,0:T(8,128)S(1)} %local.2.refs_1_, f32[768,128]{1,0:T(8,128)S(1)} %get-tuple-element.44.refs_2_, bf16[768,256]{1,0:T(8,128)(2,1)S(1)} %get-tuple-element.43.refs_4_.refs_3_, f32[1,4096]{1,0:T(1,128)S(1)} %bitcast.31, ...), custom_call_target="tpu_custom_call", output_to_operand_aliasing={{}: (9, {})} | custom-call | flops 1610612736 | bytes 9437184 | tf_op jit(solution)/shard_map/finish/pallas_call | solution.py:385
  (16 shorter events, 0.1 us)
Async XLA Ops:
  0.0 1.0 %copy-start = (bf16[768,256]{1,0:T(8,128)(2,1)S(1)}, bf16[768,256]{1,0:T(8,128)(2,1)}, u32[]{:S(2)}) copy-start(bf16[768,256]{1,0:T(8,128)(2,1)} %refs_2_.1) | copy-start | bytes 1179652
  1.0 5.9 %copy-start.7 = (f32[64]{0:T(128)S(1)}, f32[64]{0:T(128)}, u32[]{:S(2)}) copy-start(f32[64]{0:T(128)} %param.14) | copy-start | bytes 772
  1.0 6.0 %copy-start.3 = (f32[768,64]{0,1:T(8,128)S(1)}, f32[768,64]{0,1:T(8,128)}, u32[]{:S(2)}) copy-start(f32[768,64]{0,1:T(8,128)} %param.11) | copy-start | bytes 589828
  1.0 6.0 %copy-start.4 = (f32[768,64]{0,1:T(8,128)S(1)}, f32[768,64]{0,1:T(8,128)}, u32[]{:S(2)}) copy-start(f32[768,64]{0,1:T(8,128)} %param.10) | copy-start | bytes 589828
  1.0 7.5 %copy-start.1 = (bf16[768,256]{1,0:T(8,128)(2,1)S(1)}, bf16[768,256]{1,0:T(8,128)(2,1)}, u32[]{:S(2)}) copy-start(bf16[768,256]{1,0:T(8,128)(2,1)} %refs_2_.1) | copy-start | bytes 1179652
  1.0 7.5 %copy-start.2 = (f32[4,4096]{1,0:T(4,128)S(1)}, f32[4,4096]{1,0:T(4,128)}, u32[]{:S(2)}) copy-start(f32[4,4096]{1,0:T(4,128)} %refs_3_.1) | copy-start | bytes 196612
  1.0 7.5 %copy-start.6 = (f32[4,256]{1,0:T(4,128)S(1)}, f32[4,256]{1,0:T(4,128)}, u32[]{:S(2)}) copy-start(f32[4,256]{1,0:T(4,128)} %refs_5_.1) | copy-start | bytes 12292
  2.1 6.4 %collective-permute-start = (bf16[3,4352]{1,0:T(4,128)(2,1)S(1)}, bf16[3,4352]{1,0:T(4,128)(2,1)S(1)}, u32[]{:S(2)}, u32[]{:S(2)}) collective-permute-start(bf16[3,4352]{1,0:T(4,128)(2,1)S(1)} %slice.68), channel_id=1, source_target_pairs={{0,4},{4,8},{8,12},{12,16},{16,20},{20,24},{24,28},{1,5},{5,9},{9,... | collective-permute-start | bytes 78344 | tf_op jit(solution)/shard_map/ppermute | solution.py:400
  14.9 18.5 %collective-permute-start.1 = (bf16[144,512]{1,0:T(8,128)(2,1)S(1)}, bf16[144,512]{1,0:T(8,128)(2,1)S(1)}, u32[]{:S(2)}, u32[]{:S(2)}) collective-permute-start(bf16[144,512]{1,0:T(8,128)(2,1)S(1)} %get-tuple-element.36), channel_id=1, source_target_pairs={{0,4},{4,0},{8,12},{12,8},{16,20},{20,16},{24,28},{28,24},{1,5},{5... | collective-permute-start | bytes 442376 | tf_op jit(solution)/shard_map/ppermute | solution.py:405
  17.3 17.0 %collective-permute-start.2 = (bf16[144,512]{1,0:T(8,128)(2,1)S(1)}, bf16[144,512]{1,0:T(8,128)(2,1)S(1)}, u32[]{:S(2)}, u32[]{:S(2)}) collective-permute-start(bf16[144,512]{1,0:T(8,128)(2,1)S(1)} %get-tuple-element.37), channel_id=1, source_target_pairs={{0,8},{4,12},{8,0},{12,4},{16,24},{20,28},{24,16},{28,20},{1,9},{5... | collective-permute-start | bytes 442376 | tf_op jit(solution)/shard_map/ppermute | solution.py:405
  18.9 15.5 %collective-permute-start.3 = (bf16[144,512]{1,0:T(8,128)(2,1)S(1)}, bf16[144,512]{1,0:T(8,128)(2,1)S(1)}, u32[]{:S(2)}, u32[]{:S(2)}) collective-permute-start(bf16[144,512]{1,0:T(8,128)(2,1)S(1)} %get-tuple-element.38), channel_id=1, source_target_pairs={{0,12},{4,8},{8,4},{12,0},{16,28},{20,24},{24,20},{28,16},{1,13},{... | collective-permute-start | bytes 442376 | tf_op jit(solution)/shard_map/ppermute | solution.py:405
  25.2 14.3 %collective-permute-start.4 = (bf16[144,512]{1,0:T(8,128)(2,1)S(1)}, bf16[144,512]{1,0:T(8,128)(2,1)S(1)}, u32[]{:S(2)}, u32[]{:S(2)}) collective-permute-start(bf16[144,512]{1,0:T(8,128)(2,1)S(1)} %get-tuple-element.46), channel_id=1, source_target_pairs={{0,4},{4,0},{8,12},{12,8},{16,20},{20,16},{24,28},{28,24},{1,5},{5... | collective-permute-start | bytes 442376 | tf_op jit(solution)/shard_map/ppermute | solution.py:405
  26.3 13.2 %collective-permute-start.5 = (bf16[144,512]{1,0:T(8,128)(2,1)S(1)}, bf16[144,512]{1,0:T(8,128)(2,1)S(1)}, u32[]{:S(2)}, u32[]{:S(2)}) collective-permute-start(bf16[144,512]{1,0:T(8,128)(2,1)S(1)} %get-tuple-element.47), channel_id=1, source_target_pairs={{0,8},{4,12},{8,0},{12,4},{16,24},{20,28},{24,16},{28,20},{1,9},{5... | collective-permute-start | bytes 442376 | tf_op jit(solution)/shard_map/ppermute | solution.py:405
  33.4 6.2 %collective-permute-start.6 = (bf16[144,512]{1,0:T(8,128)(2,1)S(1)}, bf16[144,512]{1,0:T(8,128)(2,1)S(1)}, u32[]{:S(2)}, u32[]{:S(2)}) collective-permute-start(bf16[144,512]{1,0:T(8,128)(2,1)S(1)} %get-tuple-element.48), channel_id=1, source_target_pairs={{0,12},{4,8},{8,4},{12,0},{16,28},{20,24},{24,20},{28,16},{1,13},{... | collective-permute-start | bytes 442376 | tf_op jit(solution)/shard_map/ppermute | solution.py:405
  34.6 15.4 %collective-permute-start.11 = (bf16[128,512]{1,0:T(8,128)(2,1)S(1)}, bf16[128,512]{1,0:T(8,128)(2,1)S(1)}, u32[]{:S(2)}, u32[]{:S(2)}) collective-permute-start(bf16[128,512]{1,0:T(8,128)(2,1)S(1)} %get-tuple-element.39), channel_id=1, source_target_pairs={{0,16},{4,20},{8,24},{12,28},{1,17},{5,21},{9,25},{13,29},{2,18},{... | collective-permute-start | bytes 393224 | tf_op jit(solution)/shard_map/ppermute | solution.py:400
  39.8 13.9 %collective-permute-start.7 = (bf16[128,512]{1,0:T(8,128)(2,1)S(1)}, bf16[128,512]{1,0:T(8,128)(2,1)S(1)}, u32[]{:S(2)}, u32[]{:S(2)}) collective-permute-start(bf16[128,512]{1,0:T(8,128)(2,1)S(1)} %get-tuple-element.51), channel_id=1, source_target_pairs={{0,16},{4,20},{8,24},{12,28},{1,17},{5,21},{9,25},{13,29},{2,18},{... | collective-permute-start | bytes 393224 | tf_op jit(solution)/shard_map/ppermute | solution.py:400
  44.5 13.9 %copy-start.5 = (f32[4096]{0:T(1024)S(1)}, f32[4096]{0:T(1024)}, u32[]{:S(2)}) copy-start(f32[4096]{0:T(1024)} %param.15) | copy-start | bytes 49156
  50.2 6.7 %collective-permute-start.12 = (bf16[128,512]{1,0:T(8,128)(2,1)S(1)}, bf16[128,512]{1,0:T(8,128)(2,1)S(1)}, u32[]{:S(2)}, u32[]{:S(2)}) collective-permute-start(bf16[128,512]{1,0:T(8,128)(2,1)S(1)} %get-tuple-element.56), channel_id=1, source_target_pairs={{0,4},{4,0},{8,12},{12,8},{16,20},{20,16},{24,28},{28,24},{1,5},{5... | collective-permute-start | bytes 393224 | tf_op jit(solution)/shard_map/ppermute | solution.py:405
  51.7 6.4 %collective-permute-start.13 = (bf16[128,512]{1,0:T(8,128)(2,1)S(1)}, bf16[128,512]{1,0:T(8,128)(2,1)S(1)}, u32[]{:S(2)}, u32[]{:S(2)}) collective-permute-start(bf16[128,512]{1,0:T(8,128)(2,1)S(1)} %get-tuple-element.57), channel_id=1, source_target_pairs={{0,8},{4,12},{8,0},{12,4},{16,24},{20,28},{24,16},{28,20},{1,9},{5... | collective-permute-start | bytes 393224 | tf_op jit(solution)/shard_map/ppermute | solution.py:405
  52.5 5.9 %collective-permute-start.14 = (bf16[128,512]{1,0:T(8,128)(2,1)S(1)}, bf16[128,512]{1,0:T(8,128)(2,1)S(1)}, u32[]{:S(2)}, u32[]{:S(2)}) collective-permute-start(bf16[128,512]{1,0:T(8,128)(2,1)S(1)} %get-tuple-element.55), channel_id=1, source_target_pairs={{0,12},{4,8},{8,4},{12,0},{16,28},{20,24},{24,20},{28,16},{1,13},{... | collective-permute-start | bytes 393224 | tf_op jit(solution)/shard_map/ppermute | solution.py:405
  53.9 8.0 %collective-permute-start.10 = (bf16[128,512]{1,0:T(8,128)(2,1)S(1)}, bf16[128,512]{1,0:T(8,128)(2,1)S(1)}, u32[]{:S(2)}, u32[]{:S(2)}) collective-permute-start(bf16[128,512]{1,0:T(8,128)(2,1)S(1)} %get-tuple-element.59), channel_id=1, source_target_pairs={{0,12},{4,8},{8,4},{12,0},{16,28},{20,24},{24,20},{28,16},{1,13},{... | collective-permute-start | bytes 393224 | tf_op jit(solution)/shard_map/ppermute | solution.py:405
  55.7 6.3 %collective-permute-start.8 = (bf16[128,512]{1,0:T(8,128)(2,1)S(1)}, bf16[128,512]{1,0:T(8,128)(2,1)S(1)}, u32[]{:S(2)}, u32[]{:S(2)}) collective-permute-start(bf16[128,512]{1,0:T(8,128)(2,1)S(1)} %get-tuple-element.60), channel_id=1, source_target_pairs={{0,4},{4,0},{8,12},{12,8},{16,20},{20,16},{24,28},{28,24},{1,5},{5... | collective-permute-start | bytes 393224 | tf_op jit(solution)/shard_map/ppermute | solution.py:405
  56.9 5.1 %collective-permute-start.9 = (bf16[128,512]{1,0:T(8,128)(2,1)S(1)}, bf16[128,512]{1,0:T(8,128)(2,1)S(1)}, u32[]{:S(2)}, u32[]{:S(2)}) collective-permute-start(bf16[128,512]{1,0:T(8,128)(2,1)S(1)} %get-tuple-element.61), channel_id=1, source_target_pairs={{0,8},{4,12},{8,0},{12,4},{16,24},{20,28},{24,16},{28,20},{1,9},{5... | collective-permute-start | bytes 393224 | tf_op jit(solution)/shard_map/ppermute | solution.py:405

commit v4 on v3

v4 whole, which is shorter than its diff:
```python
import jax
import jax.numpy as jnp
from jax import lax
from jax.experimental import pallas as pl
from jax.experimental.pallas import tpu as pltpu
from jax.sharding import PartitionSpec as P

CHUNK = 128
SQUARE = 4
GROUPS = 2
SUB = 256
EDGE = 16
LANES = 128
F32 = jnp.float32
BF16 = jnp.bfloat16


def params(mib=16):
    return pltpu.CompilerParams(vmem_limit_bytes=mib * 1024 * 1024)


def dot(a, b):
    return jnp.dot(a, b, preferred_element_type=F32)


def dot_rows(a, b):
    return lax.dot_general(a, b, (((1,), (1,)), ((), ())), preferred_element_type=F32)


def pieces(value, count):
    out = []
    for _ in range(count):
        out.append(value.astype(BF16))
        value = value - out[-1].astype(F32)
    return out


def iota(shape, axis):
    return lax.broadcasted_iota(jnp.int32, shape, axis)


def hint(moved):
    return pl.CostEstimate(flops=0, bytes_accessed=moved, transcendentals=0)


def vmem():
    return pl.BlockSpec(memory_space=pltpu.VMEM)


def smem():
    return pl.BlockSpec(memory_space=pltpu.SMEM)


def anywhere():
    return pl.BlockSpec(memory_space=pl.ANY)


def over_heads(values, head_width, first, cols):
    blocks = []
    for lane in range(0, cols, LANES):
        head = (first + lane + iota(values.shape, 1)) // head_width
        blocks.append(jnp.take_along_axis(values, head, axis=1, mode="promise_in_bounds"))
    return jnp.concatenate(blocks, axis=1)


def silu_conv(rows_back, taps):
    count = len(taps)
    half = sum(rows_back(k) * (0.5 * taps[count - 1 - k]) for k in range(count))
    return half + half * jnp.tanh(half)


def edges_kernel(inner_ref, proj_ref, out_ref, sems):
    width = inner_ref.shape[1]
    last = pl.ds(inner_ref.shape[0] - EDGE, EDGE)
    copies = [
        pltpu.make_async_copy(inner_ref.at[last, :], out_ref.at[:, :width], sems.at[0]),
        pltpu.make_async_copy(proj_ref.at[last, :], out_ref.at[:, width:], sems.at[1]),
    ]
    for copy in copies:
        copy.start()
    for copy in copies:
        copy.wait()


def last_rows(inner, proj):
    width = inner.shape[1] + proj.shape[1]
    return pl.pallas_call(
        edges_kernel,
        in_specs=[anywhere()] * 2,
        out_specs=vmem(),
        out_shape=jax.ShapeDtypeStruct((EDGE, width), BF16),
        scratch_shapes=[pltpu.SemaphoreType.DMA((2,))],
        compiler_params=params(),
        name="edges",
    )(inner, proj)


def first_chunk(in_ref, head_ref, sem, first):
    return pltpu.make_async_copy(in_ref.at[pl.ds(0, CHUNK), pl.ds(first, head_ref.shape[1])], head_ref, sem)


def decay_kernel(decay_ref, step_ref, skip_ref, inner_ref, fwd_ref, inv_ref, dev_ref, fac_ref, head_ref, sem):
    head = first_chunk(inner_ref, head_ref, sem, 0)
    head.start()
    heads, rows = decay_ref.shape
    chunks = rows // CHUNK
    lower = jnp.where(iota((CHUNK, CHUNK), 0) >= iota((CHUNK, CHUNK), 1), 1.0, 0.0).astype(BF16)
    same = jnp.where(iota((CHUNK, CHUNK), 0) == iota((CHUNK, CHUNK), 1), 1.0, 0.0).astype(BF16)
    copies = LANES // heads
    cums, steps = [], []
    for c in range(chunks):
        at = pl.ds(c * CHUNK, CHUNK)
        decay = jnp.concatenate([decay_ref[:, at]] * copies, axis=0)
        step = jnp.concatenate([step_ref[:, at]] * copies, axis=0)
        cums.append(sum(dot_rows(lower, piece) for piece in pieces(decay, 3)))
        steps.append(sum(dot_rows(same, piece) for piece in pieces(step, 3)))
    totals = [cum[CHUNK - 1 :] for cum in cums]
    middles = [cum[CHUNK // 2 - 1 : CHUNK // 2] for cum in cums]
    before = [jnp.zeros_like(totals[0])]
    for c in range(chunks):
        before.append(before[c] + totals[c])
    fac_ref[...] = jnp.zeros_like(fac_ref)
    for c in range(chunks):
        at = pl.ds(c * CHUNK, CHUNK)
        fwd_ref[at, :] = jnp.exp(cums[c] - middles[c])
        inv_ref[at, :] = jnp.exp(middles[c] - cums[c]) * steps[c]
        dev_ref[at, :] = jnp.exp(before[c] + cums[c])
        following = middles[c + 1] if c + 1 < chunks else 0.0
        fac_ref[c : c + 1, :] = jnp.exp(totals[c] - middles[c] + following)
    fac_ref[chunks : chunks + 1, :] = skip_ref[:1]
    fac_ref[8:9, :] = jnp.exp(before[chunks])
    head.wait()


def decays(decay_log, step_size, skip_weight, inner):
    rows, heads = decay_log.shape
    wide = jax.ShapeDtypeStruct((rows, LANES), F32)
    return pl.pallas_call(
        decay_kernel,
        in_specs=[vmem()] * 3 + [anywhere()],
        out_specs=[vmem()] * 5,
        out_shape=(wide, wide, wide, jax.ShapeDtypeStruct((16, LANES), F32), jax.ShapeDtypeStruct((CHUNK, inner.shape[1] // GROUPS), BF16)),
        scratch_shapes=[pltpu.SemaphoreType.DMA],
        compiler_params=params(),
        name="decays",
    )(decay_log.T, step_size.T, jnp.broadcast_to(jnp.tile(skip_weight, LANES // heads)[None], (8, LANES)), inner)


def project(proj_ref, edge_ref, taps_ref, mix_ref, bt_ref, wide_ref):
    rows, width = proj_ref.shape
    state = width // 2
    taps = [taps_ref[k : k + 1, :] for k in range(taps_ref.shape[0])]
    causal = iota((CHUNK, CHUNK), 0) >= iota((CHUNK, CHUNK), 1)
    past = edge_ref.shape[0]
    wide_ref[EDGE - past : EDGE, :] = edge_ref[:, edge_ref.shape[1] - width :].astype(F32)
    wide_ref[EDGE:, :] = proj_ref[...].astype(F32)
    for c in range(rows // CHUNK):
        at = pl.ds(c * CHUNK, CHUNK)
        both = silu_conv(lambda k: wide_ref[pl.ds(EDGE + c * CHUNK - k, CHUNK), :], taps).astype(BF16)
        b_rows, c_rows = both[:, :state], both[:, state:]
        mix_ref[at, :CHUNK] = jnp.where(causal, dot_rows(c_rows, b_rows), 0.0).astype(BF16)
        mix_ref[at, CHUNK:] = c_rows
        bt_ref[:, at] = b_rows.astype(F32).T.astype(BF16)


def summarize(place_ref, in_ref, ready, edge_ref, taps_ref, inv_ref, fac_ref, bt_ref, x_ref, scaled_ref, opening_ref, slots, window_ref, sum_ref, row_ref, head_width, first):
    rows, wide = x_ref.shape
    cols = wide // SQUARE
    state = bt_ref.shape[0]
    count = taps_ref.shape[0]
    chunks = rows // CHUNK
    for block in range(wide // LANES):
        at_lanes = pl.ds(first + block * LANES, LANES)
        window_ref[block, EDGE + CHUNK - count + 1 :, :] = edge_ref[:, at_lanes].astype(F32)
    row_ref[...] = over_heads(fac_ref[...], head_width, first, wide)
    sum_ref[...] = jnp.zeros_like(sum_ref)

    def chunk_step(c, _):
        ready(c)
        at = pl.ds(pl.multiple_of(c * CHUNK, CHUNK), CHUNK)
        for sub in range(wide // SUB):
            at_cols = pl.ds(sub * SUB, SUB)
            here = first + sub * SUB
            rows_here = in_ref[at, at_cols].astype(F32)
            xs = []
            for lane in range(0, SUB, LANES):
                block = (sub * SUB + lane) // LANES
                window_ref[block, EDGE - 8 : EDGE, :] = window_ref[block, EDGE + CHUNK - 8 :, :]
                window_ref[block, EDGE:, :] = rows_here[:, lane : lane + LANES]
                taps = [taps_ref[k : k + 1, pl.ds(here + lane, LANES)] for k in range(count)]
                xs.append(silu_conv(lambda k: window_ref[block, pl.ds(EDGE - k, CHUNK), :], taps))
            x = jnp.concatenate(xs, axis=1)
            x_ref[at, at_cols] = x.astype(BF16)
            scaled = (over_heads(inv_ref[at, :], head_width, here, SUB) * x).astype(BF16)
            scaled_ref[at, at_cols] = scaled
            running = sum_ref[:, at_cols]
            opening_ref[at, at_cols] = running.astype(BF16)
            sum_ref[:, at_cols] = row_ref[pl.ds(c, 1), at_cols] * (running + dot(bt_ref[:, at], scaled))
        return 0

    lax.fori_loop(0, chunks, chunk_step, 0)
    row = iota((EDGE, cols), 0)
    for k, slot in enumerate(slots):
        start = pl.multiple_of((k ^ place_ref[0]) * cols, cols)
        slot[:state, :] = sum_ref[:, pl.ds(start, cols)].astype(BF16)
        decay = row_ref[8:16, pl.ds(start, cols)][:1]
        high = decay.astype(BF16).astype(F32)
        slot[state:, :] = jnp.where(row == 0, high, jnp.where(row == 1, decay - high, 0.0)).astype(BF16)


def first_kernel(place_ref, in_ref, head_ref, proj_ref, edge_ref, taps_ref, proj_taps_ref, inv_ref, fac_ref, x_ref, scaled_ref, opening_ref, mix_ref, bt_ref, next_ref, *rest, head_width):
    slots, (block_ref, wide_ref, window_ref, sum_ref, row_ref, sems) = rest[:SQUARE], rest[SQUARE:]
    rows, wide = x_ref.shape

    def fetch(c):
        at = pl.ds(pl.multiple_of(c * CHUNK, CHUNK), CHUNK)
        return pltpu.make_async_copy(in_ref.at[at, pl.ds(0, wide)], block_ref.at[at, :], sems.at[c])

    for c in range(1, rows // CHUNK):
        fetch(c).start()
    upcoming = first_chunk(in_ref, next_ref, sems.at[0], wide)
    upcoming.start()
    block_ref[:CHUNK, :] = head_ref[...]
    project(proj_ref, edge_ref, proj_taps_ref, mix_ref, bt_ref, wide_ref)
    summarize(place_ref, block_ref, lambda c: pl.when(c > 0)(lambda: fetch(c).wait()), edge_ref, taps_ref, inv_ref, fac_ref, bt_ref, x_ref, scaled_ref, opening_ref, slots, window_ref, sum_ref, row_ref, head_width, 0)
    upcoming.wait()


def slot_shapes(state, wide):
    return [jax.ShapeDtypeStruct((state + EDGE, wide // SQUARE), BF16)] * SQUARE


def sum_scratch(state, wide):
    return [pltpu.VMEM((wide // LANES, EDGE + CHUNK, LANES), F32), pltpu.VMEM((state, wide), F32), pltpu.VMEM((16, wide), F32)]


def first_states(place, inner, head, proj, edge, taps, proj_taps, inv, fac, head_width):
    rows, width = inner.shape
    state = proj.shape[1] // 2
    wide = width // GROUPS
    chunks = rows // CHUNK
    out = pl.pallas_call(
        lambda *refs: first_kernel(*refs, head_width=head_width),
        in_specs=[smem(), anywhere()] + [vmem()] * 7,
        out_specs=[vmem()] * (SQUARE + 6),
        out_shape=[
            jax.ShapeDtypeStruct((rows, wide), BF16),
            jax.ShapeDtypeStruct((rows, wide), BF16),
            jax.ShapeDtypeStruct((chunks * state, wide), BF16),
            jax.ShapeDtypeStruct((rows, CHUNK + state), BF16),
            jax.ShapeDtypeStruct((state, rows), BF16),
            jax.ShapeDtypeStruct((CHUNK, wide), BF16),
        ]
        + slot_shapes(state, wide),
        scratch_shapes=[pltpu.VMEM((rows, wide), BF16), pltpu.VMEM((EDGE + rows, 2 * state), F32)]
        + sum_scratch(state, wide)
        + [pltpu.SemaphoreType.DMA((chunks,))],
        compiler_params=params(),
        name="first_states",
    )(place, inner, head, proj, edge, taps, proj_taps, inv, fac)
    return out[:3], out[3:6], out[6:]


def later_kernel(place_ref, in_ref, head_ref, edge_ref, taps_ref, inv_ref, fac_ref, bt_ref, x_ref, scaled_ref, opening_ref, *rest, head_width, first):
    slots, (block_ref, window_ref, sum_ref, row_ref, sems) = rest[:SQUARE], rest[SQUARE:]
    rows, wide = x_ref.shape

    def fetch(c):
        at = pl.ds(pl.multiple_of(c * CHUNK, CHUNK), CHUNK)
        return pltpu.make_async_copy(in_ref.at[at, pl.ds(first, wide)], block_ref.at[at, :], sems.at[c])

    for c in range(1, rows // CHUNK):
        fetch(c).start()
    block_ref[:CHUNK, :] = head_ref[...]
    summarize(place_ref, block_ref, lambda c: pl.when(c > 0)(lambda: fetch(c).wait()), edge_ref, taps_ref, inv_ref, fac_ref, bt_ref, x_ref, scaled_ref, opening_ref, slots, window_ref, sum_ref, row_ref, head_width, first)


def later_states(place, inner, head, edge, taps, inv, fac, bt, head_width, group):
    rows, width = inner.shape
    wide = width // GROUPS
    state = bt.shape[0]
    chunks = rows // CHUNK
    out = pl.pallas_call(
        lambda *refs: later_kernel(*refs, head_width=head_width, first=group * wide),
        in_specs=[smem(), anywhere()] + [vmem()] * 6,
        out_specs=[vmem()] * (SQUARE + 3),
        out_shape=[
            jax.ShapeDtypeStruct((rows, wide), BF16),
            jax.ShapeDtypeStruct((rows, wide), BF16),
            jax.ShapeDtypeStruct((chunks * state, wide), BF16),
        ]
        + slot_shapes(state, wide),
        scratch_shapes=[pltpu.VMEM((rows, wide), BF16)] + sum_scratch(state, wide) + [pltpu.SemaphoreType.DMA((chunks,))],
        compiler_params=params(),
        name="later_states",
    )(place, inner, head, edge, taps, inv, fac, bt)
    return out[:3], out[3:]


def combine_kernel(place_ref, *refs):
    slots, (leaving_ref, prefix_ref, opening_ref, placed_ref) = refs[:SQUARE], refs[SQUARE:]
    state, cols = leaving_ref.shape
    spot = place_ref[0]
    for k in range(SQUARE):
        placed_ref[spot ^ k] = slots[k][...]
    running = jnp.zeros((state, cols), F32)
    opening = jnp.ones((1, cols), F32)
    for p in range(SQUARE):
        prefix_ref[spot ^ p] = running
        opening_ref[spot ^ p] = jnp.broadcast_to(opening, (8, cols))
        tail = placed_ref[p, state:, :].astype(F32)
        decay = tail[0:1] + tail[1:2]
        running = decay * running + placed_ref[p, :state, :].astype(F32)
        opening = decay * opening
    leaving_ref[...] = running.astype(BF16)
    opening_ref[SQUARE] = jnp.broadcast_to(opening, (8, cols))


def combine(place, slots):
    rows, cols = slots[0].shape
    state = rows - EDGE
    return pl.pallas_call(
        combine_kernel,
        in_specs=[smem()] + [vmem()] * SQUARE,
        out_specs=[vmem()] * 3,
        out_shape=(
            jax.ShapeDtypeStruct((state, cols), BF16),
            jax.ShapeDtypeStruct((SQUARE, state, cols), F32),
            jax.ShapeDtypeStruct((SQUARE + 1, 8, cols), F32),
        ),
        scratch_shapes=[pltpu.VMEM((SQUARE, rows, cols), BF16)],
        compiler_params=params(),
        name="combine",
    )(place, *slots)


def local_kernel(x_ref, scaled_ref, opening_ref, fwd_ref, fac_ref, mix_ref, out_ref, *, head_width, first):
    rows, wide = x_ref.shape
    chunks = rows // CHUNK
    state = opening_ref.shape[0] // chunks
    cols = wide // SQUARE

    def tile_step(j, _):
        base = pl.multiple_of(j * cols, cols)
        at_cols = pl.ds(base, cols)
        skip = over_heads(fac_ref[...], head_width, first + base, cols)[chunks : chunks + 1]
        for c in range(chunks):
            at = pl.ds(c * CHUNK, CHUNK)
            both = jnp.concatenate([scaled_ref[at, at_cols], opening_ref[pl.ds(c * state, state), at_cols]], axis=0)
            mixed = over_heads(fwd_ref[at, :], head_width, first + base, cols) * dot(mix_ref[at, :], both)
            out_ref[at, at_cols] = mixed + skip * x_ref[at, at_cols].astype(F32)
        return 0

    lax.fori_loop(0, SQUARE, tile_step, 0)


def local_parts(x, scaled, opening, fwd, fac, mix, head_width, group):
    rows, wide = x.shape
    return pl.pallas_call(
        lambda *refs: local_kernel(*refs, head_width=head_width, first=group * wide),
        in_specs=[vmem()] * 6,
        out_specs=vmem(),
        out_shape=jax.ShapeDtypeStruct((rows, wide), F32),
        compiler_params=params(),
        name="local",
    )(x, scaled, opening, fwd, fac, mix)


def normalize(place_ref, local_ref, dev_ref, mix_ref, gain_ref, slots, head_width, first, done):
    rows, wide = local_ref.shape
    cols = wide // SQUARE
    mean = jnp.where(iota((SUB, SUB), 0) // head_width == iota((SUB, SUB), 1) // head_width, 1.0 / head_width, 0.0).astype(BF16)
    for k in range(SQUARE):
        base = pl.multiple_of((k ^ place_ref[0]) * cols, cols)
        for sub in range(cols // SUB):
            at_cols = pl.ds(base + sub * SUB, SUB)
            here = first + base + sub * SUB
            carried = dot(mix_ref[:, CHUNK:], slots[k][:, sub * SUB : (sub + 1) * SUB])
            combined = local_ref[:, at_cols] + over_heads(dev_ref[...], head_width, here, SUB) * carried
            squares = dot((combined * combined).astype(BF16), mean)
            result = combined * lax.rsqrt(squares + 1e-05) * gain_ref[:, pl.ds(here, SUB)]
            done(k * (cols // SUB) + sub, base + sub * SUB, result.astype(BF16))


def finish_first_kernel(place_ref, local_ref, dev_ref, mix_ref, gain_ref, *rest, head_width):
    slots, out_ref = rest[:SQUARE], rest[SQUARE]

    def done(turn, column, result):
        out_ref[:, pl.ds(column, SUB)] = result

    normalize(place_ref, local_ref, dev_ref, mix_ref, gain_ref, slots, head_width, 0, done)


def finish_first(place, local, dev, mix, gain, slots, head_width):
    rows, wide = local.shape
    return pl.pallas_call(
        lambda *refs: finish_first_kernel(*refs, head_width=head_width),
        in_specs=[smem()] + [vmem()] * (4 + SQUARE),
        out_specs=vmem(),
        out_shape=jax.ShapeDtypeStruct((rows, wide), BF16),
        compiler_params=params(),
        name="finish_first",
    )(place, local, dev, mix, gain, *slots)


def finish_kernel(place_ref, local_ref, dev_ref, mix_ref, gain_ref, *rest, head_width):
    slots, (earlier_ref, out_ref, stage_ref, sems, earlier_sem) = rest[:SQUARE], rest[SQUARE:]
    first = earlier_ref.shape[1]
    earlier = pltpu.make_async_copy(earlier_ref, out_ref.at[:, pl.ds(0, first)], earlier_sem)
    earlier.start()
    copies = []

    def done(turn, column, result):
        stage_ref[turn] = result
        copies.append(pltpu.make_async_copy(stage_ref.at[turn], out_ref.at[:, pl.ds(first + column, SUB)], sems.at[turn]))
        copies[-1].start()

    normalize(place_ref, local_ref, dev_ref, mix_ref, gain_ref, slots, head_width, first, done)
    earlier.wait()
    for copy in copies:
        copy.wait()


def finish(place, local, dev, mix, gain, slots, earlier, head_width):
    rows, wide = local.shape
    return pl.pallas_call(
        lambda *refs: finish_kernel(*refs, head_width=head_width),
        in_specs=[smem()] + [vmem()] * (5 + SQUARE),
        out_specs=anywhere(),
        out_shape=jax.ShapeDtypeStruct((rows, wide * GROUPS), BF16),
        scratch_shapes=[pltpu.VMEM((wide // SUB, rows, SUB), BF16), pltpu.SemaphoreType.DMA((wide // SUB,)), pltpu.SemaphoreType.DMA],
        compiler_params=params(),
        name="finish",
    )(place, local, dev, mix, gain, *slots, earlier)


def shifted(x, by):
    length = lax.axis_size("ctx")
    return lax.ppermute(x, "ctx", [(i, i + by) for i in range(length - by)])


def swapped(x, k):
    length = lax.axis_size("ctx")
    return lax.ppermute(x, "ctx", [(i, i ^ k) for i in range(length)])


def previous_squares(leaving, decay):
    squares = lax.axis_size("ctx") // SQUARE
    entering = shifted(leaving, SQUARE)
    span = 1
    if squares > 2:
        window = shifted(decay, SQUARE)
    while span < squares - 1:
        behind = shifted(entering, SQUARE * span)
        entering = (entering.astype(F32) + window * behind.astype(F32)).astype(BF16)
        window = window * shifted(window, SQUARE * span)
        span *= 2
    return entering


def body(inner_input, state_proj, step_size, decay_log, conv_inner, conv_proj, skip_weight, norm_gain):
    rows, width = inner_input.shape
    heads = step_size.shape[1]
    head_width = width // heads
    past = conv_inner.shape[0] - 1
    kept, kept_proj = [pltpu.with_memory_space_constraint(a, pltpu.HBM) for a in (inner_input, state_proj)]
    place = jnp.full((1,), lax.axis_index("ctx") % SQUARE, jnp.int32)
    edge = shifted(last_rows(kept, kept_proj)[EDGE - past :], 1)
    fwd, inv, dev, fac, head = decays(decay_log, step_size, skip_weight, kept)
    gain = norm_gain[None]
    made, sent = [], []
    parts, (mix, bt, head), slots = first_states(place, kept, head, state_proj, edge, conv_inner, conv_proj, inv, fac, head_width)
    made.append(parts)
    sent.append([slots[0]] + [swapped(slots[k], k) for k in range(1, SQUARE)])
    parts, slots = later_states(place, kept, head, edge, conv_inner, inv, fac, bt, head_width, 1)
    made.append(parts)
    sent.append([slots[0]] + [swapped(slots[k], k) for k in range(1, SQUARE)])
    combined = [combine(place, sent[group]) for group in range(GROUPS)]
    arrived = [previous_squares(leaving, opening[SQUARE, :1]) for leaving, _, opening in combined]
    locals_ = [local_parts(*made[group], fwd, fac, mix, head_width, group) for group in range(GROUPS)]
    arrived[0], locals_[0] = lax.optimization_barrier((arrived[0], locals_[0]))
    returned = []
    for group in range(GROUPS):
        _, prefix, opening = combined[group]
        entering = [(prefix[k] + opening[k, :1] * arrived[group].astype(F32)).astype(BF16) for k in range(SQUARE)]
        returned.append([entering[0]] + [swapped(entering[k], k) for k in range(1, SQUARE)])
    earlier = finish_first(place, locals_[0], dev, mix, gain, returned[0], head_width)
    return finish(place, locals_[1], dev, mix, gain, returned[1], earlier, head_width)


def solution(mesh):
    split = P(("dp", "ctx"), None)
    return jax.shard_map(
        body, mesh=mesh, in_specs=(split, split, split, split, P(), P(), P(), P()), out_specs=split, check_vma=False
    )
```

time: 65.9 us -> 58.9 us (0.89)
  Pallas kernels: 32.4 us -> 26.2 us
  starting transfers between devices: 30.5 us -> 31.7 us
  local copies, waits for them, and re-layouts: 1.15 us -> 0.16 us
  waiting for transfers between devices: 0.91 us -> 0.04 us
    pallas_call x2, Pallas kernels: 11 us -> 5.29 us  [local_parts(): pl.pallas_call(lambda *refs: local_kernel(*refs, head_width=head_width, f...]
    ppermute x12, starting transfers between devices: 16.1 us -> 17.5 us  [swapped(): return lax.ppermute(x, 'ctx', [(i, i ^ k) for i in range(length)])]
    unnamed x16 -> x14, local copies, waits for them, and re-layouts: 1.02 us -> 0.03 us
  transfers between devices with their start and end apart: 15 -> 15, of which waited for: 3 -> 0; matrix products, arithmetic and copies ran while one was open for 1% -> 1% of each run, Pallas kernels for 33% -> 27%
where the time goes in v4:
time: 58.9 us; the launch traced here: 58.7 us
  starting transfers between devices  31.7 us (54%)
  Pallas kernels  26.2 us (44%)
    ppermute x12, starting transfers between devices, swapped(): return lax.ppermute(x, 'ctx', [(i, i ^ k) for i in range(length)])  17.5 us
    ppermute x3, starting transfers between devices, shifted(): return lax.ppermute(x, 'ctx', [(i, i + by) for i in range(length - by)])  14.2 us
    pallas_call x1, Pallas kernels, first_states(): pl.pallas_call(lambda *refs: first_kernel(*refs, head_width=head_width),...  6.11 us
    pallas_call x1, Pallas kernels, later_states(): pl.pallas_call(lambda *refs: later_kernel(*refs, head_width=head_width, f...  5.49 us
    pallas_call x2, Pallas kernels, local_parts(): pl.pallas_call(lambda *refs: local_kernel(*refs, head_width=head_width, f...  5.29 us
    pallas_call x1, Pallas kernels, finish(): pl.pallas_call(lambda *refs: finish_kernel(*refs, head_width=head_width),...  3.51 us
    pallas_call x1, Pallas kernels, finish_first(): pl.pallas_call(lambda *refs: finish_first_kernel(*refs, head_width=head_w...  2.68 us
    pallas_call x1, Pallas kernels, decays(): pl.pallas_call(decay_kernel, in_specs=[vmem()] * 3 + [anywhere()], out_sp...  1.71 us
  transfers between devices with their start and end apart: 15, of which 0 were waited for; matrix products, arithmetic and copies ran while one was open for 1% of the time, Pallas kernels for 27%

profile of v4, /device:TPU:0, one launch (start us, length us, event | category | flops | bytes accessed | tf_op | source)
XLA Modules:
  0.0 58.7 jit_solution(5970359640245483184)
XLA Ops:
  0.0 1.0 %edges.1 = bf16[16,4352]{1,0:T(8,128)(2,1)S(1)} custom-call(bf16[768,4096]{1,0:T(8,128)(2,1)} %refs_1_.3, bf16[768,256]{1,0:T(8,128)(2,1)} %refs_3_.1), custom_call_target="tpu_custom_call" | custom-call | tf_op jit(solution)/shard_map/edges/pallas_call | solution.py:87
  1.0 4.9 %collective-permute-start = (bf16[3,4352]{1,0:T(4,128)(2,1)S(1)}, bf16[3,4352]{1,0:T(4,128)(2,1)S(1)}, u32[]{:S(2)}, u32[]{:S(2)}) collective-permute-start(bf16[3,4352]{1,0:T(4,128)(2,1)S(1)} %slice.68), channel_id=1, source_target_pairs={{0,4},{4,8},{8,12},{12,16},{16,20},{20,24},{24,28},{1,5},{5,9},{9,... | collective-permute-start | bytes 78344 | tf_op jit(solution)/shard_map/ppermute | solution.py:439
  5.9 0.0 copy-done.6
  5.9 0.1 broadcast_in_dim.14
  6.0 0.0 copy-done.2
  6.0 0.0 copy-start.1
  6.0 0.0 copy-start.5
  6.0 1.7 %decays.1 = (f32[768,128]{1,0:T(8,128)S(1)}, f32[768,128]{1,0:T(8,128)S(1)}, f32[768,128]{1,0:T(8,128)S(1)}, f32[16,128]{1,0:T(8,128)S(1)}, bf16[128,2048]{1,0:T(8,128)(2,1)S(1)}) custom-call(f32[64,768]{1,0:T(8,128)S(1)} %bitcast.28, f32[64,768]{1,0:T(8,128)S(1)} %bitcast.29, f32[8,128]{1,0:T(8,128)S(1)} %broadcast_in_dim.15.skip_ref, bf16[768,4096]{1,0:T(8,128)(2,1)} %refs_1_.3), custom_call_target="tpu_custom_call" | custom-call | tf_op jit(solution)/shard_map/decays/pallas_call | solution.py:138
  7.7 0.0 collective-permute-done.refs_4_.refs_3_
  7.8 6.1 %first_states.1 = (bf16[768,2048]{1,0:T(8,128)(2,1)S(1)}, bf16[768,2048]{1,0:T(8,128)(2,1)S(1)}, bf16[768,2048]{1,0:T(8,128)(2,1)S(1)}, bf16[768,256]{1,0:T(8,12...) custom-call(s32[1]{0:T(128)} %bitcast.refs_0_.place_ref, ...), custom_call_target="tpu_custom_call" | custom-call | tf_op jit(solution)/shard_map/first_states/pallas_call | solution.py:242
  13.9 3.1 %collective-permute-start.10 = (bf16[144,512]{1,0:T(8,128)(2,1)S(1)}, bf16[144,512]{1,0:T(8,128)(2,1)S(1)}, u32[]{:S(2)}, u32[]{:S(2)}) collective-permute-start(bf16[144,512]{1,0:T(8,128)(2,1)S(1)} %get-tuple-element.56), channel_id=1, source_target_pairs={{0,12},{4,8},{8,4},{12,0},{16,28},{20,24},{24,20},{28,16},{1,13},{... | collective-permute-start | bytes 442376 | tf_op jit(solution)/shard_map/ppermute | solution.py:444
  17.0 1.4 %collective-permute-start.8 = (bf16[144,512]{1,0:T(8,128)(2,1)S(1)}, bf16[144,512]{1,0:T(8,128)(2,1)S(1)}, u32[]{:S(2)}, u32[]{:S(2)}) collective-permute-start(bf16[144,512]{1,0:T(8,128)(2,1)S(1)} %get-tuple-element.54), channel_id=1, source_target_pairs={{0,4},{4,0},{8,12},{12,8},{16,20},{20,16},{24,28},{28,24},{1,5},{5... | collective-permute-start | bytes 442376 | tf_op jit(solution)/shard_map/ppermute | solution.py:444
  18.4 0.0 collective-permute-start.9
  18.4 5.5 %later_states.1 = (bf16[768,2048]{1,0:T(8,128)(2,1)S(1)}, bf16[768,2048]{1,0:T(8,128)(2,1)S(1)}, bf16[768,2048]{1,0:T(8,128)(2,1)S(1)}, bf16[144,512]{1,0:T(8,12...) custom-call(s32[1]{0:T(128)} %bitcast.refs_0_.place_ref, ...), custom_call_target="tpu_custom_call" | custom-call | tf_op jit(solution)/shard_map/later_states/pallas_call | solution.py:283
  23.9 1.1 %collective-permute-start.1 = (bf16[144,512]{1,0:T(8,128)(2,1)S(1)}, bf16[144,512]{1,0:T(8,128)(2,1)S(1)}, u32[]{:S(2)}, u32[]{:S(2)}) collective-permute-start(bf16[144,512]{1,0:T(8,128)(2,1)S(1)} %get-tuple-element.47), channel_id=1, source_target_pairs={{0,4},{4,0},{8,12},{12,8},{16,20},{20,16},{24,28},{28,24},{1,5},{5... | collective-permute-start | bytes 442376 | tf_op jit(solution)/shard_map/ppermute | solution.py:444
  25.0 1.6 %collective-permute-start.2 = (bf16[144,512]{1,0:T(8,128)(2,1)S(1)}, bf16[144,512]{1,0:T(8,128)(2,1)S(1)}, u32[]{:S(2)}, u32[]{:S(2)}) collective-permute-start(bf16[144,512]{1,0:T(8,128)(2,1)S(1)} %get-tuple-element.48), channel_id=1, source_target_pairs={{0,8},{4,12},{8,0},{12,4},{16,24},{20,28},{24,16},{28,20},{1,9},{5... | collective-permute-start | bytes 442376 | tf_op jit(solution)/shard_map/ppermute | solution.py:444
  26.6 2.6 %local.3.refs_1_ = f32[768,2048]{1,0:T(8,128)S(1)} custom-call(bf16[768,2048]{1,0:T(8,128)(2,1)S(1)} %get-tuple-element.58.refs_0_, bf16[768,2048]{1,0:T(8,128)(2,1)S(1)} %get-tuple-element.59.refs_1_, bf16[768,2048]{1,0:T(8,128)(2,1)S(1)} %get-tuple-element.60.refs_2_, f32[768,128]{1,0:T(8,128)S(1)} %get-tuple-element.43.refs_3_, ...), custom_call_target="tpu_custom_call" | custom-call | tf_op jit(solution)/shard_map/local/pallas_call | solution.py:359
  29.3 0.0 collective-permute-done.10.refs_3_
  29.3 0.9 %collective-permute-start.3 = (bf16[144,512]{1,0:T(8,128)(2,1)S(1)}, bf16[144,512]{1,0:T(8,128)(2,1)S(1)}, u32[]{:S(2)}, u32[]{:S(2)}) collective-permute-start(bf16[144,512]{1,0:T(8,128)(2,1)S(1)} %get-tuple-element.49), channel_id=1, source_target_pairs={{0,12},{4,8},{8,4},{12,0},{16,28},{20,24},{24,20},{28,16},{1,13},{... | collective-permute-start | bytes 442376 | tf_op jit(solution)/shard_map/ppermute | solution.py:444
  30.2 0.0 collective-permute-done.8.refs_1_
  30.2 0.0 collective-permute-done.9.refs_2_
  30.2 0.2 combine.3
  30.5 4.9 %collective-permute-start.11 = (bf16[128,512]{1,0:T(8,128)(2,1)S(1)}, bf16[128,512]{1,0:T(8,128)(2,1)S(1)}, u32[]{:S(2)}, u32[]{:S(2)}) collective-permute-start(bf16[128,512]{1,0:T(8,128)(2,1)S(1)} %get-tuple-element.57), channel_id=1, source_target_pairs={{0,16},{4,20},{8,24},{12,28},{1,17},{5,21},{9,25},{13,29},{2,18},{... | collective-permute-start | bytes 393224 | tf_op jit(solution)/shard_map/ppermute | solution.py:439
  35.4 0.0 collective-permute-done.1.refs_1_
  35.4 0.0 collective-permute-done.2.refs_2_
  35.4 0.0 collective-permute-done.3.refs_3_
  35.5 0.2 combine.2
  35.7 4.4 %collective-permute-start.4 = (bf16[128,512]{1,0:T(8,128)(2,1)S(1)}, bf16[128,512]{1,0:T(8,128)(2,1)S(1)}, u32[]{:S(2)}, u32[]{:S(2)}) collective-permute-start(bf16[128,512]{1,0:T(8,128)(2,1)S(1)} %get-tuple-element.52), channel_id=1, source_target_pairs={{0,16},{4,20},{8,24},{12,28},{1,17},{5,21},{9,25},{13,29},{2,18},{... | collective-permute-start | bytes 393224 | tf_op jit(solution)/shard_map/ppermute | solution.py:439
  40.1 0.0 collective-permute-done.11
  40.1 0.2 fusion.15
  40.3 1.5 %collective-permute-start.12 = (bf16[128,512]{1,0:T(8,128)(2,1)S(1)}, bf16[128,512]{1,0:T(8,128)(2,1)S(1)}, u32[]{:S(2)}, u32[]{:S(2)}) collective-permute-start(bf16[128,512]{1,0:T(8,128)(2,1)S(1)} %get-tuple-element.66), channel_id=1, source_target_pairs={{0,4},{4,0},{8,12},{12,8},{16,20},{20,16},{24,28},{28,24},{1,5},{5... | collective-permute-start | bytes 393224 | tf_op jit(solution)/shard_map/ppermute | solution.py:444
  41.8 2.5 %collective-permute-start.13 = (bf16[128,512]{1,0:T(8,128)(2,1)S(1)}, bf16[128,512]{1,0:T(8,128)(2,1)S(1)}, u32[]{:S(2)}, u32[]{:S(2)}) collective-permute-start(bf16[128,512]{1,0:T(8,128)(2,1)S(1)} %get-tuple-element.67), channel_id=1, source_target_pairs={{0,8},{4,12},{8,0},{12,4},{16,24},{20,28},{24,16},{28,20},{1,9},{5... | collective-permute-start | bytes 393224 | tf_op jit(solution)/shard_map/ppermute | solution.py:444
  44.3 1.2 %collective-permute-start.14 = (bf16[128,512]{1,0:T(8,128)(2,1)S(1)}, bf16[128,512]{1,0:T(8,128)(2,1)S(1)}, u32[]{:S(2)}, u32[]{:S(2)}) collective-permute-start(bf16[128,512]{1,0:T(8,128)(2,1)S(1)} %get-tuple-element.65), channel_id=1, source_target_pairs={{0,12},{4,8},{8,4},{12,0},{16,28},{20,24},{24,20},{28,16},{1,13},{... | collective-permute-start | bytes 393224 | tf_op jit(solution)/shard_map/ppermute | solution.py:444
  45.6 0.0 collective-permute-done.4
  45.6 0.2 fusion.7
  45.7 0.6 %collective-permute-start.5 = (bf16[128,512]{1,0:T(8,128)(2,1)S(1)}, bf16[128,512]{1,0:T(8,128)(2,1)S(1)}, u32[]{:S(2)}, u32[]{:S(2)}) collective-permute-start(bf16[128,512]{1,0:T(8,128)(2,1)S(1)} %get-tuple-element.70), channel_id=1, source_target_pairs={{0,4},{4,0},{8,12},{12,8},{16,20},{20,16},{24,28},{28,24},{1,5},{5... | collective-permute-start | bytes 393224 | tf_op jit(solution)/shard_map/ppermute | solution.py:444
  46.3 1.7 %collective-permute-start.6 = (bf16[128,512]{1,0:T(8,128)(2,1)S(1)}, bf16[128,512]{1,0:T(8,128)(2,1)S(1)}, u32[]{:S(2)}, u32[]{:S(2)}) collective-permute-start(bf16[128,512]{1,0:T(8,128)(2,1)S(1)} %get-tuple-element.71), channel_id=1, source_target_pairs={{0,8},{4,12},{8,0},{12,4},{16,24},{20,28},{24,16},{28,20},{1,9},{5... | collective-permute-start | bytes 393224 | tf_op jit(solution)/shard_map/ppermute | solution.py:444
  48.0 0.0 collective-permute-done.12.refs_6_
  48.1 1.7 %collective-permute-start.7 = (bf16[128,512]{1,0:T(8,128)(2,1)S(1)}, bf16[128,512]{1,0:T(8,128)(2,1)S(1)}, u32[]{:S(2)}, u32[]{:S(2)}) collective-permute-start(bf16[128,512]{1,0:T(8,128)(2,1)S(1)} %get-tuple-element.69), channel_id=1, source_target_pairs={{0,12},{4,8},{8,4},{12,0},{16,28},{20,24},{24,20},{28,16},{1,13},{... | collective-permute-start | bytes 393224 | tf_op jit(solution)/shard_map/ppermute | solution.py:444
  49.8 2.6 %local.2.refs_1_ = f32[768,2048]{1,0:T(8,128)S(1)} custom-call(bf16[768,2048]{1,0:T(8,128)(2,1)S(1)} %get-tuple-element.40.refs_0_, bf16[768,2048]{1,0:T(8,128)(2,1)S(1)} %get-tuple-element.41.refs_1_, bf16[768,2048]{1,0:T(8,128)(2,1)S(1)} %get-tuple-element.42.refs_2_, f32[768,128]{1,0:T(8,128)S(1)} %get-tuple-element.43.refs_3_, ...), custom_call_target="tpu_custom_call" | custom-call | tf_op jit(solution)/shard_map/local/pallas_call | solution.py:359
  52.5 0.0 collective-permute-done.13.refs_7_
  52.5 0.0 collective-permute-done.14.refs_8_
  52.5 0.0 copy-done.4
  52.5 2.7 %finish_first.1.refs_9_ = bf16[768,2048]{1,0:T(8,128)(2,1)S(1)} custom-call(s32[1]{0:T(128)} %bitcast.refs_0_.place_ref, f32[768,2048]{1,0:T(8,128)S(1)} %local.3.refs_1_, f32[768,128]{1,0:T(8,128)S(1)} %get-tuple-element.45.refs_2_, bf16[768,256]{1,0:T(8,128)(2,1)S(1)} %get-tuple-element.44.refs_5_.refs_3_, f32[1,4096]{1,0:T(1,128)S(1)} %bitcast.30, ...), custom_call_target="tpu_custom_call" | custom-call | tf_op jit(solution)/shard_map/finish_first/pallas_call | solution.py:396
  55.2 0.0 collective-permute-done.5.refs_6_
  55.2 0.0 collective-permute-done.6.refs_7_
  55.2 0.0 collective-permute-done.7.refs_8_
  55.2 3.5 %finish.1 = bf16[768,4096]{1,0:T(8,128)(2,1)} custom-call(s32[1]{0:T(128)} %bitcast.refs_0_.place_ref, f32[768,2048]{1,0:T(8,128)S(1)} %local.2.refs_1_, f32[768,128]{1,0:T(8,128)S(1)} %get-tuple-element.45.refs_2_, bf16[768,256]{1,0:T(8,128)(2,1)S(1)} %get-tuple-element.44.refs_5_.refs_3_, f32[1,4096]{1,0:T(1,128)S(1)} %bitcast.31, ...), custom_call_target="tpu_custom_call" | custom-call | tf_op jit(solution)/shard_map/finish/pallas_call | solution.py:426
  (14 shorter events, 0.1 us)
Async XLA Ops:
  0.0 5.9 %copy-start.6 = (f32[64]{0:T(128)S(1)}, f32[64]{0:T(128)}, u32[]{:S(2)}) copy-start(f32[64]{0:T(128)} %param.14) | copy-start | bytes 772
  0.0 6.0 %copy-start.2 = (f32[768,64]{0,1:T(8,128)S(1)}, f32[768,64]{0,1:T(8,128)}, u32[]{:S(2)}) copy-start(f32[768,64]{0,1:T(8,128)} %param.11) | copy-start | bytes 589828
  0.0 6.0 %copy-start.3 = (f32[768,64]{0,1:T(8,128)S(1)}, f32[768,64]{0,1:T(8,128)}, u32[]{:S(2)}) copy-start(f32[768,64]{0,1:T(8,128)} %param.10) | copy-start | bytes 589828
  1.0 6.7 %collective-permute-start = (bf16[3,4352]{1,0:T(4,128)(2,1)S(1)}, bf16[3,4352]{1,0:T(4,128)(2,1)S(1)}, u32[]{:S(2)}, u32[]{:S(2)}) collective-permute-start(bf16[3,4352]{1,0:T(4,128)(2,1)S(1)} %slice.68), channel_id=1, source_target_pairs={{0,4},{4,8},{8,12},{12,16},{16,20},{20,24},{24,28},{1,5},{5,9},{9,... | collective-permute-start | bytes 78344 | tf_op jit(solution)/shard_map/ppermute | solution.py:439
  6.0 1.8 %copy-start = (bf16[768,256]{1,0:T(8,128)(2,1)S(1)}, bf16[768,256]{1,0:T(8,128)(2,1)}, u32[]{:S(2)}) copy-start(bf16[768,256]{1,0:T(8,128)(2,1)} %refs_3_.1) | copy-start | bytes 1179652
  6.0 1.8 %copy-start.1 = (f32[4,4096]{1,0:T(4,128)S(1)}, f32[4,4096]{1,0:T(4,128)}, u32[]{:S(2)}) copy-start(f32[4,4096]{1,0:T(4,128)} %refs_4_.1) | copy-start | bytes 196612
  6.0 1.8 %copy-start.5 = (f32[4,256]{1,0:T(4,128)S(1)}, f32[4,256]{1,0:T(4,128)}, u32[]{:S(2)}) copy-start(f32[4,256]{1,0:T(4,128)} %refs_6_.1) | copy-start | bytes 12292
  13.9 15.4 %collective-permute-start.10 = (bf16[144,512]{1,0:T(8,128)(2,1)S(1)}, bf16[144,512]{1,0:T(8,128)(2,1)S(1)}, u32[]{:S(2)}, u32[]{:S(2)}) collective-permute-start(bf16[144,512]{1,0:T(8,128)(2,1)S(1)} %get-tuple-element.56), channel_id=1, source_target_pairs={{0,12},{4,8},{8,4},{12,0},{16,28},{20,24},{24,20},{28,16},{1,13},{... | collective-permute-start | bytes 442376 | tf_op jit(solution)/shard_map/ppermute | solution.py:444
  17.0 13.2 %collective-permute-start.8 = (bf16[144,512]{1,0:T(8,128)(2,1)S(1)}, bf16[144,512]{1,0:T(8,128)(2,1)S(1)}, u32[]{:S(2)}, u32[]{:S(2)}) collective-permute-start(bf16[144,512]{1,0:T(8,128)(2,1)S(1)} %get-tuple-element.54), channel_id=1, source_target_pairs={{0,4},{4,0},{8,12},{12,8},{16,20},{20,16},{24,28},{28,24},{1,5},{5... | collective-permute-start | bytes 442376 | tf_op jit(solution)/shard_map/ppermute | solution.py:444
  18.4 11.8 %collective-permute-start.9 = (bf16[144,512]{1,0:T(8,128)(2,1)S(1)}, bf16[144,512]{1,0:T(8,128)(2,1)S(1)}, u32[]{:S(2)}, u32[]{:S(2)}) collective-permute-start(bf16[144,512]{1,0:T(8,128)(2,1)S(1)} %get-tuple-element.55), channel_id=1, source_target_pairs={{0,8},{4,12},{8,0},{12,4},{16,24},{20,28},{24,16},{28,20},{1,9},{5... | collective-permute-start | bytes 442376 | tf_op jit(solution)/shard_map/ppermute | solution.py:444
  23.9 11.5 %collective-permute-start.1 = (bf16[144,512]{1,0:T(8,128)(2,1)S(1)}, bf16[144,512]{1,0:T(8,128)(2,1)S(1)}, u32[]{:S(2)}, u32[]{:S(2)}) collective-permute-start(bf16[144,512]{1,0:T(8,128)(2,1)S(1)} %get-tuple-element.47), channel_id=1, source_target_pairs={{0,4},{4,0},{8,12},{12,8},{16,20},{20,16},{24,28},{28,24},{1,5},{5... | collective-permute-start | bytes 442376 | tf_op jit(solution)/shard_map/ppermute | solution.py:444
  25.0 10.4 %collective-permute-start.2 = (bf16[144,512]{1,0:T(8,128)(2,1)S(1)}, bf16[144,512]{1,0:T(8,128)(2,1)S(1)}, u32[]{:S(2)}, u32[]{:S(2)}) collective-permute-start(bf16[144,512]{1,0:T(8,128)(2,1)S(1)} %get-tuple-element.48), channel_id=1, source_target_pairs={{0,8},{4,12},{8,0},{12,4},{16,24},{20,28},{24,16},{28,20},{1,9},{5... | collective-permute-start | bytes 442376 | tf_op jit(solution)/shard_map/ppermute | solution.py:444
  29.3 6.2 %collective-permute-start.3 = (bf16[144,512]{1,0:T(8,128)(2,1)S(1)}, bf16[144,512]{1,0:T(8,128)(2,1)S(1)}, u32[]{:S(2)}, u32[]{:S(2)}) collective-permute-start(bf16[144,512]{1,0:T(8,128)(2,1)S(1)} %get-tuple-element.49), channel_id=1, source_target_pairs={{0,12},{4,8},{8,4},{12,0},{16,28},{20,24},{24,20},{28,16},{1,13},{... | collective-permute-start | bytes 442376 | tf_op jit(solution)/shard_map/ppermute | solution.py:444
  30.5 9.7 %collective-permute-start.11 = (bf16[128,512]{1,0:T(8,128)(2,1)S(1)}, bf16[128,512]{1,0:T(8,128)(2,1)S(1)}, u32[]{:S(2)}, u32[]{:S(2)}) collective-permute-start(bf16[128,512]{1,0:T(8,128)(2,1)S(1)} %get-tuple-element.57), channel_id=1, source_target_pairs={{0,16},{4,20},{8,24},{12,28},{1,17},{5,21},{9,25},{13,29},{2,18},{... | collective-permute-start | bytes 393224 | tf_op jit(solution)/shard_map/ppermute | solution.py:439
  35.7 9.8 %collective-permute-start.4 = (bf16[128,512]{1,0:T(8,128)(2,1)S(1)}, bf16[128,512]{1,0:T(8,128)(2,1)S(1)}, u32[]{:S(2)}, u32[]{:S(2)}) collective-permute-start(bf16[128,512]{1,0:T(8,128)(2,1)S(1)} %get-tuple-element.52), channel_id=1, source_target_pairs={{0,16},{4,20},{8,24},{12,28},{1,17},{5,21},{9,25},{13,29},{2,18},{... | collective-permute-start | bytes 393224 | tf_op jit(solution)/shard_map/ppermute | solution.py:439
  40.3 7.7 %collective-permute-start.12 = (bf16[128,512]{1,0:T(8,128)(2,1)S(1)}, bf16[128,512]{1,0:T(8,128)(2,1)S(1)}, u32[]{:S(2)}, u32[]{:S(2)}) collective-permute-start(bf16[128,512]{1,0:T(8,128)(2,1)S(1)} %get-tuple-element.66), channel_id=1, source_target_pairs={{0,4},{4,0},{8,12},{12,8},{16,20},{20,16},{24,28},{28,24},{1,5},{5... | collective-permute-start | bytes 393224 | tf_op jit(solution)/shard_map/ppermute | solution.py:444
  41.8 10.6 %collective-permute-start.13 = (bf16[128,512]{1,0:T(8,128)(2,1)S(1)}, bf16[128,512]{1,0:T(8,128)(2,1)S(1)}, u32[]{:S(2)}, u32[]{:S(2)}) collective-permute-start(bf16[128,512]{1,0:T(8,128)(2,1)S(1)} %get-tuple-element.67), channel_id=1, source_target_pairs={{0,8},{4,12},{8,0},{12,4},{16,24},{20,28},{24,16},{28,20},{1,9},{5... | collective-permute-start | bytes 393224 | tf_op jit(solution)/shard_map/ppermute | solution.py:444
  44.3 8.1 %collective-permute-start.14 = (bf16[128,512]{1,0:T(8,128)(2,1)S(1)}, bf16[128,512]{1,0:T(8,128)(2,1)S(1)}, u32[]{:S(2)}, u32[]{:S(2)}) collective-permute-start(bf16[128,512]{1,0:T(8,128)(2,1)S(1)} %get-tuple-element.65), channel_id=1, source_target_pairs={{0,12},{4,8},{8,4},{12,0},{16,28},{20,24},{24,20},{28,16},{1,13},{... | collective-permute-start | bytes 393224 | tf_op jit(solution)/shard_map/ppermute | solution.py:444
  45.7 9.5 %collective-permute-start.5 = (bf16[128,512]{1,0:T(8,128)(2,1)S(1)}, bf16[128,512]{1,0:T(8,128)(2,1)S(1)}, u32[]{:S(2)}, u32[]{:S(2)}) collective-permute-start(bf16[128,512]{1,0:T(8,128)(2,1)S(1)} %get-tuple-element.70), channel_id=1, source_target_pairs={{0,4},{4,0},{8,12},{12,8},{16,20},{20,16},{24,28},{28,24},{1,5},{5... | collective-permute-start | bytes 393224 | tf_op jit(solution)/shard_map/ppermute | solution.py:444
  46.3 8.8 %collective-permute-start.6 = (bf16[128,512]{1,0:T(8,128)(2,1)S(1)}, bf16[128,512]{1,0:T(8,128)(2,1)S(1)}, u32[]{:S(2)}, u32[]{:S(2)}) collective-permute-start(bf16[128,512]{1,0:T(8,128)(2,1)S(1)} %get-tuple-element.71), channel_id=1, source_target_pairs={{0,8},{4,12},{8,0},{12,4},{16,24},{20,28},{24,16},{28,20},{1,9},{5... | collective-permute-start | bytes 393224 | tf_op jit(solution)/shard_map/ppermute | solution.py:444
  48.1 7.1 %collective-permute-start.7 = (bf16[128,512]{1,0:T(8,128)(2,1)S(1)}, bf16[128,512]{1,0:T(8,128)(2,1)S(1)}, u32[]{:S(2)}, u32[]{:S(2)}) collective-permute-start(bf16[128,512]{1,0:T(8,128)(2,1)S(1)} %get-tuple-element.69), channel_id=1, source_target_pairs={{0,12},{4,8},{8,4},{12,0},{16,28},{20,24},{24,20},{28,16},{1,13},{... | collective-permute-start | bytes 393224 | tf_op jit(solution)/shard_map/ppermute | solution.py:444
  49.8 2.7 %copy-start.4 = (f32[4096]{0:T(1024)S(1)}, f32[4096]{0:T(1024)}, u32[]{:S(2)}) copy-start(f32[4096]{0:T(1024)} %param.15) | copy-start | bytes 49156

commit v5 on v4

--- a/solution.py
+++ b/solution.py
@@ -15,7 +15,7 @@
 BF16 = jnp.bfloat16
 
 
-def params(mib=16):
+def params(mib=9):
     return pltpu.CompilerParams(vmem_limit_bytes=mib * 1024 * 1024)
 
 
@@ -191,7 +191,7 @@
                 xs.append(silu_conv(lambda k: window_ref[block, pl.ds(EDGE - k, CHUNK), :], taps))
             x = jnp.concatenate(xs, axis=1)
             x_ref[at, at_cols] = x.astype(BF16)
-            scaled = (over_heads(inv_ref[at, :], head_width, here, SUB) * x).astype(BF16)
+            scaled = over_heads(inv_ref[at, :], head_width, here, SUB).astype(BF16) * x.astype(BF16)
             scaled_ref[at, at_cols] = scaled
             running = sum_ref[:, at_cols]
             opening_ref[at, at_cols] = running.astype(BF16)
@@ -201,7 +201,7 @@
     lax.fori_loop(0, chunks, chunk_step, 0)
     row = iota((EDGE, cols), 0)
     for k, slot in enumerate(slots):
-        start = pl.multiple_of((k ^ place_ref[0]) * cols, cols)
+        start = pl.multiple_of((k ^ lax.rem(place_ref[0], SQUARE)) * cols, cols)
         slot[:state, :] = sum_ref[:, pl.ds(start, cols)].astype(BF16)
         decay = row_ref[8:16, pl.ds(start, cols)][:1]
         high = decay.astype(BF16).astype(F32)
@@ -300,14 +300,15 @@
 def combine_kernel(place_ref, *refs):
     slots, (leaving_ref, prefix_ref, opening_ref, placed_ref) = refs[:SQUARE], refs[SQUARE:]
     state, cols = leaving_ref.shape
-    spot = place_ref[0]
+    spot = lax.rem(place_ref[0], SQUARE)
     for k in range(SQUARE):
         placed_ref[spot ^ k] = slots[k][...]
     running = jnp.zeros((state, cols), F32)
     opening = jnp.ones((1, cols), F32)
+    begun = jnp.where(place_ref[0] < SQUARE, 0.0, 1.0)
     for p in range(SQUARE):
         prefix_ref[spot ^ p] = running
-        opening_ref[spot ^ p] = jnp.broadcast_to(opening, (8, cols))
+        opening_ref[spot ^ p] = jnp.broadcast_to(begun * opening, (8, cols))
         tail = placed_ref[p, state:, :].astype(F32)
         decay = tail[0:1] + tail[1:2]
         running = decay * running + placed_ref[p, :state, :].astype(F32)
@@ -371,7 +372,7 @@
     cols = wide // SQUARE
     mean = jnp.where(iota((SUB, SUB), 0) // head_width == iota((SUB, SUB), 1) // head_width, 1.0 / head_width, 0.0).astype(BF16)
     for k in range(SQUARE):
-        base = pl.multiple_of((k ^ place_ref[0]) * cols, cols)
+        base = pl.multiple_of((k ^ lax.rem(place_ref[0], SQUARE)) * cols, cols)
         for sub in range(cols // SUB):
             at_cols = pl.ds(base + sub * SUB, SUB)
             here = first + base + sub * SUB
@@ -445,10 +446,12 @@
 
 
 def previous_squares(leaving, decay):
-    squares = lax.axis_size("ctx") // SQUARE
-    entering = shifted(leaving, SQUARE)
+    length = lax.axis_size("ctx")
+    squares = length // SQUARE
+    entering = lax.ppermute(leaving, "ctx", [(i, (i + SQUARE) % length) for i in range(length)])
     span = 1
     if squares > 2:
+        entering = jnp.where(lax.axis_index("ctx") < SQUARE, jnp.zeros_like(entering), entering)
         window = shifted(decay, SQUARE)
     while span < squares - 1:
         behind = shifted(entering, SQUARE * span)
@@ -464,7 +467,7 @@
     head_width = width // heads
     past = conv_inner.shape[0] - 1
     kept, kept_proj = [pltpu.with_memory_space_constraint(a, pltpu.HBM) for a in (inner_input, state_proj)]
-    place = jnp.full((1,), lax.axis_index("ctx") % SQUARE, jnp.int32)
+    place = jnp.full((1,), lax.axis_index("ctx"), jnp.int32)
     edge = shifted(last_rows(kept, kept_proj)[EDGE - past :], 1)
     fwd, inv, dev, fac, head = decays(decay_log, step_size, skip_weight, kept)
     gain = norm_gain[None]

time: 58.9 us -> 57.6 us (0.978)
  starting transfers between devices: 31.7 us -> 27.2 us
  waiting for transfers between devices: 0.04 us -> 3.42 us
    ppermute x3 -> x1, starting transfers between devices: 14.2 us -> 4.85 us  [shifted(): return lax.ppermute(x, 'ctx', [(i, i + by) for i in range(length - by)])]
    ppermute x0 -> x2, starting transfers between devices: none -> 6.15 us  [previous_squares(): lax.ppermute(leaving, 'ctx', [(i, (i + SQUARE) % length) for i in range(l...]
    ppermute x12, waiting for transfers between devices: 0.03 us -> 2.38 us  [swapped(): return lax.ppermute(x, 'ctx', [(i, i ^ k) for i in range(length)])]
    ppermute x12, starting transfers between devices: 17.5 us -> 16.2 us  [swapped(): return lax.ppermute(x, 'ctx', [(i, i ^ k) for i in range(length)])]
    ppermute x0 -> x2, waiting for transfers between devices: none -> 1.03 us  [previous_squares(): lax.ppermute(leaving, 'ctx', [(i, (i + SQUARE) % length) for i in range(l...]
  transfers between devices with their start and end apart: 15 -> 15, of which waited for: 0 -> 3; matrix products, arithmetic and copies ran while one was open for 1% -> 1% of each run, Pallas kernels for 27% -> 27%
where the time goes in v5:
time: 57.6 us; the launch traced here: 57.4 us
  starting transfers between devices  27.2 us (47%)
  Pallas kernels  26.1 us (45%)
  waiting for transfers between devices  3.42 us (6%)
    ppermute x12, starting transfers between devices, swapped(): return lax.ppermute(x, 'ctx', [(i, i ^ k) for i in range(length)])  16.2 us
    ppermute x2, starting transfers between devices, previous_squares(): lax.ppermute(leaving, 'ctx', [(i, (i + SQUARE) % length) for i in range(l...  6.15 us
    pallas_call x1, Pallas kernels, first_states(): pl.pallas_call(lambda *refs: first_kernel(*refs, head_width=head_width),...  5.99 us
    pallas_call x1, Pallas kernels, later_states(): pl.pallas_call(lambda *refs: later_kernel(*refs, head_width=head_width, f...  5.42 us
    pallas_call x2, Pallas kernels, local_parts(): pl.pallas_call(lambda *refs: local_kernel(*refs, head_width=head_width, f...  5.29 us
    ppermute x1, starting transfers between devices, shifted(): return lax.ppermute(x, 'ctx', [(i, i + by) for i in range(length - by)])  4.85 us
    pallas_call x1, Pallas kernels, finish(): pl.pallas_call(lambda *refs: finish_kernel(*refs, head_width=head_width),...  3.49 us
    pallas_call x1, Pallas kernels, finish_first(): pl.pallas_call(lambda *refs: finish_first_kernel(*refs, head_width=head_w...  2.69 us
  transfers between devices with their start and end apart: 15, of which 3 were waited for; matrix products, arithmetic and copies ran while one was open for 1% of the time, Pallas kernels for 27%

profile of v5, /device:TPU:0, one launch (start us, length us, event | category | flops | bytes accessed | tf_op | source)
XLA Modules:
  0.0 57.4 jit_solution(14458214030458831801)
XLA Ops:
  0.0 1.0 %edges.1 = bf16[16,4352]{1,0:T(8,128)(2,1)S(1)} custom-call(bf16[768,4096]{1,0:T(8,128)(2,1)} %refs_1_.3, bf16[768,256]{1,0:T(8,128)(2,1)} %refs_3_.1), custom_call_target="tpu_custom_call" | custom-call | tf_op jit(solution)/shard_map/edges/pallas_call | solution.py:87
  1.0 4.9 %collective-permute-start = (bf16[3,4352]{1,0:T(4,128)(2,1)S(1)}, bf16[3,4352]{1,0:T(4,128)(2,1)S(1)}, u32[]{:S(2)}, u32[]{:S(2)}) collective-permute-start(bf16[3,4352]{1,0:T(4,128)(2,1)S(1)} %slice.68), channel_id=1, source_target_pairs={{0,4},{4,8},{8,12},{12,16},{16,20},{20,24},{24,28},{1,5},{5,9},{9,... | collective-permute-start | bytes 78344 | tf_op jit(solution)/shard_map/ppermute | solution.py:440
  5.9 0.1 broadcast_in_dim.14
  6.0 0.0 copy-start.1
  6.0 0.0 copy-start.5
  6.0 1.7 %decays.1 = (f32[768,128]{1,0:T(8,128)S(1)}, f32[768,128]{1,0:T(8,128)S(1)}, f32[768,128]{1,0:T(8,128)S(1)}, f32[16,128]{1,0:T(8,128)S(1)}, bf16[128,2048]{1,0:T(8,128)(2,1)S(1)}) custom-call(f32[64,768]{1,0:T(8,128)S(1)} %bitcast.28, f32[64,768]{1,0:T(8,128)S(1)} %bitcast.29, f32[8,128]{1,0:T(8,128)S(1)} %broadcast_in_dim.15.skip_ref, bf16[768,4096]{1,0:T(8,128)(2,1)} %refs_1_.3), custom_call_target="tpu_custom_call" | custom-call | tf_op jit(solution)/shard_map/decays/pallas_call | solution.py:138
  7.7 0.0 collective-permute-done.refs_4_.refs_3_
  7.8 0.0 copy-done
  7.8 0.0 copy-done.1
  7.8 0.0 copy-done.5
  7.8 6.0 %first_states.1 = (bf16[768,2048]{1,0:T(8,128)(2,1)S(1)}, bf16[768,2048]{1,0:T(8,128)(2,1)S(1)}, bf16[768,2048]{1,0:T(8,128)(2,1)S(1)}, bf16[768,256]{1,0:T(8,12...) custom-call(s32[1]{0:T(128)} %bitcast.refs_0_.place_ref, ...), custom_call_target="tpu_custom_call" | custom-call | tf_op jit(solution)/shard_map/first_states/pallas_call | solution.py:242
  13.8 3.1 %collective-permute-start.10 = (bf16[144,512]{1,0:T(8,128)(2,1)S(1)}, bf16[144,512]{1,0:T(8,128)(2,1)S(1)}, u32[]{:S(2)}, u32[]{:S(2)}) collective-permute-start(bf16[144,512]{1,0:T(8,128)(2,1)S(1)} %get-tuple-element.56), channel_id=1, source_target_pairs={{0,12},{4,8},{8,4},{12,0},{16,28},{20,24},{24,20},{28,16},{1,13},{... | collective-permute-start | bytes 442376 | tf_op jit(solution)/shard_map/ppermute | solution.py:445
  16.9 1.4 %collective-permute-start.8 = (bf16[144,512]{1,0:T(8,128)(2,1)S(1)}, bf16[144,512]{1,0:T(8,128)(2,1)S(1)}, u32[]{:S(2)}, u32[]{:S(2)}) collective-permute-start(bf16[144,512]{1,0:T(8,128)(2,1)S(1)} %get-tuple-element.54), channel_id=1, source_target_pairs={{0,4},{4,0},{8,12},{12,8},{16,20},{20,16},{24,28},{28,24},{1,5},{5... | collective-permute-start | bytes 442376 | tf_op jit(solution)/shard_map/ppermute | solution.py:445
  18.3 0.0 collective-permute-start.9
  18.3 5.4 %later_states.1 = (bf16[768,2048]{1,0:T(8,128)(2,1)S(1)}, bf16[768,2048]{1,0:T(8,128)(2,1)S(1)}, bf16[768,2048]{1,0:T(8,128)(2,1)S(1)}, bf16[144,512]{1,0:T(8,12...) custom-call(s32[1]{0:T(128)} %bitcast.refs_0_.place_ref, ...), custom_call_target="tpu_custom_call" | custom-call | tf_op jit(solution)/shard_map/later_states/pallas_call | solution.py:283
  23.7 1.1 %collective-permute-start.1 = (bf16[144,512]{1,0:T(8,128)(2,1)S(1)}, bf16[144,512]{1,0:T(8,128)(2,1)S(1)}, u32[]{:S(2)}, u32[]{:S(2)}) collective-permute-start(bf16[144,512]{1,0:T(8,128)(2,1)S(1)} %get-tuple-element.47), channel_id=1, source_target_pairs={{0,4},{4,0},{8,12},{12,8},{16,20},{20,16},{24,28},{28,24},{1,5},{5... | collective-permute-start | bytes 442376 | tf_op jit(solution)/shard_map/ppermute | solution.py:445
  24.9 1.6 %collective-permute-start.2 = (bf16[144,512]{1,0:T(8,128)(2,1)S(1)}, bf16[144,512]{1,0:T(8,128)(2,1)S(1)}, u32[]{:S(2)}, u32[]{:S(2)}) collective-permute-start(bf16[144,512]{1,0:T(8,128)(2,1)S(1)} %get-tuple-element.48), channel_id=1, source_target_pairs={{0,8},{4,12},{8,0},{12,4},{16,24},{20,28},{24,16},{28,20},{1,9},{5... | collective-permute-start | bytes 442376 | tf_op jit(solution)/shard_map/ppermute | solution.py:445
  26.4 2.6 %local.3.refs_1_ = f32[768,2048]{1,0:T(8,128)S(1)} custom-call(bf16[768,2048]{1,0:T(8,128)(2,1)S(1)} %get-tuple-element.58.refs_0_, bf16[768,2048]{1,0:T(8,128)(2,1)S(1)} %get-tuple-element.59.refs_1_, bf16[768,2048]{1,0:T(8,128)(2,1)S(1)} %get-tuple-element.60.refs_2_, f32[768,128]{1,0:T(8,128)S(1)} %get-tuple-element.43.refs_3_, ...), custom_call_target="tpu_custom_call" | custom-call | tf_op jit(solution)/shard_map/local/pallas_call | solution.py:360
  29.1 0.0 collective-permute-done.10.refs_3_
  29.1 0.9 %collective-permute-start.3 = (bf16[144,512]{1,0:T(8,128)(2,1)S(1)}, bf16[144,512]{1,0:T(8,128)(2,1)S(1)}, u32[]{:S(2)}, u32[]{:S(2)}) collective-permute-start(bf16[144,512]{1,0:T(8,128)(2,1)S(1)} %get-tuple-element.49), channel_id=1, source_target_pairs={{0,12},{4,8},{8,4},{12,0},{16,28},{20,24},{24,20},{28,16},{1,13},{... | collective-permute-start | bytes 442376 | tf_op jit(solution)/shard_map/ppermute | solution.py:445
  30.0 0.0 collective-permute-done.8.refs_1_
  30.0 0.0 collective-permute-done.9.refs_2_
  30.0 0.3 combine.3
  30.3 3.1 %collective-permute-start.11 = (bf16[128,512]{1,0:T(8,128)(2,1)S(1)}, bf16[128,512]{1,0:T(8,128)(2,1)S(1)}, u32[]{:S(2)}, u32[]{:S(2)}) collective-permute-start(bf16[128,512]{1,0:T(8,128)(2,1)S(1)} %get-tuple-element.57), channel_id=1, source_target_pairs={{0,16},{4,20},{8,24},{12,28},{16,0},{20,4},{24,8},{28,12},{1,17},{... | collective-permute-start | bytes 393224 | tf_op jit(solution)/shard_map/ppermute | solution.py:451
  33.4 0.0 collective-permute-done.1.refs_1_
  33.4 0.0 collective-permute-done.2.refs_2_
  33.4 1.8 %collective-permute-done.3.refs_3_ = bf16[144,512]{1,0:T(8,128)(2,1)S(1)} collective-permute-done((bf16[144,512]{1,0:T(8,128)(2,1)S(1)}, bf16[144,512]{1,0:T(8,128)(2,1)S(1)}, u32[]{:S(2)}, u32[]{:S(2)}) %collective-permute-start.3) | collective-permute-done | bytes 147488 | tf_op jit(solution)/shard_map/ppermute | solution.py:445
  35.2 0.3 combine.2
  35.4 3.0 %collective-permute-start.4 = (bf16[128,512]{1,0:T(8,128)(2,1)S(1)}, bf16[128,512]{1,0:T(8,128)(2,1)S(1)}, u32[]{:S(2)}, u32[]{:S(2)}) collective-permute-start(bf16[128,512]{1,0:T(8,128)(2,1)S(1)} %get-tuple-element.52), channel_id=1, source_target_pairs={{0,16},{4,20},{8,24},{12,28},{16,0},{20,4},{24,8},{28,12},{1,17},{... | collective-permute-start | bytes 393224 | tf_op jit(solution)/shard_map/ppermute | solution.py:451
  38.5 0.0 collective-permute-done.11
  38.5 0.2 fusion.15
  38.7 1.1 %collective-permute-start.12 = (bf16[128,512]{1,0:T(8,128)(2,1)S(1)}, bf16[128,512]{1,0:T(8,128)(2,1)S(1)}, u32[]{:S(2)}, u32[]{:S(2)}) collective-permute-start(bf16[128,512]{1,0:T(8,128)(2,1)S(1)} %get-tuple-element.66), channel_id=1, source_target_pairs={{0,4},{4,0},{8,12},{12,8},{16,20},{20,16},{24,28},{28,24},{1,5},{5... | collective-permute-start | bytes 393224 | tf_op jit(solution)/shard_map/ppermute | solution.py:445
  39.8 2.5 %collective-permute-start.13 = (bf16[128,512]{1,0:T(8,128)(2,1)S(1)}, bf16[128,512]{1,0:T(8,128)(2,1)S(1)}, u32[]{:S(2)}, u32[]{:S(2)}) collective-permute-start(bf16[128,512]{1,0:T(8,128)(2,1)S(1)} %get-tuple-element.67), channel_id=1, source_target_pairs={{0,8},{4,12},{8,0},{12,4},{16,24},{20,28},{24,16},{28,20},{1,9},{5... | collective-permute-start | bytes 393224 | tf_op jit(solution)/shard_map/ppermute | solution.py:445
  42.3 0.8 %collective-permute-start.14 = (bf16[128,512]{1,0:T(8,128)(2,1)S(1)}, bf16[128,512]{1,0:T(8,128)(2,1)S(1)}, u32[]{:S(2)}, u32[]{:S(2)}) collective-permute-start(bf16[128,512]{1,0:T(8,128)(2,1)S(1)} %get-tuple-element.65), channel_id=1, source_target_pairs={{0,12},{4,8},{8,4},{12,0},{16,28},{20,24},{24,20},{28,16},{1,13},{... | collective-permute-start | bytes 393224 | tf_op jit(solution)/shard_map/ppermute | solution.py:445
  43.1 1.0 %collective-permute-done.4 = bf16[128,512]{1,0:T(8,128)(2,1)S(1)} collective-permute-done((bf16[128,512]{1,0:T(8,128)(2,1)S(1)}, bf16[128,512]{1,0:T(8,128)(2,1)S(1)}, u32[]{:S(2)}, u32[]{:S(2)}) %collective-permute-start.4) | collective-permute-done | bytes 131104 | tf_op jit(solution)/shard_map/ppermute | solution.py:451
  44.1 0.2 fusion.7
  44.3 1.2 %collective-permute-start.5 = (bf16[128,512]{1,0:T(8,128)(2,1)S(1)}, bf16[128,512]{1,0:T(8,128)(2,1)S(1)}, u32[]{:S(2)}, u32[]{:S(2)}) collective-permute-start(bf16[128,512]{1,0:T(8,128)(2,1)S(1)} %get-tuple-element.70), channel_id=1, source_target_pairs={{0,4},{4,0},{8,12},{12,8},{16,20},{20,16},{24,28},{28,24},{1,5},{5... | collective-permute-start | bytes 393224 | tf_op jit(solution)/shard_map/ppermute | solution.py:445
  45.5 0.6 collective-permute-start.6
  46.0 0.0 collective-permute-done.12.refs_6_
  46.0 1.9 %collective-permute-start.7 = (bf16[128,512]{1,0:T(8,128)(2,1)S(1)}, bf16[128,512]{1,0:T(8,128)(2,1)S(1)}, u32[]{:S(2)}, u32[]{:S(2)}) collective-permute-start(bf16[128,512]{1,0:T(8,128)(2,1)S(1)} %get-tuple-element.69), channel_id=1, source_target_pairs={{0,12},{4,8},{8,4},{12,0},{16,28},{20,24},{24,20},{28,16},{1,13},{... | collective-permute-start | bytes 393224 | tf_op jit(solution)/shard_map/ppermute | solution.py:445
  47.9 2.6 %local.2.refs_1_ = f32[768,2048]{1,0:T(8,128)S(1)} custom-call(bf16[768,2048]{1,0:T(8,128)(2,1)S(1)} %get-tuple-element.40.refs_0_, bf16[768,2048]{1,0:T(8,128)(2,1)S(1)} %get-tuple-element.41.refs_1_, bf16[768,2048]{1,0:T(8,128)(2,1)S(1)} %get-tuple-element.42.refs_2_, f32[768,128]{1,0:T(8,128)S(1)} %get-tuple-element.43.refs_3_, ...), custom_call_target="tpu_custom_call" | custom-call | tf_op jit(solution)/shard_map/local/pallas_call | solution.py:360
  50.6 0.0 collective-permute-done.13.refs_7_
  50.6 0.0 collective-permute-done.14.refs_8_
  50.6 2.7 %finish_first.1.refs_9_ = bf16[768,2048]{1,0:T(8,128)(2,1)S(1)} custom-call(s32[1]{0:T(128)} %bitcast.refs_0_.place_ref, f32[768,2048]{1,0:T(8,128)S(1)} %local.3.refs_1_, f32[768,128]{1,0:T(8,128)S(1)} %get-tuple-element.45.refs_2_, bf16[768,256]{1,0:T(8,128)(2,1)S(1)} %get-tuple-element.44.refs_5_.refs_3_, f32[1,4096]{1,0:T(1,128)S(1)} %bitcast.30, ...), custom_call_target="tpu_custom_call" | custom-call | tf_op jit(solution)/shard_map/finish_first/pallas_call | solution.py:397
  53.3 0.0 collective-permute-done.5.refs_6_
  53.3 0.0 collective-permute-done.6.refs_7_
  53.3 0.6 collective-permute-done.7.refs_8_
  53.9 3.5 %finish.1 = bf16[768,4096]{1,0:T(8,128)(2,1)} custom-call(s32[1]{0:T(128)} %bitcast.refs_0_.place_ref, f32[768,2048]{1,0:T(8,128)S(1)} %local.2.refs_1_, f32[768,128]{1,0:T(8,128)S(1)} %get-tuple-element.45.refs_2_, bf16[768,256]{1,0:T(8,128)(2,1)S(1)} %get-tuple-element.44.refs_5_.refs_3_, f32[1,4096]{1,0:T(1,128)S(1)} %bitcast.31, ...), custom_call_target="tpu_custom_call" | custom-call | tf_op jit(solution)/shard_map/finish/pallas_call | solution.py:427
  (14 shorter events, 0.1 us)
Async XLA Ops:
  0.0 5.9 %copy-start.6 = (f32[64]{0:T(128)S(1)}, f32[64]{0:T(128)}, u32[]{:S(2)}) copy-start(f32[64]{0:T(128)} %param.14) | copy-start | bytes 772
  0.0 6.0 %copy-start.2 = (f32[768,64]{0,1:T(8,128)S(1)}, f32[768,64]{0,1:T(8,128)}, u32[]{:S(2)}) copy-start(f32[768,64]{0,1:T(8,128)} %param.11) | copy-start | bytes 589828
  0.0 6.0 %copy-start.3 = (f32[768,64]{0,1:T(8,128)S(1)}, f32[768,64]{0,1:T(8,128)}, u32[]{:S(2)}) copy-start(f32[768,64]{0,1:T(8,128)} %param.10) | copy-start | bytes 589828
  1.0 6.7 %collective-permute-start = (bf16[3,4352]{1,0:T(4,128)(2,1)S(1)}, bf16[3,4352]{1,0:T(4,128)(2,1)S(1)}, u32[]{:S(2)}, u32[]{:S(2)}) collective-permute-start(bf16[3,4352]{1,0:T(4,128)(2,1)S(1)} %slice.68), channel_id=1, source_target_pairs={{0,4},{4,8},{8,12},{12,16},{16,20},{20,24},{24,28},{1,5},{5,9},{9,... | collective-permute-start | bytes 78344 | tf_op jit(solution)/shard_map/ppermute | solution.py:440
  6.0 1.8 %copy-start = (bf16[768,256]{1,0:T(8,128)(2,1)S(1)}, bf16[768,256]{1,0:T(8,128)(2,1)}, u32[]{:S(2)}) copy-start(bf16[768,256]{1,0:T(8,128)(2,1)} %refs_3_.1) | copy-start | bytes 1179652
  6.0 1.8 %copy-start.1 = (f32[4,4096]{1,0:T(4,128)S(1)}, f32[4,4096]{1,0:T(4,128)}, u32[]{:S(2)}) copy-start(f32[4,4096]{1,0:T(4,128)} %refs_4_.1) | copy-start | bytes 196612
  6.0 1.8 %copy-start.5 = (f32[4,256]{1,0:T(4,128)S(1)}, f32[4,256]{1,0:T(4,128)}, u32[]{:S(2)}) copy-start(f32[4,256]{1,0:T(4,128)} %refs_6_.1) | copy-start | bytes 12292
  13.8 15.3 %collective-permute-start.10 = (bf16[144,512]{1,0:T(8,128)(2,1)S(1)}, bf16[144,512]{1,0:T(8,128)(2,1)S(1)}, u32[]{:S(2)}, u32[]{:S(2)}) collective-permute-start(bf16[144,512]{1,0:T(8,128)(2,1)S(1)} %get-tuple-element.56), channel_id=1, source_target_pairs={{0,12},{4,8},{8,4},{12,0},{16,28},{20,24},{24,20},{28,16},{1,13},{... | collective-permute-start | bytes 442376 | tf_op jit(solution)/shard_map/ppermute | solution.py:445
  16.9 13.1 %collective-permute-start.8 = (bf16[144,512]{1,0:T(8,128)(2,1)S(1)}, bf16[144,512]{1,0:T(8,128)(2,1)S(1)}, u32[]{:S(2)}, u32[]{:S(2)}) collective-permute-start(bf16[144,512]{1,0:T(8,128)(2,1)S(1)} %get-tuple-element.54), channel_id=1, source_target_pairs={{0,4},{4,0},{8,12},{12,8},{16,20},{20,16},{24,28},{28,24},{1,5},{5... | collective-permute-start | bytes 442376 | tf_op jit(solution)/shard_map/ppermute | solution.py:445
  18.3 11.7 %collective-permute-start.9 = (bf16[144,512]{1,0:T(8,128)(2,1)S(1)}, bf16[144,512]{1,0:T(8,128)(2,1)S(1)}, u32[]{:S(2)}, u32[]{:S(2)}) collective-permute-start(bf16[144,512]{1,0:T(8,128)(2,1)S(1)} %get-tuple-element.55), channel_id=1, source_target_pairs={{0,8},{4,12},{8,0},{12,4},{16,24},{20,28},{24,16},{28,20},{1,9},{5... | collective-permute-start | bytes 442376 | tf_op jit(solution)/shard_map/ppermute | solution.py:445
  23.7 9.6 %collective-permute-start.1 = (bf16[144,512]{1,0:T(8,128)(2,1)S(1)}, bf16[144,512]{1,0:T(8,128)(2,1)S(1)}, u32[]{:S(2)}, u32[]{:S(2)}) collective-permute-start(bf16[144,512]{1,0:T(8,128)(2,1)S(1)} %get-tuple-element.47), channel_id=1, source_target_pairs={{0,4},{4,0},{8,12},{12,8},{16,20},{20,16},{24,28},{28,24},{1,5},{5... | collective-permute-start | bytes 442376 | tf_op jit(solution)/shard_map/ppermute | solution.py:445
  24.9 8.5 %collective-permute-start.2 = (bf16[144,512]{1,0:T(8,128)(2,1)S(1)}, bf16[144,512]{1,0:T(8,128)(2,1)S(1)}, u32[]{:S(2)}, u32[]{:S(2)}) collective-permute-start(bf16[144,512]{1,0:T(8,128)(2,1)S(1)} %get-tuple-element.48), channel_id=1, source_target_pairs={{0,8},{4,12},{8,0},{12,4},{16,24},{20,28},{24,16},{28,20},{1,9},{5... | collective-permute-start | bytes 442376 | tf_op jit(solution)/shard_map/ppermute | solution.py:445
  29.1 6.1 %collective-permute-start.3 = (bf16[144,512]{1,0:T(8,128)(2,1)S(1)}, bf16[144,512]{1,0:T(8,128)(2,1)S(1)}, u32[]{:S(2)}, u32[]{:S(2)}) collective-permute-start(bf16[144,512]{1,0:T(8,128)(2,1)S(1)} %get-tuple-element.49), channel_id=1, source_target_pairs={{0,12},{4,8},{8,4},{12,0},{16,28},{20,24},{24,20},{28,16},{1,13},{... | collective-permute-start | bytes 442376 | tf_op jit(solution)/shard_map/ppermute | solution.py:445
  30.3 8.2 %collective-permute-start.11 = (bf16[128,512]{1,0:T(8,128)(2,1)S(1)}, bf16[128,512]{1,0:T(8,128)(2,1)S(1)}, u32[]{:S(2)}, u32[]{:S(2)}) collective-permute-start(bf16[128,512]{1,0:T(8,128)(2,1)S(1)} %get-tuple-element.57), channel_id=1, source_target_pairs={{0,16},{4,20},{8,24},{12,28},{16,0},{20,4},{24,8},{28,12},{1,17},{... | collective-permute-start | bytes 393224 | tf_op jit(solution)/shard_map/ppermute | solution.py:451
  35.4 8.7 %collective-permute-start.4 = (bf16[128,512]{1,0:T(8,128)(2,1)S(1)}, bf16[128,512]{1,0:T(8,128)(2,1)S(1)}, u32[]{:S(2)}, u32[]{:S(2)}) collective-permute-start(bf16[128,512]{1,0:T(8,128)(2,1)S(1)} %get-tuple-element.52), channel_id=1, source_target_pairs={{0,16},{4,20},{8,24},{12,28},{16,0},{20,4},{24,8},{28,12},{1,17},{... | collective-permute-start | bytes 393224 | tf_op jit(solution)/shard_map/ppermute | solution.py:451
  38.7 7.4 %collective-permute-start.12 = (bf16[128,512]{1,0:T(8,128)(2,1)S(1)}, bf16[128,512]{1,0:T(8,128)(2,1)S(1)}, u32[]{:S(2)}, u32[]{:S(2)}) collective-permute-start(bf16[128,512]{1,0:T(8,128)(2,1)S(1)} %get-tuple-element.66), channel_id=1, source_target_pairs={{0,4},{4,0},{8,12},{12,8},{16,20},{20,16},{24,28},{28,24},{1,5},{5... | collective-permute-start | bytes 393224 | tf_op jit(solution)/shard_map/ppermute | solution.py:445
  39.8 10.8 %collective-permute-start.13 = (bf16[128,512]{1,0:T(8,128)(2,1)S(1)}, bf16[128,512]{1,0:T(8,128)(2,1)S(1)}, u32[]{:S(2)}, u32[]{:S(2)}) collective-permute-start(bf16[128,512]{1,0:T(8,128)(2,1)S(1)} %get-tuple-element.67), channel_id=1, source_target_pairs={{0,8},{4,12},{8,0},{12,4},{16,24},{20,28},{24,16},{28,20},{1,9},{5... | collective-permute-start | bytes 393224 | tf_op jit(solution)/shard_map/ppermute | solution.py:445
  42.3 8.3 %collective-permute-start.14 = (bf16[128,512]{1,0:T(8,128)(2,1)S(1)}, bf16[128,512]{1,0:T(8,128)(2,1)S(1)}, u32[]{:S(2)}, u32[]{:S(2)}) collective-permute-start(bf16[128,512]{1,0:T(8,128)(2,1)S(1)} %get-tuple-element.65), channel_id=1, source_target_pairs={{0,12},{4,8},{8,4},{12,0},{16,28},{20,24},{24,20},{28,16},{1,13},{... | collective-permute-start | bytes 393224 | tf_op jit(solution)/shard_map/ppermute | solution.py:445
  44.3 9.1 %collective-permute-start.5 = (bf16[128,512]{1,0:T(8,128)(2,1)S(1)}, bf16[128,512]{1,0:T(8,128)(2,1)S(1)}, u32[]{:S(2)}, u32[]{:S(2)}) collective-permute-start(bf16[128,512]{1,0:T(8,128)(2,1)S(1)} %get-tuple-element.70), channel_id=1, source_target_pairs={{0,4},{4,0},{8,12},{12,8},{16,20},{20,16},{24,28},{28,24},{1,5},{5... | collective-permute-start | bytes 393224 | tf_op jit(solution)/shard_map/ppermute | solution.py:445
  45.5 7.8 %collective-permute-start.6 = (bf16[128,512]{1,0:T(8,128)(2,1)S(1)}, bf16[128,512]{1,0:T(8,128)(2,1)S(1)}, u32[]{:S(2)}, u32[]{:S(2)}) collective-permute-start(bf16[128,512]{1,0:T(8,128)(2,1)S(1)} %get-tuple-element.71), channel_id=1, source_target_pairs={{0,8},{4,12},{8,0},{12,4},{16,24},{20,28},{24,16},{28,20},{1,9},{5... | collective-permute-start | bytes 393224 | tf_op jit(solution)/shard_map/ppermute | solution.py:445
  46.0 7.9 %collective-permute-start.7 = (bf16[128,512]{1,0:T(8,128)(2,1)S(1)}, bf16[128,512]{1,0:T(8,128)(2,1)S(1)}, u32[]{:S(2)}, u32[]{:S(2)}) collective-permute-start(bf16[128,512]{1,0:T(8,128)(2,1)S(1)} %get-tuple-element.69), channel_id=1, source_target_pairs={{0,12},{4,8},{8,4},{12,0},{16,28},{20,24},{24,20},{28,16},{1,13},{... | collective-permute-start | bytes 393224 | tf_op jit(solution)/shard_map/ppermute | solution.py:445
  47.9 2.7 %copy-start.4 = (f32[4096]{0:T(1024)S(1)}, f32[4096]{0:T(1024)}, u32[]{:S(2)}) copy-start(f32[4096]{0:T(1024)} %param.15) | copy-start | bytes 49156

commit v6 on v5

--- a/solution.py
+++ b/solution.py
@@ -65,16 +65,21 @@
 
 def silu_conv(rows_back, taps):
     count = len(taps)
-    half = sum(rows_back(k) * (0.5 * taps[count - 1 - k]) for k in range(count))
+    half = sum(rows_back(k) * taps[count - 1 - k] for k in range(count))
     return half + half * jnp.tanh(half)
 
 
-def edges_kernel(inner_ref, proj_ref, out_ref, sems):
+def first_chunk(in_ref, head_ref, sem, first):
+    return pltpu.make_async_copy(in_ref.at[pl.ds(0, CHUNK), pl.ds(first, head_ref.shape[1])], head_ref, sem)
+
+
+def edges_kernel(inner_ref, proj_ref, out_ref, head_ref, sems):
     width = inner_ref.shape[1]
     last = pl.ds(inner_ref.shape[0] - EDGE, EDGE)
     copies = [
         pltpu.make_async_copy(inner_ref.at[last, :], out_ref.at[:, :width], sems.at[0]),
         pltpu.make_async_copy(proj_ref.at[last, :], out_ref.at[:, width:], sems.at[1]),
+        first_chunk(inner_ref, head_ref, sems.at[2], 0),
     ]
     for copy in copies:
         copy.start()
@@ -87,21 +92,15 @@
     return pl.pallas_call(
         edges_kernel,
         in_specs=[anywhere()] * 2,
-        out_specs=vmem(),
-        out_shape=jax.ShapeDtypeStruct((EDGE, width), BF16),
-        scratch_shapes=[pltpu.SemaphoreType.DMA((2,))],
+        out_specs=[vmem()] * 2,
+        out_shape=[jax.ShapeDtypeStruct((EDGE, width), BF16), jax.ShapeDtypeStruct((CHUNK, inner.shape[1] // GROUPS), BF16)],
+        scratch_shapes=[pltpu.SemaphoreType.DMA((3,))],
         compiler_params=params(),
         name="edges",
     )(inner, proj)
 
 
-def first_chunk(in_ref, head_ref, sem, first):
-    return pltpu.make_async_copy(in_ref.at[pl.ds(0, CHUNK), pl.ds(first, head_ref.shape[1])], head_ref, sem)
-
-
-def decay_kernel(decay_ref, step_ref, skip_ref, inner_ref, fwd_ref, inv_ref, dev_ref, fac_ref, head_ref, sem):
-    head = first_chunk(inner_ref, head_ref, sem, 0)
-    head.start()
+def decay_kernel(decay_ref, step_ref, skip_ref, fwd_ref, inv_ref, dev_ref, fac_ref):
     heads, rows = decay_ref.shape
     chunks = rows // CHUNK
     lower = jnp.where(iota((CHUNK, CHUNK), 0) >= iota((CHUNK, CHUNK), 1), 1.0, 0.0).astype(BF16)
@@ -129,27 +128,23 @@
         fac_ref[c : c + 1, :] = jnp.exp(totals[c] - middles[c] + following)
     fac_ref[chunks : chunks + 1, :] = skip_ref[:1]
     fac_ref[8:9, :] = jnp.exp(before[chunks])
-    head.wait()
-
-
-def decays(decay_log, step_size, skip_weight, inner):
+
+
+def decays(decay_log, step_size, skip_weight):
     rows, heads = decay_log.shape
     wide = jax.ShapeDtypeStruct((rows, LANES), F32)
     return pl.pallas_call(
         decay_kernel,
-        in_specs=[vmem()] * 3 + [anywhere()],
-        out_specs=[vmem()] * 5,
-        out_shape=(wide, wide, wide, jax.ShapeDtypeStruct((16, LANES), F32), jax.ShapeDtypeStruct((CHUNK, inner.shape[1] // GROUPS), BF16)),
-        scratch_shapes=[pltpu.SemaphoreType.DMA],
+        out_shape=(wide, wide, wide, jax.ShapeDtypeStruct((16, LANES), F32)),
         compiler_params=params(),
         name="decays",
-    )(decay_log.T, step_size.T, jnp.broadcast_to(jnp.tile(skip_weight, LANES // heads)[None], (8, LANES)), inner)
+    )(decay_log.T, step_size.T, jnp.broadcast_to(jnp.tile(skip_weight, LANES // heads)[None], (8, LANES)))
 
 
 def project(proj_ref, edge_ref, taps_ref, mix_ref, bt_ref, wide_ref):
     rows, width = proj_ref.shape
     state = width // 2
-    taps = [taps_ref[k : k + 1, :] for k in range(taps_ref.shape[0])]
+    taps = [0.5 * taps_ref[k : k + 1, :] for k in range(taps_ref.shape[0])]
     causal = iota((CHUNK, CHUNK), 0) >= iota((CHUNK, CHUNK), 1)
     past = edge_ref.shape[0]
     wide_ref[EDGE - past : EDGE, :] = edge_ref[:, edge_ref.shape[1] - width :].astype(F32)
@@ -163,7 +158,7 @@
         bt_ref[:, at] = b_rows.astype(F32).T.astype(BF16)
 
 
-def summarize(place_ref, in_ref, ready, edge_ref, taps_ref, inv_ref, fac_ref, bt_ref, x_ref, scaled_ref, opening_ref, slots, window_ref, sum_ref, row_ref, head_width, first):
+def summarize(place_ref, in_ref, ready, edge_ref, taps_ref, inv_ref, fac_ref, bt_ref, x_ref, scaled_ref, opening_ref, slots, window_ref, sum_ref, row_ref, half_ref, head_width, first):
     rows, wide = x_ref.shape
     cols = wide // SQUARE
     state = bt_ref.shape[0]
@@ -172,6 +167,7 @@
     for block in range(wide // LANES):
         at_lanes = pl.ds(first + block * LANES, LANES)
         window_ref[block, EDGE + CHUNK - count + 1 :, :] = edge_ref[:, at_lanes].astype(F32)
+        half_ref[block] = 0.5 * taps_ref[:, at_lanes]
     row_ref[...] = over_heads(fac_ref[...], head_width, first, wide)
     sum_ref[...] = jnp.zeros_like(sum_ref)
 
@@ -187,7 +183,7 @@
                 block = (sub * SUB + lane) // LANES
                 window_ref[block, EDGE - 8 : EDGE, :] = window_ref[block, EDGE + CHUNK - 8 :, :]
                 window_ref[block, EDGE:, :] = rows_here[:, lane : lane + LANES]
-                taps = [taps_ref[k : k + 1, pl.ds(here + lane, LANES)] for k in range(count)]
+                taps = [half_ref[block, k : k + 1, :] for k in range(count)]
                 xs.append(silu_conv(lambda k: window_ref[block, pl.ds(EDGE - k, CHUNK), :], taps))
             x = jnp.concatenate(xs, axis=1)
             x_ref[at, at_cols] = x.astype(BF16)
@@ -209,7 +205,7 @@
 
 
 def first_kernel(place_ref, in_ref, head_ref, proj_ref, edge_ref, taps_ref, proj_taps_ref, inv_ref, fac_ref, x_ref, scaled_ref, opening_ref, mix_ref, bt_ref, next_ref, *rest, head_width):
-    slots, (block_ref, wide_ref, window_ref, sum_ref, row_ref, sems) = rest[:SQUARE], rest[SQUARE:]
+    slots, (block_ref, wide_ref, window_ref, sum_ref, row_ref, half_ref, sems) = rest[:SQUARE], rest[SQUARE:]
     rows, wide = x_ref.shape
 
     def fetch(c):
@@ -222,7 +218,7 @@
     upcoming.start()
     block_ref[:CHUNK, :] = head_ref[...]
     project(proj_ref, edge_ref, proj_taps_ref, mix_ref, bt_ref, wide_ref)
-    summarize(place_ref, block_ref, lambda c: pl.when(c > 0)(lambda: fetch(c).wait()), edge_ref, taps_ref, inv_ref, fac_ref, bt_ref, x_ref, scaled_ref, opening_ref, slots, window_ref, sum_ref, row_ref, head_width, 0)
+    summarize(place_ref, block_ref, lambda c: pl.when(c > 0)(lambda: fetch(c).wait()), edge_ref, taps_ref, inv_ref, fac_ref, bt_ref, x_ref, scaled_ref, opening_ref, slots, window_ref, sum_ref, row_ref, half_ref, head_width, 0)
     upcoming.wait()
 
 
@@ -230,8 +226,8 @@
     return [jax.ShapeDtypeStruct((state + EDGE, wide // SQUARE), BF16)] * SQUARE
 
 
-def sum_scratch(state, wide):
-    return [pltpu.VMEM((wide // LANES, EDGE + CHUNK, LANES), F32), pltpu.VMEM((state, wide), F32), pltpu.VMEM((16, wide), F32)]
+def sum_scratch(state, wide, taps):
+    return [pltpu.VMEM((wide // LANES, EDGE + CHUNK, LANES), F32), pltpu.VMEM((state, wide), F32), pltpu.VMEM((16, wide), F32), pltpu.VMEM((wide // LANES, taps, LANES), F32)]
 
 
 def first_states(place, inner, head, proj, edge, taps, proj_taps, inv, fac, head_width):
@@ -253,7 +249,7 @@
         ]
         + slot_shapes(state, wide),
         scratch_shapes=[pltpu.VMEM((rows, wide), BF16), pltpu.VMEM((EDGE + rows, 2 * state), F32)]
-        + sum_scratch(state, wide)
+        + sum_scratch(state, wide, taps.shape[0])
         + [pltpu.SemaphoreType.DMA((chunks,))],
         compiler_params=params(),
         name="first_states",
@@ -262,7 +258,7 @@
 
 
 def later_kernel(place_ref, in_ref, head_ref, edge_ref, taps_ref, inv_ref, fac_ref, bt_ref, x_ref, scaled_ref, opening_ref, *rest, head_width, first):
-    slots, (block_ref, window_ref, sum_ref, row_ref, sems) = rest[:SQUARE], rest[SQUARE:]
+    slots, (block_ref, window_ref, sum_ref, row_ref, half_ref, sems) = rest[:SQUARE], rest[SQUARE:]
     rows, wide = x_ref.shape
 
     def fetch(c):
@@ -272,7 +268,7 @@
     for c in range(1, rows // CHUNK):
         fetch(c).start()
     block_ref[:CHUNK, :] = head_ref[...]
-    summarize(place_ref, block_ref, lambda c: pl.when(c > 0)(lambda: fetch(c).wait()), edge_ref, taps_ref, inv_ref, fac_ref, bt_ref, x_ref, scaled_ref, opening_ref, slots, window_ref, sum_ref, row_ref, head_width, first)
+    summarize(place_ref, block_ref, lambda c: pl.when(c > 0)(lambda: fetch(c).wait()), edge_ref, taps_ref, inv_ref, fac_ref, bt_ref, x_ref, scaled_ref, opening_ref, slots, window_ref, sum_ref, row_ref, half_ref, head_width, first)
 
 
 def later_states(place, inner, head, edge, taps, inv, fac, bt, head_width, group):
@@ -290,7 +286,7 @@
             jax.ShapeDtypeStruct((chunks * state, wide), BF16),
         ]
         + slot_shapes(state, wide),
-        scratch_shapes=[pltpu.VMEM((rows, wide), BF16)] + sum_scratch(state, wide) + [pltpu.SemaphoreType.DMA((chunks,))],
+        scratch_shapes=[pltpu.VMEM((rows, wide), BF16)] + sum_scratch(state, wide, taps.shape[0]) + [pltpu.SemaphoreType.DMA((chunks,))],
         compiler_params=params(),
         name="later_states",
     )(place, inner, head, edge, taps, inv, fac, bt)
@@ -352,7 +348,7 @@
             out_ref[at, at_cols] = mixed + skip * x_ref[at, at_cols].astype(F32)
         return 0
 
-    lax.fori_loop(0, SQUARE, tile_step, 0)
+    lax.fori_loop(0, SQUARE, tile_step, 0, unroll=2)
 
 
 def local_parts(x, scaled, opening, fwd, fac, mix, head_width, group):
@@ -468,8 +464,9 @@
     past = conv_inner.shape[0] - 1
     kept, kept_proj = [pltpu.with_memory_space_constraint(a, pltpu.HBM) for a in (inner_input, state_proj)]
     place = jnp.full((1,), lax.axis_index("ctx"), jnp.int32)
-    edge = shifted(last_rows(kept, kept_proj)[EDGE - past :], 1)
-    fwd, inv, dev, fac, head = decays(decay_log, step_size, skip_weight, kept)
+    edge, head = last_rows(kept, kept_proj)
+    edge = shifted(edge[EDGE - past :], 1)
+    fwd, inv, dev, fac = decays(decay_log, step_size, skip_weight)
     gain = norm_gain[None]
     made, sent = [], []
     parts, (mix, bt, head), slots = first_states(place, kept, head, state_proj, edge, conv_inner, conv_proj, inv, fac, head_width)
@@ -478,6 +475,7 @@
     parts, slots = later_states(place, kept, head, edge, conv_inner, inv, fac, bt, head_width, 1)
     made.append(parts)
     sent.append([slots[0]] + [swapped(slots[k], k) for k in range(1, SQUARE)])
+    made[0], sent[0] = lax.optimization_barrier((made[0], sent[0]))
     combined = [combine(place, sent[group]) for group in range(GROUPS)]
     arrived = [previous_squares(leaving, opening[SQUARE, :1]) for leaving, _, opening in combined]
     locals_ = [local_parts(*made[group], fwd, fac, mix, head_width, group) for group in range(GROUPS)]

time: 57.6 us -> 56.9 us (0.988)
  waiting for transfers between devices: 3.42 us -> 5.62 us
  starting transfers between devices: 27.2 us -> 25.4 us
  Pallas kernels: 26.1 us -> 25.1 us
    ppermute x12, waiting for transfers between devices: 2.38 us -> 5.1 us  [swapped(): return lax.ppermute(x, 'ctx', [(i, i ^ k) for i in range(length)])]
    ppermute x12, starting transfers between devices: 16.2 us -> 14.4 us  [swapped(): return lax.ppermute(x, 'ctx', [(i, i ^ k) for i in range(length)])]
    ppermute x2, waiting for transfers between devices: 1.03 us -> 0.01 us  [previous_squares(): lax.ppermute(leaving, 'ctx', [(i, (i + SQUARE) % length) for i in range(l...]
  transfers between devices with their start and end apart: 15 -> 15, of which waited for: 3 -> 4; matrix products, arithmetic and copies ran while one was open for 1% -> 1% of each run, Pallas kernels for 27% -> 26%
where the time goes in v6:
time: 56.9 us; the launch traced here: 56.7 us
  starting transfers between devices  25.4 us (45%)
  Pallas kernels  25.1 us (44%)
  waiting for transfers between devices  5.62 us (10%)
    ppermute x12, starting transfers between devices, swapped(): return lax.ppermute(x, 'ctx', [(i, i ^ k) for i in range(length)])  14.4 us
    ppermute x2, starting transfers between devices, previous_squares(): lax.ppermute(leaving, 'ctx', [(i, (i + SQUARE) % length) for i in range(l...  6.14 us
    pallas_call x1, Pallas kernels, first_states(): pl.pallas_call(lambda *refs: first_kernel(*refs, head_width=head_width),...  5.81 us
    pallas_call x1, Pallas kernels, later_states(): pl.pallas_call(lambda *refs: later_kernel(*refs, head_width=head_width, f...  5.27 us
    pallas_call x2, Pallas kernels, local_parts(): pl.pallas_call(lambda *refs: local_kernel(*refs, head_width=head_width, f...  5.12 us
    ppermute x12, waiting for transfers between devices, swapped(): return lax.ppermute(x, 'ctx', [(i, i ^ k) for i in range(length)])  5.1 us
    ppermute x1, starting transfers between devices, shifted(): return lax.ppermute(x, 'ctx', [(i, i + by) for i in range(length - by)])  4.86 us
    pallas_call x1, Pallas kernels, finish(): pl.pallas_call(lambda *refs: finish_kernel(*refs, head_width=head_width),...  3.51 us
  transfers between devices with their start and end apart: 15, of which 4 were waited for; matrix products, arithmetic and copies ran while one was open for 1% of the time, Pallas kernels for 26%

profile of v6, /device:TPU:0, one launch (start us, length us, event | category | flops | bytes accessed | tf_op | source)
XLA Modules:
  0.0 56.7 jit_solution(8124442255246112215)
XLA Ops:
  0.0 0.0 copy-start.5
  0.0 1.2 %edges.1 = (bf16[16,4352]{1,0:T(8,128)(2,1)S(1)}, bf16[128,2048]{1,0:T(8,128)(2,1)S(1)}) custom-call(bf16[768,4096]{1,0:T(8,128)(2,1)} %refs_1_.3, bf16[768,256]{1,0:T(8,128)(2,1)} %refs_3_.1), custom_call_target="tpu_custom_call" | custom-call | tf_op jit(solution)/shard_map/edges/pallas_call | solution.py:92
  1.3 4.9 %collective-permute-start = (bf16[3,4352]{1,0:T(4,128)(2,1)S(1)}, bf16[3,4352]{1,0:T(4,128)(2,1)S(1)}, u32[]{:S(2)}, u32[]{:S(2)}) collective-permute-start(bf16[3,4352]{1,0:T(4,128)(2,1)S(1)} %slice.51), channel_id=1, source_target_pairs={{0,4},{4,8},{8,12},{12,16},{16,20},{20,24},{24,28},{1,5},{5,9},{9,... | collective-permute-start | bytes 78344 | tf_op jit(solution)/shard_map/ppermute | solution.py:436
  6.2 0.0 copy-done.6
  6.2 0.1 broadcast_in_dim.14
  6.3 0.0 copy-done.2
  6.3 0.0 copy-done.3
  6.3 1.0 %decays.1 = (f32[768,128]{1,0:T(8,128)S(1)}, f32[768,128]{1,0:T(8,128)S(1)}, f32[768,128]{1,0:T(8,128)S(1)}, f32[16,128]{1,0:T(8,128)S(1)}) custom-call(f32[64,768]{1,0:T(8,128)S(1)} %bitcast.28, f32[64,768]{1,0:T(8,128)S(1)} %bitcast.29, f32[8,128]{1,0:T(8,128)S(1)} %broadcast_in_dim.15.skip_ref), custom_call_target="tpu_custom_call" | custom-call | tf_op jit(solution)/shard_map/decays/pallas_call | solution.py:136
  7.2 0.5 collective-permute-done.refs_4_.refs_3_
  7.7 0.0 copy-done
  7.8 5.8 %first_states.1 = (bf16[768,2048]{1,0:T(8,128)(2,1)S(1)}, bf16[768,2048]{1,0:T(8,128)(2,1)S(1)}, bf16[768,2048]{1,0:T(8,128)(2,1)S(1)}, bf16[768,256]{1,0:T(8,12...) custom-call(s32[1]{0:T(128)} %bitcast.refs_0_.place_ref, ...), custom_call_target="tpu_custom_call" | custom-call | tf_op jit(solution)/shard_map/first_states/pallas_call | solution.py:238
  13.6 3.4 %collective-permute-start.10 = (bf16[144,512]{1,0:T(8,128)(2,1)S(1)}, bf16[144,512]{1,0:T(8,128)(2,1)S(1)}, u32[]{:S(2)}, u32[]{:S(2)}) collective-permute-start(bf16[144,512]{1,0:T(8,128)(2,1)S(1)} %get-tuple-element.68), channel_id=1, source_target_pairs={{0,12},{4,8},{8,4},{12,0},{16,28},{20,24},{24,20},{28,16},{1,13},{... | collective-permute-start | bytes 442376 | tf_op jit(solution)/shard_map/ppermute | solution.py:441
  17.0 1.4 %collective-permute-start.8 = (bf16[144,512]{1,0:T(8,128)(2,1)S(1)}, bf16[144,512]{1,0:T(8,128)(2,1)S(1)}, u32[]{:S(2)}, u32[]{:S(2)}) collective-permute-start(bf16[144,512]{1,0:T(8,128)(2,1)S(1)} %get-tuple-element.66), channel_id=1, source_target_pairs={{0,4},{4,0},{8,12},{12,8},{16,20},{20,16},{24,28},{28,24},{1,5},{5... | collective-permute-start | bytes 442376 | tf_op jit(solution)/shard_map/ppermute | solution.py:441
  18.4 0.0 collective-permute-start.9
  18.4 5.3 %later_states.1 = (bf16[768,2048]{1,0:T(8,128)(2,1)S(1)}, bf16[768,2048]{1,0:T(8,128)(2,1)S(1)}, bf16[768,2048]{1,0:T(8,128)(2,1)S(1)}, bf16[144,512]{1,0:T(8,12...) custom-call(s32[1]{0:T(128)} %bitcast.refs_0_.place_ref, ...), custom_call_target="tpu_custom_call" | custom-call | tf_op jit(solution)/shard_map/later_states/pallas_call | solution.py:279
  23.7 1.1 %collective-permute-start.1 = (bf16[144,512]{1,0:T(8,128)(2,1)S(1)}, bf16[144,512]{1,0:T(8,128)(2,1)S(1)}, u32[]{:S(2)}, u32[]{:S(2)}) collective-permute-start(bf16[144,512]{1,0:T(8,128)(2,1)S(1)} %get-tuple-element.56), channel_id=1, source_target_pairs={{0,4},{4,0},{8,12},{12,8},{16,20},{20,16},{24,28},{28,24},{1,5},{5... | collective-permute-start | bytes 442376 | tf_op jit(solution)/shard_map/ppermute | solution.py:441
  24.8 1.6 %collective-permute-start.2 = (bf16[144,512]{1,0:T(8,128)(2,1)S(1)}, bf16[144,512]{1,0:T(8,128)(2,1)S(1)}, u32[]{:S(2)}, u32[]{:S(2)}) collective-permute-start(bf16[144,512]{1,0:T(8,128)(2,1)S(1)} %get-tuple-element.57), channel_id=1, source_target_pairs={{0,8},{4,12},{8,0},{12,4},{16,24},{20,28},{24,16},{28,20},{1,9},{5... | collective-permute-start | bytes 442376 | tf_op jit(solution)/shard_map/ppermute | solution.py:441
  26.4 0.0 collective-permute-done.10.refs_3_
  26.4 0.9 %collective-permute-start.3 = (bf16[144,512]{1,0:T(8,128)(2,1)S(1)}, bf16[144,512]{1,0:T(8,128)(2,1)S(1)}, u32[]{:S(2)}, u32[]{:S(2)}) collective-permute-start(bf16[144,512]{1,0:T(8,128)(2,1)S(1)} %get-tuple-element.58), channel_id=1, source_target_pairs={{0,12},{4,8},{8,4},{12,0},{16,28},{20,24},{24,20},{28,16},{1,13},{... | collective-permute-start | bytes 442376 | tf_op jit(solution)/shard_map/ppermute | solution.py:441
  27.3 0.0 collective-permute-done.8.refs_1_
  27.3 0.0 collective-permute-done.9.refs_2_
  27.3 0.3 combine.3
  27.5 3.1 %collective-permute-start.11 = (bf16[128,512]{1,0:T(8,128)(2,1)S(1)}, bf16[128,512]{1,0:T(8,128)(2,1)S(1)}, u32[]{:S(2)}, u32[]{:S(2)}) collective-permute-start(bf16[128,512]{1,0:T(8,128)(2,1)S(1)} %get-tuple-element.73), channel_id=1, source_target_pairs={{0,16},{4,20},{8,24},{12,28},{16,0},{20,4},{24,8},{28,12},{1,17},{... | collective-permute-start | bytes 393224 | tf_op jit(solution)/shard_map/ppermute | solution.py:447
  30.6 0.0 collective-permute-done.1.refs_1_
  30.6 1.1 %collective-permute-done.2.refs_2_ = bf16[144,512]{1,0:T(8,128)(2,1)S(1)} collective-permute-done((bf16[144,512]{1,0:T(8,128)(2,1)S(1)}, bf16[144,512]{1,0:T(8,128)(2,1)S(1)}, u32[]{:S(2)}, u32[]{:S(2)}) %collective-permute-start.2) | collective-permute-done | bytes 147488 | tf_op jit(solution)/shard_map/ppermute | solution.py:441
  31.7 2.8 %collective-permute-done.3.refs_3_ = bf16[144,512]{1,0:T(8,128)(2,1)S(1)} collective-permute-done((bf16[144,512]{1,0:T(8,128)(2,1)S(1)}, bf16[144,512]{1,0:T(8,128)(2,1)S(1)}, u32[]{:S(2)}, u32[]{:S(2)}) %collective-permute-start.3) | collective-permute-done | bytes 147488 | tf_op jit(solution)/shard_map/ppermute | solution.py:441
  34.6 0.3 combine.2
  34.8 3.0 %collective-permute-start.4 = (bf16[128,512]{1,0:T(8,128)(2,1)S(1)}, bf16[128,512]{1,0:T(8,128)(2,1)S(1)}, u32[]{:S(2)}, u32[]{:S(2)}) collective-permute-start(bf16[128,512]{1,0:T(8,128)(2,1)S(1)} %get-tuple-element.61), channel_id=1, source_target_pairs={{0,16},{4,20},{8,24},{12,28},{16,0},{20,4},{24,8},{28,12},{1,17},{... | collective-permute-start | bytes 393224 | tf_op jit(solution)/shard_map/ppermute | solution.py:447
  37.9 2.6 %local.3.refs_1_ = f32[768,2048]{1,0:T(8,128)S(1)} custom-call(bf16[768,2048]{1,0:T(8,128)(2,1)S(1)} %get-tuple-element.74.refs_0_, bf16[768,2048]{1,0:T(8,128)(2,1)S(1)} %get-tuple-element.75.refs_1_, bf16[768,2048]{1,0:T(8,128)(2,1)S(1)} %get-tuple-element.76.refs_2_, f32[768,128]{1,0:T(8,128)S(1)} %get-tuple-element.52.refs_3_, ...), custom_call_target="tpu_custom_call" | custom-call | tf_op jit(solution)/shard_map/local/pallas_call | solution.py:356
  40.5 0.0 collective-permute-done.11
  40.5 0.2 fusion.15
  40.6 1.3 %collective-permute-start.12 = (bf16[128,512]{1,0:T(8,128)(2,1)S(1)}, bf16[128,512]{1,0:T(8,128)(2,1)S(1)}, u32[]{:S(2)}, u32[]{:S(2)}) collective-permute-start(bf16[128,512]{1,0:T(8,128)(2,1)S(1)} %get-tuple-element.82), channel_id=1, source_target_pairs={{0,4},{4,0},{8,12},{12,8},{16,20},{20,16},{24,28},{28,24},{1,5},{5... | collective-permute-start | bytes 393224 | tf_op jit(solution)/shard_map/ppermute | solution.py:441
  41.9 0.1 collective-permute-start.13
  42.0 2.2 %collective-permute-start.14 = (bf16[128,512]{1,0:T(8,128)(2,1)S(1)}, bf16[128,512]{1,0:T(8,128)(2,1)S(1)}, u32[]{:S(2)}, u32[]{:S(2)}) collective-permute-start(bf16[128,512]{1,0:T(8,128)(2,1)S(1)} %get-tuple-element.81), channel_id=1, source_target_pairs={{0,12},{4,8},{8,4},{12,0},{16,28},{20,24},{24,20},{28,16},{1,13},{... | collective-permute-start | bytes 393224 | tf_op jit(solution)/shard_map/ppermute | solution.py:441
  44.2 0.0 collective-permute-done.4
  44.2 0.2 fusion.7
  44.4 1.3 %collective-permute-start.5 = (bf16[128,512]{1,0:T(8,128)(2,1)S(1)}, bf16[128,512]{1,0:T(8,128)(2,1)S(1)}, u32[]{:S(2)}, u32[]{:S(2)}) collective-permute-start(bf16[128,512]{1,0:T(8,128)(2,1)S(1)} %get-tuple-element.86), channel_id=1, source_target_pairs={{0,4},{4,0},{8,12},{12,8},{16,20},{20,16},{24,28},{28,24},{1,5},{5... | collective-permute-start | bytes 393224 | tf_op jit(solution)/shard_map/ppermute | solution.py:441
  45.6 0.1 collective-permute-start.6
  45.8 1.1 %collective-permute-done.12.refs_6_ = bf16[128,512]{1,0:T(8,128)(2,1)S(1)} collective-permute-done((bf16[128,512]{1,0:T(8,128)(2,1)S(1)}, bf16[128,512]{1,0:T(8,128)(2,1)S(1)}, u32[]{:S(2)}, u32[]{:S(2)}) %collective-permute-start.12) | collective-permute-done | bytes 131104 | tf_op jit(solution)/shard_map/ppermute | solution.py:441
  46.9 1.0 %collective-permute-start.7 = (bf16[128,512]{1,0:T(8,128)(2,1)S(1)}, bf16[128,512]{1,0:T(8,128)(2,1)S(1)}, u32[]{:S(2)}, u32[]{:S(2)}) collective-permute-start(bf16[128,512]{1,0:T(8,128)(2,1)S(1)} %get-tuple-element.85), channel_id=1, source_target_pairs={{0,12},{4,8},{8,4},{12,0},{16,28},{20,24},{24,20},{28,16},{1,13},{... | collective-permute-start | bytes 393224 | tf_op jit(solution)/shard_map/ppermute | solution.py:441
  47.9 2.5 %local.2.refs_1_ = f32[768,2048]{1,0:T(8,128)S(1)} custom-call(bf16[768,2048]{1,0:T(8,128)(2,1)S(1)} %get-tuple-element.49.refs_0_, bf16[768,2048]{1,0:T(8,128)(2,1)S(1)} %get-tuple-element.50.refs_1_, bf16[768,2048]{1,0:T(8,128)(2,1)S(1)} %get-tuple-element.51.refs_2_, f32[768,128]{1,0:T(8,128)S(1)} %get-tuple-element.52.refs_3_, ...), custom_call_target="tpu_custom_call" | custom-call | tf_op jit(solution)/shard_map/local/pallas_call | solution.py:356
  50.5 0.0 collective-permute-done.13.refs_7_
  50.5 0.0 collective-permute-done.14.refs_8_
  50.5 2.7 %finish_first.1.refs_9_ = bf16[768,2048]{1,0:T(8,128)(2,1)S(1)} custom-call(s32[1]{0:T(128)} %bitcast.refs_0_.place_ref, f32[768,2048]{1,0:T(8,128)S(1)} %local.3.refs_1_, f32[768,128]{1,0:T(8,128)S(1)} %get-tuple-element.54.refs_2_, bf16[768,256]{1,0:T(8,128)(2,1)S(1)} %get-tuple-element.53.refs_5_.refs_3_, f32[1,4096]{1,0:T(1,128)S(1)} %bitcast.30, ...), custom_call_target="tpu_custom_call" | custom-call | tf_op jit(solution)/shard_map/finish_first/pallas_call | solution.py:393
  53.2 0.0 collective-permute-done.5.refs_6_
  53.2 0.0 collective-permute-done.6.refs_7_
  53.2 0.0 collective-permute-done.7.refs_8_
  53.2 3.5 %finish.1 = bf16[768,4096]{1,0:T(8,128)(2,1)} custom-call(s32[1]{0:T(128)} %bitcast.refs_0_.place_ref, f32[768,2048]{1,0:T(8,128)S(1)} %local.2.refs_1_, f32[768,128]{1,0:T(8,128)S(1)} %get-tuple-element.54.refs_2_, bf16[768,256]{1,0:T(8,128)(2,1)S(1)} %get-tuple-element.53.refs_5_.refs_3_, f32[1,4096]{1,0:T(1,128)S(1)} %bitcast.31, ...), custom_call_target="tpu_custom_call" | custom-call | tf_op jit(solution)/shard_map/finish/pallas_call | solution.py:423
  (14 shorter events, 0.1 us)
Async XLA Ops:
  0.0 7.7 %copy-start = (bf16[768,256]{1,0:T(8,128)(2,1)S(1)}, bf16[768,256]{1,0:T(8,128)(2,1)}, u32[]{:S(2)}) copy-start(bf16[768,256]{1,0:T(8,128)(2,1)} %refs_3_.1) | copy-start | bytes 1179652
  0.0 6.2 %copy-start.6 = (f32[64]{0:T(128)S(1)}, f32[64]{0:T(128)}, u32[]{:S(2)}) copy-start(f32[64]{0:T(128)} %param.14) | copy-start | bytes 772
  0.0 6.3 %copy-start.2 = (f32[768,64]{0,1:T(8,128)S(1)}, f32[768,64]{0,1:T(8,128)}, u32[]{:S(2)}) copy-start(f32[768,64]{0,1:T(8,128)} %param.11) | copy-start | bytes 589828
  0.0 6.3 %copy-start.3 = (f32[768,64]{0,1:T(8,128)S(1)}, f32[768,64]{0,1:T(8,128)}, u32[]{:S(2)}) copy-start(f32[768,64]{0,1:T(8,128)} %param.10) | copy-start | bytes 589828
  0.0 7.7 %copy-start.1 = (f32[4,4096]{1,0:T(4,128)S(1)}, f32[4,4096]{1,0:T(4,128)}, u32[]{:S(2)}) copy-start(f32[4,4096]{1,0:T(4,128)} %refs_4_.1) | copy-start | bytes 196612
  0.0 7.7 %copy-start.5 = (f32[4,256]{1,0:T(4,128)S(1)}, f32[4,256]{1,0:T(4,128)}, u32[]{:S(2)}) copy-start(f32[4,256]{1,0:T(4,128)} %refs_6_.1) | copy-start | bytes 12292
  1.3 6.5 %collective-permute-start = (bf16[3,4352]{1,0:T(4,128)(2,1)S(1)}, bf16[3,4352]{1,0:T(4,128)(2,1)S(1)}, u32[]{:S(2)}, u32[]{:S(2)}) collective-permute-start(bf16[3,4352]{1,0:T(4,128)(2,1)S(1)} %slice.51), channel_id=1, source_target_pairs={{0,4},{4,8},{8,12},{12,16},{16,20},{20,24},{24,28},{1,5},{5,9},{9,... | collective-permute-start | bytes 78344 | tf_op jit(solution)/shard_map/ppermute | solution.py:436
  13.6 12.8 %collective-permute-start.10 = (bf16[144,512]{1,0:T(8,128)(2,1)S(1)}, bf16[144,512]{1,0:T(8,128)(2,1)S(1)}, u32[]{:S(2)}, u32[]{:S(2)}) collective-permute-start(bf16[144,512]{1,0:T(8,128)(2,1)S(1)} %get-tuple-element.68), channel_id=1, source_target_pairs={{0,12},{4,8},{8,4},{12,0},{16,28},{20,24},{24,20},{28,16},{1,13},{... | collective-permute-start | bytes 442376 | tf_op jit(solution)/shard_map/ppermute | solution.py:441
  17.0 10.3 %collective-permute-start.8 = (bf16[144,512]{1,0:T(8,128)(2,1)S(1)}, bf16[144,512]{1,0:T(8,128)(2,1)S(1)}, u32[]{:S(2)}, u32[]{:S(2)}) collective-permute-start(bf16[144,512]{1,0:T(8,128)(2,1)S(1)} %get-tuple-element.66), channel_id=1, source_target_pairs={{0,4},{4,0},{8,12},{12,8},{16,20},{20,16},{24,28},{28,24},{1,5},{5... | collective-permute-start | bytes 442376 | tf_op jit(solution)/shard_map/ppermute | solution.py:441
  18.4 8.8 %collective-permute-start.9 = (bf16[144,512]{1,0:T(8,128)(2,1)S(1)}, bf16[144,512]{1,0:T(8,128)(2,1)S(1)}, u32[]{:S(2)}, u32[]{:S(2)}) collective-permute-start(bf16[144,512]{1,0:T(8,128)(2,1)S(1)} %get-tuple-element.67), channel_id=1, source_target_pairs={{0,8},{4,12},{8,0},{12,4},{16,24},{20,28},{24,16},{28,20},{1,9},{5... | collective-permute-start | bytes 442376 | tf_op jit(solution)/shard_map/ppermute | solution.py:441
  23.7 6.9 %collective-permute-start.1 = (bf16[144,512]{1,0:T(8,128)(2,1)S(1)}, bf16[144,512]{1,0:T(8,128)(2,1)S(1)}, u32[]{:S(2)}, u32[]{:S(2)}) collective-permute-start(bf16[144,512]{1,0:T(8,128)(2,1)S(1)} %get-tuple-element.56), channel_id=1, source_target_pairs={{0,4},{4,0},{8,12},{12,8},{16,20},{20,16},{24,28},{28,24},{1,5},{5... | collective-permute-start | bytes 442376 | tf_op jit(solution)/shard_map/ppermute | solution.py:441
  24.8 6.9 %collective-permute-start.2 = (bf16[144,512]{1,0:T(8,128)(2,1)S(1)}, bf16[144,512]{1,0:T(8,128)(2,1)S(1)}, u32[]{:S(2)}, u32[]{:S(2)}) collective-permute-start(bf16[144,512]{1,0:T(8,128)(2,1)S(1)} %get-tuple-element.57), channel_id=1, source_target_pairs={{0,8},{4,12},{8,0},{12,4},{16,24},{20,28},{24,16},{28,20},{1,9},{5... | collective-permute-start | bytes 442376 | tf_op jit(solution)/shard_map/ppermute | solution.py:441
  26.4 8.2 %collective-permute-start.3 = (bf16[144,512]{1,0:T(8,128)(2,1)S(1)}, bf16[144,512]{1,0:T(8,128)(2,1)S(1)}, u32[]{:S(2)}, u32[]{:S(2)}) collective-permute-start(bf16[144,512]{1,0:T(8,128)(2,1)S(1)} %get-tuple-element.58), channel_id=1, source_target_pairs={{0,12},{4,8},{8,4},{12,0},{16,28},{20,24},{24,20},{28,16},{1,13},{... | collective-permute-start | bytes 442376 | tf_op jit(solution)/shard_map/ppermute | solution.py:441
  27.5 13.0 %collective-permute-start.11 = (bf16[128,512]{1,0:T(8,128)(2,1)S(1)}, bf16[128,512]{1,0:T(8,128)(2,1)S(1)}, u32[]{:S(2)}, u32[]{:S(2)}) collective-permute-start(bf16[128,512]{1,0:T(8,128)(2,1)S(1)} %get-tuple-element.73), channel_id=1, source_target_pairs={{0,16},{4,20},{8,24},{12,28},{16,0},{20,4},{24,8},{28,12},{1,17},{... | collective-permute-start | bytes 393224 | tf_op jit(solution)/shard_map/ppermute | solution.py:447
  34.8 9.4 %collective-permute-start.4 = (bf16[128,512]{1,0:T(8,128)(2,1)S(1)}, bf16[128,512]{1,0:T(8,128)(2,1)S(1)}, u32[]{:S(2)}, u32[]{:S(2)}) collective-permute-start(bf16[128,512]{1,0:T(8,128)(2,1)S(1)} %get-tuple-element.61), channel_id=1, source_target_pairs={{0,16},{4,20},{8,24},{12,28},{16,0},{20,4},{24,8},{28,12},{1,17},{... | collective-permute-start | bytes 393224 | tf_op jit(solution)/shard_map/ppermute | solution.py:447
  40.6 6.2 %collective-permute-start.12 = (bf16[128,512]{1,0:T(8,128)(2,1)S(1)}, bf16[128,512]{1,0:T(8,128)(2,1)S(1)}, u32[]{:S(2)}, u32[]{:S(2)}) collective-permute-start(bf16[128,512]{1,0:T(8,128)(2,1)S(1)} %get-tuple-element.82), channel_id=1, source_target_pairs={{0,4},{4,0},{8,12},{12,8},{16,20},{20,16},{24,28},{28,24},{1,5},{5... | collective-permute-start | bytes 393224 | tf_op jit(solution)/shard_map/ppermute | solution.py:441
  41.9 8.5 %collective-permute-start.13 = (bf16[128,512]{1,0:T(8,128)(2,1)S(1)}, bf16[128,512]{1,0:T(8,128)(2,1)S(1)}, u32[]{:S(2)}, u32[]{:S(2)}) collective-permute-start(bf16[128,512]{1,0:T(8,128)(2,1)S(1)} %get-tuple-element.83), channel_id=1, source_target_pairs={{0,8},{4,12},{8,0},{12,4},{16,24},{20,28},{24,16},{28,20},{1,9},{5... | collective-permute-start | bytes 393224 | tf_op jit(solution)/shard_map/ppermute | solution.py:441
  42.0 8.4 %collective-permute-start.14 = (bf16[128,512]{1,0:T(8,128)(2,1)S(1)}, bf16[128,512]{1,0:T(8,128)(2,1)S(1)}, u32[]{:S(2)}, u32[]{:S(2)}) collective-permute-start(bf16[128,512]{1,0:T(8,128)(2,1)S(1)} %get-tuple-element.81), channel_id=1, source_target_pairs={{0,12},{4,8},{8,4},{12,0},{16,28},{20,24},{24,20},{28,16},{1,13},{... | collective-permute-start | bytes 393224 | tf_op jit(solution)/shard_map/ppermute | solution.py:441
  44.4 8.8 %collective-permute-start.5 = (bf16[128,512]{1,0:T(8,128)(2,1)S(1)}, bf16[128,512]{1,0:T(8,128)(2,1)S(1)}, u32[]{:S(2)}, u32[]{:S(2)}) collective-permute-start(bf16[128,512]{1,0:T(8,128)(2,1)S(1)} %get-tuple-element.86), channel_id=1, source_target_pairs={{0,4},{4,0},{8,12},{12,8},{16,20},{20,16},{24,28},{28,24},{1,5},{5... | collective-permute-start | bytes 393224 | tf_op jit(solution)/shard_map/ppermute | solution.py:441
  45.6 7.6 %collective-permute-start.6 = (bf16[128,512]{1,0:T(8,128)(2,1)S(1)}, bf16[128,512]{1,0:T(8,128)(2,1)S(1)}, u32[]{:S(2)}, u32[]{:S(2)}) collective-permute-start(bf16[128,512]{1,0:T(8,128)(2,1)S(1)} %get-tuple-element.87), channel_id=1, source_target_pairs={{0,8},{4,12},{8,0},{12,4},{16,24},{20,28},{24,16},{28,20},{1,9},{5... | collective-permute-start | bytes 393224 | tf_op jit(solution)/shard_map/ppermute | solution.py:441
  46.9 6.3 %collective-permute-start.7 = (bf16[128,512]{1,0:T(8,128)(2,1)S(1)}, bf16[128,512]{1,0:T(8,128)(2,1)S(1)}, u32[]{:S(2)}, u32[]{:S(2)}) collective-permute-start(bf16[128,512]{1,0:T(8,128)(2,1)S(1)} %get-tuple-element.85), channel_id=1, source_target_pairs={{0,12},{4,8},{8,4},{12,0},{16,28},{20,24},{24,20},{28,16},{1,13},{... | collective-permute-start | bytes 393224 | tf_op jit(solution)/shard_map/ppermute | solution.py:441
  47.9 2.6 %copy-start.4 = (f32[4096]{0:T(1024)S(1)}, f32[4096]{0:T(1024)}, u32[]{:S(2)}) copy-start(f32[4096]{0:T(1024)} %param.15) | copy-start | bytes 49156

commit v7 on v6

--- a/solution.py
+++ b/solution.py
@@ -441,6 +441,11 @@
     return lax.ppermute(x, "ctx", [(i, i ^ k) for i in range(length)])
 
 
+def exchanged(slots):
+    received = [swapped(slots[k], k) for k in range(SQUARE - 1, 0, -1)]
+    return [slots[0]] + received[::-1]
+
+
 def previous_squares(leaving, decay):
     length = lax.axis_size("ctx")
     squares = length // SQUARE
@@ -471,20 +476,22 @@
     made, sent = [], []
     parts, (mix, bt, head), slots = first_states(place, kept, head, state_proj, edge, conv_inner, conv_proj, inv, fac, head_width)
     made.append(parts)
-    sent.append([slots[0]] + [swapped(slots[k], k) for k in range(1, SQUARE)])
+    sent.append(exchanged(slots))
     parts, slots = later_states(place, kept, head, edge, conv_inner, inv, fac, bt, head_width, 1)
     made.append(parts)
-    sent.append([slots[0]] + [swapped(slots[k], k) for k in range(1, SQUARE)])
+    sent.append(exchanged(slots))
     made[0], sent[0] = lax.optimization_barrier((made[0], sent[0]))
-    combined = [combine(place, sent[group]) for group in range(GROUPS)]
+    combined = [combine(place, sent[0])]
+    locals_ = [local_parts(*made[group], fwd, fac, mix, head_width, group) for group in range(GROUPS)]
+    sent[1], locals_[0] = lax.optimization_barrier((sent[1], locals_[0]))
+    combined.append(combine(place, sent[1]))
     arrived = [previous_squares(leaving, opening[SQUARE, :1]) for leaving, _, opening in combined]
-    locals_ = [local_parts(*made[group], fwd, fac, mix, head_width, group) for group in range(GROUPS)]
-    arrived[0], locals_[0] = lax.optimization_barrier((arrived[0], locals_[0]))
+    arrived[1], locals_[1] = lax.optimization_barrier((arrived[1], locals_[1]))
     returned = []
     for group in range(GROUPS):
         _, prefix, opening = combined[group]
         entering = [(prefix[k] + opening[k, :1] * arrived[group].astype(F32)).astype(BF16) for k in range(SQUARE)]
-        returned.append([entering[0]] + [swapped(entering[k], k) for k in range(1, SQUARE)])
+        returned.append(exchanged(entering))
     earlier = finish_first(place, locals_[0], dev, mix, gain, returned[0], head_width)
     return finish(place, locals_[1], dev, mix, gain, returned[1], earlier, head_width)
 

time: 56.9 us -> 56.8 us (level)
  waiting for transfers between devices: 5.62 us -> 2.37 us
  starting transfers between devices: 25.4 us -> 28.6 us
    ppermute x12, starting transfers between devices: 14.4 us -> 18.4 us  [swapped(): return lax.ppermute(x, 'ctx', [(i, i ^ k) for i in range(length)])]
    ppermute x12, waiting for transfers between devices: 5.1 us -> 1.75 us  [swapped(): return lax.ppermute(x, 'ctx', [(i, i ^ k) for i in range(length)])]
    ppermute x2, starting transfers between devices: 6.14 us -> 5.3 us  [previous_squares(): lax.ppermute(leaving, 'ctx', [(i, (i + SQUARE) % length) for i in range(l...]
where the time goes in v7:
time: 56.8 us; the launch traced here: 56.6 us
  starting transfers between devices  28.6 us (50%)
  Pallas kernels  25 us (44%)
  waiting for transfers between devices  2.37 us (4%)
    ppermute x12, starting transfers between devices, swapped(): return lax.ppermute(x, 'ctx', [(i, i ^ k) for i in range(length)])  18.4 us
    pallas_call x1, Pallas kernels, first_states(): pl.pallas_call(lambda *refs: first_kernel(*refs, head_width=head_width),...  5.81 us
    ppermute x2, starting transfers between devices, previous_squares(): lax.ppermute(leaving, 'ctx', [(i, (i + SQUARE) % length) for i in range(l...  5.3 us
    pallas_call x1, Pallas kernels, later_states(): pl.pallas_call(lambda *refs: later_kernel(*refs, head_width=head_width, f...  5.27 us
    pallas_call x2, Pallas kernels, local_parts(): pl.pallas_call(lambda *refs: local_kernel(*refs, head_width=head_width, f...  5.06 us
    ppermute x1, starting transfers between devices, shifted(): return lax.ppermute(x, 'ctx', [(i, i + by) for i in range(length - by)])  4.86 us
    pallas_call x1, Pallas kernels, finish(): pl.pallas_call(lambda *refs: finish_kernel(*refs, head_width=head_width),...  3.5 us
    pallas_call x1, Pallas kernels, finish_first(): pl.pallas_call(lambda *refs: finish_first_kernel(*refs, head_width=head_w...  2.68 us
  transfers between devices with their start and end apart: 15, of which 4 were waited for; matrix products, arithmetic and copies ran while one was open for 1% of the time, Pallas kernels for 26%

profile of v7, /device:TPU:0, one launch (start us, length us, event | category | flops | bytes accessed | tf_op | source)
XLA Modules:
  0.0 56.6 jit_solution(3597812229316904195)
XLA Ops:
  0.0 0.0 copy-start.5
  0.0 1.2 %edges.1 = (bf16[16,4352]{1,0:T(8,128)(2,1)S(1)}, bf16[128,2048]{1,0:T(8,128)(2,1)S(1)}) custom-call(bf16[768,4096]{1,0:T(8,128)(2,1)} %refs_1_.3, bf16[768,256]{1,0:T(8,128)(2,1)} %refs_3_.1), custom_call_target="tpu_custom_call" | custom-call | tf_op jit(solution)/shard_map/edges/pallas_call | solution.py:92
  1.3 4.9 %collective-permute-start = (bf16[3,4352]{1,0:T(4,128)(2,1)S(1)}, bf16[3,4352]{1,0:T(4,128)(2,1)S(1)}, u32[]{:S(2)}, u32[]{:S(2)}) collective-permute-start(bf16[3,4352]{1,0:T(4,128)(2,1)S(1)} %slice.51), channel_id=1, source_target_pairs={{0,4},{4,8},{8,12},{12,16},{16,20},{20,24},{24,28},{1,5},{5,9},{9,... | collective-permute-start | bytes 78344 | tf_op jit(solution)/shard_map/ppermute | solution.py:436
  6.2 0.0 copy-done.6
  6.2 0.1 broadcast_in_dim.14
  6.3 1.0 %decays.1 = (f32[768,128]{1,0:T(8,128)S(1)}, f32[768,128]{1,0:T(8,128)S(1)}, f32[768,128]{1,0:T(8,128)S(1)}, f32[16,128]{1,0:T(8,128)S(1)}) custom-call(f32[64,768]{1,0:T(8,128)S(1)} %bitcast.28, f32[64,768]{1,0:T(8,128)S(1)} %bitcast.29, f32[8,128]{1,0:T(8,128)S(1)} %broadcast_in_dim.15.skip_ref), custom_call_target="tpu_custom_call" | custom-call | tf_op jit(solution)/shard_map/decays/pallas_call | solution.py:136
  7.2 0.5 collective-permute-done.refs_4_.refs_3_
  7.7 0.0 copy-done
  7.8 0.0 copy-done.5
  7.8 5.8 %first_states.1 = (bf16[768,2048]{1,0:T(8,128)(2,1)S(1)}, bf16[768,2048]{1,0:T(8,128)(2,1)S(1)}, bf16[768,2048]{1,0:T(8,128)(2,1)S(1)}, bf16[768,256]{1,0:T(8,12...) custom-call(s32[1]{0:T(128)} %bitcast.refs_0_.place_ref, ...), custom_call_target="tpu_custom_call" | custom-call | tf_op jit(solution)/shard_map/first_states/pallas_call | solution.py:238
  13.6 2.4 %collective-permute-start.4 = (bf16[144,512]{1,0:T(8,128)(2,1)S(1)}, bf16[144,512]{1,0:T(8,128)(2,1)S(1)}, u32[]{:S(2)}, u32[]{:S(2)}) collective-permute-start(bf16[144,512]{1,0:T(8,128)(2,1)S(1)} %get-tuple-element.62), channel_id=1, source_target_pairs={{0,4},{4,0},{8,12},{12,8},{16,20},{20,16},{24,28},{28,24},{1,5},{5... | collective-permute-start | bytes 442376 | tf_op jit(solution)/shard_map/ppermute | solution.py:441
  16.0 1.6 %collective-permute-start.5 = (bf16[144,512]{1,0:T(8,128)(2,1)S(1)}, bf16[144,512]{1,0:T(8,128)(2,1)S(1)}, u32[]{:S(2)}, u32[]{:S(2)}) collective-permute-start(bf16[144,512]{1,0:T(8,128)(2,1)S(1)} %get-tuple-element.63), channel_id=1, source_target_pairs={{0,8},{4,12},{8,0},{12,4},{16,24},{20,28},{24,16},{28,20},{1,9},{5... | collective-permute-start | bytes 442376 | tf_op jit(solution)/shard_map/ppermute | solution.py:441
  17.6 0.9 %collective-permute-start.6 = (bf16[144,512]{1,0:T(8,128)(2,1)S(1)}, bf16[144,512]{1,0:T(8,128)(2,1)S(1)}, u32[]{:S(2)}, u32[]{:S(2)}) collective-permute-start(bf16[144,512]{1,0:T(8,128)(2,1)S(1)} %get-tuple-element.64), channel_id=1, source_target_pairs={{0,12},{4,8},{8,4},{12,0},{16,28},{20,24},{24,20},{28,16},{1,13},{... | collective-permute-start | bytes 442376 | tf_op jit(solution)/shard_map/ppermute | solution.py:441
  18.4 5.3 %later_states.1 = (bf16[768,2048]{1,0:T(8,128)(2,1)S(1)}, bf16[768,2048]{1,0:T(8,128)(2,1)S(1)}, bf16[768,2048]{1,0:T(8,128)(2,1)S(1)}, bf16[144,512]{1,0:T(8,12...) custom-call(s32[1]{0:T(128)} %bitcast.refs_0_.place_ref, ...), custom_call_target="tpu_custom_call" | custom-call | tf_op jit(solution)/shard_map/later_states/pallas_call | solution.py:279
  23.7 1.1 %collective-permute-start.1 = (bf16[144,512]{1,0:T(8,128)(2,1)S(1)}, bf16[144,512]{1,0:T(8,128)(2,1)S(1)}, u32[]{:S(2)}, u32[]{:S(2)}) collective-permute-start(bf16[144,512]{1,0:T(8,128)(2,1)S(1)} %get-tuple-element.55), channel_id=1, source_target_pairs={{0,4},{4,0},{8,12},{12,8},{16,20},{20,16},{24,28},{28,24},{1,5},{5... | collective-permute-start | bytes 442376 | tf_op jit(solution)/shard_map/ppermute | solution.py:441
  24.8 1.6 %collective-permute-start.2 = (bf16[144,512]{1,0:T(8,128)(2,1)S(1)}, bf16[144,512]{1,0:T(8,128)(2,1)S(1)}, u32[]{:S(2)}, u32[]{:S(2)}) collective-permute-start(bf16[144,512]{1,0:T(8,128)(2,1)S(1)} %get-tuple-element.56), channel_id=1, source_target_pairs={{0,8},{4,12},{8,0},{12,4},{16,24},{20,28},{24,16},{28,20},{1,9},{5... | collective-permute-start | bytes 442376 | tf_op jit(solution)/shard_map/ppermute | solution.py:441
  26.4 2.6 %local.3.refs_1_ = f32[768,2048]{1,0:T(8,128)S(1)} custom-call(bf16[768,2048]{1,0:T(8,128)(2,1)S(1)} %get-tuple-element.75.refs_0_, bf16[768,2048]{1,0:T(8,128)(2,1)S(1)} %get-tuple-element.76.refs_1_, bf16[768,2048]{1,0:T(8,128)(2,1)S(1)} %get-tuple-element.77.refs_2_, f32[768,128]{1,0:T(8,128)S(1)} %get-tuple-element.68.refs_3_, ...), custom_call_target="tpu_custom_call" | custom-call | tf_op jit(solution)/shard_map/local/pallas_call | solution.py:356
  28.9 0.0 collective-permute-done.4.refs_1_
  29.0 0.9 %collective-permute-start.3 = (bf16[144,512]{1,0:T(8,128)(2,1)S(1)}, bf16[144,512]{1,0:T(8,128)(2,1)S(1)}, u32[]{:S(2)}, u32[]{:S(2)}) collective-permute-start(bf16[144,512]{1,0:T(8,128)(2,1)S(1)} %get-tuple-element.57), channel_id=1, source_target_pairs={{0,12},{4,8},{8,4},{12,0},{16,28},{20,24},{24,20},{28,16},{1,13},{... | collective-permute-start | bytes 442376 | tf_op jit(solution)/shard_map/ppermute | solution.py:441
  29.9 0.0 collective-permute-done.5.refs_2_
  29.9 0.0 collective-permute-done.6.refs_3_
  29.9 0.3 combine.3
  30.2 3.1 %collective-permute-start.11 = (bf16[128,512]{1,0:T(8,128)(2,1)S(1)}, bf16[128,512]{1,0:T(8,128)(2,1)S(1)}, u32[]{:S(2)}, u32[]{:S(2)}) collective-permute-start(bf16[128,512]{1,0:T(8,128)(2,1)S(1)} %get-tuple-element.90), channel_id=1, source_target_pairs={{0,16},{4,20},{8,24},{12,28},{16,0},{20,4},{24,8},{28,12},{1,17},{... | collective-permute-start | bytes 393224 | tf_op jit(solution)/shard_map/ppermute | solution.py:452
  33.3 2.5 %local.2.refs_1_ = f32[768,2048]{1,0:T(8,128)S(1)} custom-call(bf16[768,2048]{1,0:T(8,128)(2,1)S(1)} %get-tuple-element.65.refs_0_, bf16[768,2048]{1,0:T(8,128)(2,1)S(1)} %get-tuple-element.66.refs_1_, bf16[768,2048]{1,0:T(8,128)(2,1)S(1)} %get-tuple-element.67.refs_2_, f32[768,128]{1,0:T(8,128)S(1)} %get-tuple-element.68.refs_3_, ...), custom_call_target="tpu_custom_call" | custom-call | tf_op jit(solution)/shard_map/local/pallas_call | solution.py:356
  35.8 0.0 copy-start.4
  35.8 0.0 collective-permute-done.1.refs_1_
  35.8 0.0 collective-permute-done.2.refs_2_
  35.8 0.0 collective-permute-done.3.refs_3_
  35.8 0.3 combine.2
  36.1 2.2 %collective-permute-start.7 = (bf16[128,512]{1,0:T(8,128)(2,1)S(1)}, bf16[128,512]{1,0:T(8,128)(2,1)S(1)}, u32[]{:S(2)}, u32[]{:S(2)}) collective-permute-start(bf16[128,512]{1,0:T(8,128)(2,1)S(1)} %get-tuple-element.74), channel_id=1, source_target_pairs={{0,16},{4,20},{8,24},{12,28},{16,0},{20,4},{24,8},{28,12},{1,17},{... | collective-permute-start | bytes 393224 | tf_op jit(solution)/shard_map/ppermute | solution.py:452
  38.3 0.0 collective-permute-done.11
  38.3 0.2 fusion.15
  38.5 1.2 %collective-permute-start.12 = (bf16[128,512]{1,0:T(8,128)(2,1)S(1)}, bf16[128,512]{1,0:T(8,128)(2,1)S(1)}, u32[]{:S(2)}, u32[]{:S(2)}) collective-permute-start(bf16[128,512]{1,0:T(8,128)(2,1)S(1)} %get-tuple-element.92), channel_id=1, source_target_pairs={{0,4},{4,0},{8,12},{12,8},{16,20},{20,16},{24,28},{28,24},{1,5},{5... | collective-permute-start | bytes 393224 | tf_op jit(solution)/shard_map/ppermute | solution.py:441
  39.6 2.5 %collective-permute-start.13 = (bf16[128,512]{1,0:T(8,128)(2,1)S(1)}, bf16[128,512]{1,0:T(8,128)(2,1)S(1)}, u32[]{:S(2)}, u32[]{:S(2)}) collective-permute-start(bf16[128,512]{1,0:T(8,128)(2,1)S(1)} %get-tuple-element.93), channel_id=1, source_target_pairs={{0,8},{4,12},{8,0},{12,4},{16,24},{20,28},{24,16},{28,20},{1,9},{5... | collective-permute-start | bytes 393224 | tf_op jit(solution)/shard_map/ppermute | solution.py:441
  42.2 1.4 %collective-permute-start.14 = (bf16[128,512]{1,0:T(8,128)(2,1)S(1)}, bf16[128,512]{1,0:T(8,128)(2,1)S(1)}, u32[]{:S(2)}, u32[]{:S(2)}) collective-permute-start(bf16[128,512]{1,0:T(8,128)(2,1)S(1)} %get-tuple-element.91), channel_id=1, source_target_pairs={{0,12},{4,8},{8,4},{12,0},{16,28},{20,24},{24,20},{28,16},{1,13},{... | collective-permute-start | bytes 393224 | tf_op jit(solution)/shard_map/ppermute | solution.py:441
  43.6 0.1 collective-permute-done.7
  43.7 0.2 fusion.7
  43.8 1.5 %collective-permute-start.10 = (bf16[128,512]{1,0:T(8,128)(2,1)S(1)}, bf16[128,512]{1,0:T(8,128)(2,1)S(1)}, u32[]{:S(2)}, u32[]{:S(2)}) collective-permute-start(bf16[128,512]{1,0:T(8,128)(2,1)S(1)} %get-tuple-element.95), channel_id=1, source_target_pairs={{0,12},{4,8},{8,4},{12,0},{16,28},{20,24},{24,20},{28,16},{1,13},{... | collective-permute-start | bytes 393224 | tf_op jit(solution)/shard_map/ppermute | solution.py:441
  45.3 1.9 %collective-permute-start.8 = (bf16[128,512]{1,0:T(8,128)(2,1)S(1)}, bf16[128,512]{1,0:T(8,128)(2,1)S(1)}, u32[]{:S(2)}, u32[]{:S(2)}) collective-permute-start(bf16[128,512]{1,0:T(8,128)(2,1)S(1)} %get-tuple-element.96), channel_id=1, source_target_pairs={{0,4},{4,0},{8,12},{12,8},{16,20},{20,16},{24,28},{28,24},{1,5},{5... | collective-permute-start | bytes 393224 | tf_op jit(solution)/shard_map/ppermute | solution.py:441
  47.3 0.0 collective-permute-done.12.refs_6_
  47.3 1.4 %collective-permute-start.9 = (bf16[128,512]{1,0:T(8,128)(2,1)S(1)}, bf16[128,512]{1,0:T(8,128)(2,1)S(1)}, u32[]{:S(2)}, u32[]{:S(2)}) collective-permute-start(bf16[128,512]{1,0:T(8,128)(2,1)S(1)} %get-tuple-element.97), channel_id=1, source_target_pairs={{0,8},{4,12},{8,0},{12,4},{16,24},{20,28},{24,16},{28,20},{1,9},{5... | collective-permute-start | bytes 393224 | tf_op jit(solution)/shard_map/ppermute | solution.py:441
  48.7 0.0 collective-permute-done.13.refs_7_
  48.7 1.4 %collective-permute-done.14.refs_8_ = bf16[128,512]{1,0:T(8,128)(2,1)S(1)} collective-permute-done((bf16[128,512]{1,0:T(8,128)(2,1)S(1)}, bf16[128,512]{1,0:T(8,128)(2,1)S(1)}, u32[]{:S(2)}, u32[]{:S(2)}) %collective-permute-start.14) | collective-permute-done | bytes 131104 | tf_op jit(solution)/shard_map/ppermute | solution.py:441
  50.1 2.7 %finish_first.1.refs_9_ = bf16[768,2048]{1,0:T(8,128)(2,1)S(1)} custom-call(s32[1]{0:T(128)} %bitcast.refs_0_.place_ref, f32[768,2048]{1,0:T(8,128)S(1)} %local.2.refs_1_, f32[768,128]{1,0:T(8,128)S(1)} %get-tuple-element.79.refs_2_, bf16[768,256]{1,0:T(8,128)(2,1)S(1)} %get-tuple-element.69.refs_5_.refs_3_, f32[1,4096]{1,0:T(1,128)S(1)} %bitcast.30, ...), custom_call_target="tpu_custom_call" | custom-call | tf_op jit(solution)/shard_map/finish_first/pallas_call | solution.py:393
  52.8 0.0 collective-permute-done.10.refs_8_
  52.8 0.0 collective-permute-done.8.refs_6_
  52.8 0.3 collective-permute-done.9.refs_7_
  53.1 3.5 %finish.1 = bf16[768,4096]{1,0:T(8,128)(2,1)} custom-call(s32[1]{0:T(128)} %bitcast.refs_0_.place_ref, f32[768,2048]{1,0:T(8,128)S(1)} %local.3.refs_1_, f32[768,128]{1,0:T(8,128)S(1)} %get-tuple-element.79.refs_2_, bf16[768,256]{1,0:T(8,128)(2,1)S(1)} %get-tuple-element.69.refs_5_.refs_3_, f32[1,4096]{1,0:T(1,128)S(1)} %bitcast.31, ...), custom_call_target="tpu_custom_call" | custom-call | tf_op jit(solution)/shard_map/finish/pallas_call | solution.py:423
  (14 shorter events, 0.1 us)
Async XLA Ops:
  0.0 7.7 %copy-start = (bf16[768,256]{1,0:T(8,128)(2,1)S(1)}, bf16[768,256]{1,0:T(8,128)(2,1)}, u32[]{:S(2)}) copy-start(bf16[768,256]{1,0:T(8,128)(2,1)} %refs_3_.1) | copy-start | bytes 1179652
  0.0 6.2 %copy-start.6 = (f32[64]{0:T(128)S(1)}, f32[64]{0:T(128)}, u32[]{:S(2)}) copy-start(f32[64]{0:T(128)} %param.14) | copy-start | bytes 772
  0.0 6.3 %copy-start.2 = (f32[768,64]{0,1:T(8,128)S(1)}, f32[768,64]{0,1:T(8,128)}, u32[]{:S(2)}) copy-start(f32[768,64]{0,1:T(8,128)} %param.11) | copy-start | bytes 589828
  0.0 6.3 %copy-start.3 = (f32[768,64]{0,1:T(8,128)S(1)}, f32[768,64]{0,1:T(8,128)}, u32[]{:S(2)}) copy-start(f32[768,64]{0,1:T(8,128)} %param.10) | copy-start | bytes 589828
  0.0 7.7 %copy-start.1 = (f32[4,4096]{1,0:T(4,128)S(1)}, f32[4,4096]{1,0:T(4,128)}, u32[]{:S(2)}) copy-start(f32[4,4096]{1,0:T(4,128)} %refs_4_.1) | copy-start | bytes 196612
  0.0 7.7 %copy-start.5 = (f32[4,256]{1,0:T(4,128)S(1)}, f32[4,256]{1,0:T(4,128)}, u32[]{:S(2)}) copy-start(f32[4,256]{1,0:T(4,128)} %refs_6_.1) | copy-start | bytes 12292
  1.3 6.5 %collective-permute-start = (bf16[3,4352]{1,0:T(4,128)(2,1)S(1)}, bf16[3,4352]{1,0:T(4,128)(2,1)S(1)}, u32[]{:S(2)}, u32[]{:S(2)}) collective-permute-start(bf16[3,4352]{1,0:T(4,128)(2,1)S(1)} %slice.51), channel_id=1, source_target_pairs={{0,4},{4,8},{8,12},{12,16},{16,20},{20,24},{24,28},{1,5},{5,9},{9,... | collective-permute-start | bytes 78344 | tf_op jit(solution)/shard_map/ppermute | solution.py:436
  13.6 15.4 %collective-permute-start.4 = (bf16[144,512]{1,0:T(8,128)(2,1)S(1)}, bf16[144,512]{1,0:T(8,128)(2,1)S(1)}, u32[]{:S(2)}, u32[]{:S(2)}) collective-permute-start(bf16[144,512]{1,0:T(8,128)(2,1)S(1)} %get-tuple-element.62), channel_id=1, source_target_pairs={{0,4},{4,0},{8,12},{12,8},{16,20},{20,16},{24,28},{28,24},{1,5},{5... | collective-permute-start | bytes 442376 | tf_op jit(solution)/shard_map/ppermute | solution.py:441
  16.0 13.9 %collective-permute-start.5 = (bf16[144,512]{1,0:T(8,128)(2,1)S(1)}, bf16[144,512]{1,0:T(8,128)(2,1)S(1)}, u32[]{:S(2)}, u32[]{:S(2)}) collective-permute-start(bf16[144,512]{1,0:T(8,128)(2,1)S(1)} %get-tuple-element.63), channel_id=1, source_target_pairs={{0,8},{4,12},{8,0},{12,4},{16,24},{20,28},{24,16},{28,20},{1,9},{5... | collective-permute-start | bytes 442376 | tf_op jit(solution)/shard_map/ppermute | solution.py:441
  17.6 12.3 %collective-permute-start.6 = (bf16[144,512]{1,0:T(8,128)(2,1)S(1)}, bf16[144,512]{1,0:T(8,128)(2,1)S(1)}, u32[]{:S(2)}, u32[]{:S(2)}) collective-permute-start(bf16[144,512]{1,0:T(8,128)(2,1)S(1)} %get-tuple-element.64), channel_id=1, source_target_pairs={{0,12},{4,8},{8,4},{12,0},{16,28},{20,24},{24,20},{28,16},{1,13},{... | collective-permute-start | bytes 442376 | tf_op jit(solution)/shard_map/ppermute | solution.py:441
  23.7 12.1 %collective-permute-start.1 = (bf16[144,512]{1,0:T(8,128)(2,1)S(1)}, bf16[144,512]{1,0:T(8,128)(2,1)S(1)}, u32[]{:S(2)}, u32[]{:S(2)}) collective-permute-start(bf16[144,512]{1,0:T(8,128)(2,1)S(1)} %get-tuple-element.55), channel_id=1, source_target_pairs={{0,4},{4,0},{8,12},{12,8},{16,20},{20,16},{24,28},{28,24},{1,5},{5... | collective-permute-start | bytes 442376 | tf_op jit(solution)/shard_map/ppermute | solution.py:441
  24.8 11.0 %collective-permute-start.2 = (bf16[144,512]{1,0:T(8,128)(2,1)S(1)}, bf16[144,512]{1,0:T(8,128)(2,1)S(1)}, u32[]{:S(2)}, u32[]{:S(2)}) collective-permute-start(bf16[144,512]{1,0:T(8,128)(2,1)S(1)} %get-tuple-element.56), channel_id=1, source_target_pairs={{0,8},{4,12},{8,0},{12,4},{16,24},{20,28},{24,16},{28,20},{1,9},{5... | collective-permute-start | bytes 442376 | tf_op jit(solution)/shard_map/ppermute | solution.py:441
  29.0 6.9 %collective-permute-start.3 = (bf16[144,512]{1,0:T(8,128)(2,1)S(1)}, bf16[144,512]{1,0:T(8,128)(2,1)S(1)}, u32[]{:S(2)}, u32[]{:S(2)}) collective-permute-start(bf16[144,512]{1,0:T(8,128)(2,1)S(1)} %get-tuple-element.57), channel_id=1, source_target_pairs={{0,12},{4,8},{8,4},{12,0},{16,28},{20,24},{24,20},{28,16},{1,13},{... | collective-permute-start | bytes 442376 | tf_op jit(solution)/shard_map/ppermute | solution.py:441
  30.2 8.1 %collective-permute-start.11 = (bf16[128,512]{1,0:T(8,128)(2,1)S(1)}, bf16[128,512]{1,0:T(8,128)(2,1)S(1)}, u32[]{:S(2)}, u32[]{:S(2)}) collective-permute-start(bf16[128,512]{1,0:T(8,128)(2,1)S(1)} %get-tuple-element.90), channel_id=1, source_target_pairs={{0,16},{4,20},{8,24},{12,28},{16,0},{20,4},{24,8},{28,12},{1,17},{... | collective-permute-start | bytes 393224 | tf_op jit(solution)/shard_map/ppermute | solution.py:452
  35.8 14.4 %copy-start.4 = (f32[4096]{0:T(1024)S(1)}, f32[4096]{0:T(1024)}, u32[]{:S(2)}) copy-start(f32[4096]{0:T(1024)} %param.15) | copy-start | bytes 49156
  36.1 7.6 %collective-permute-start.7 = (bf16[128,512]{1,0:T(8,128)(2,1)S(1)}, bf16[128,512]{1,0:T(8,128)(2,1)S(1)}, u32[]{:S(2)}, u32[]{:S(2)}) collective-permute-start(bf16[128,512]{1,0:T(8,128)(2,1)S(1)} %get-tuple-element.74), channel_id=1, source_target_pairs={{0,16},{4,20},{8,24},{12,28},{16,0},{20,4},{24,8},{28,12},{1,17},{... | collective-permute-start | bytes 393224 | tf_op jit(solution)/shard_map/ppermute | solution.py:452
  38.5 8.8 %collective-permute-start.12 = (bf16[128,512]{1,0:T(8,128)(2,1)S(1)}, bf16[128,512]{1,0:T(8,128)(2,1)S(1)}, u32[]{:S(2)}, u32[]{:S(2)}) collective-permute-start(bf16[128,512]{1,0:T(8,128)(2,1)S(1)} %get-tuple-element.92), channel_id=1, source_target_pairs={{0,4},{4,0},{8,12},{12,8},{16,20},{20,16},{24,28},{28,24},{1,5},{5... | collective-permute-start | bytes 393224 | tf_op jit(solution)/shard_map/ppermute | solution.py:441
  39.6 9.1 %collective-permute-start.13 = (bf16[128,512]{1,0:T(8,128)(2,1)S(1)}, bf16[128,512]{1,0:T(8,128)(2,1)S(1)}, u32[]{:S(2)}, u32[]{:S(2)}) collective-permute-start(bf16[128,512]{1,0:T(8,128)(2,1)S(1)} %get-tuple-element.93), channel_id=1, source_target_pairs={{0,8},{4,12},{8,0},{12,4},{16,24},{20,28},{24,16},{28,20},{1,9},{5... | collective-permute-start | bytes 393224 | tf_op jit(solution)/shard_map/ppermute | solution.py:441
  42.2 8.0 %collective-permute-start.14 = (bf16[128,512]{1,0:T(8,128)(2,1)S(1)}, bf16[128,512]{1,0:T(8,128)(2,1)S(1)}, u32[]{:S(2)}, u32[]{:S(2)}) collective-permute-start(bf16[128,512]{1,0:T(8,128)(2,1)S(1)} %get-tuple-element.91), channel_id=1, source_target_pairs={{0,12},{4,8},{8,4},{12,0},{16,28},{20,24},{24,20},{28,16},{1,13},{... | collective-permute-start | bytes 393224 | tf_op jit(solution)/shard_map/ppermute | solution.py:441
  43.8 9.0 %collective-permute-start.10 = (bf16[128,512]{1,0:T(8,128)(2,1)S(1)}, bf16[128,512]{1,0:T(8,128)(2,1)S(1)}, u32[]{:S(2)}, u32[]{:S(2)}) collective-permute-start(bf16[128,512]{1,0:T(8,128)(2,1)S(1)} %get-tuple-element.95), channel_id=1, source_target_pairs={{0,12},{4,8},{8,4},{12,0},{16,28},{20,24},{24,20},{28,16},{1,13},{... | collective-permute-start | bytes 393224 | tf_op jit(solution)/shard_map/ppermute | solution.py:441
  45.3 7.5 %collective-permute-start.8 = (bf16[128,512]{1,0:T(8,128)(2,1)S(1)}, bf16[128,512]{1,0:T(8,128)(2,1)S(1)}, u32[]{:S(2)}, u32[]{:S(2)}) collective-permute-start(bf16[128,512]{1,0:T(8,128)(2,1)S(1)} %get-tuple-element.96), channel_id=1, source_target_pairs={{0,4},{4,0},{8,12},{12,8},{16,20},{20,16},{24,28},{28,24},{1,5},{5... | collective-permute-start | bytes 393224 | tf_op jit(solution)/shard_map/ppermute | solution.py:441
  47.3 5.9 %collective-permute-start.9 = (bf16[128,512]{1,0:T(8,128)(2,1)S(1)}, bf16[128,512]{1,0:T(8,128)(2,1)S(1)}, u32[]{:S(2)}, u32[]{:S(2)}) collective-permute-start(bf16[128,512]{1,0:T(8,128)(2,1)S(1)} %get-tuple-element.97), channel_id=1, source_target_pairs={{0,8},{4,12},{8,0},{12,4},{16,24},{20,28},{24,16},{28,20},{1,9},{5... | collective-permute-start | bytes 393224 | tf_op jit(solution)/shard_map/ppermute | solution.py:441
